TPU v7x, 32 devices: a whole 2x2x4 slice. The times are simulated.
32 devices in a mesh: view: 2 (over core), gauss: 16 (over z, y, x).
Axes of the slice: x: 2, y: 2, z: 4, core: 2. Of those that a mesh axis runs over, the one named last changes fastest.
Arguments:
- entry_grads: bfloat16 [2, 59, 81920], P('view', None, 'gauss'), may hold values from -4 to 4
- vis_ids: int32 [2, 81920], P('view', 'gauss'), may hold values from 0 to 5119
- feats: bfloat16 [256, 16, 5120], P(None, 'gauss', 'view'), may hold values from -6 to 6
- code_tab: float32 [256, 8], replicated, may hold values from -4 to 4
- subj_ids: int32 [16, 5120], P('gauss', 'view'), may hold values from 0 to 7
- bone_ids: int32 [4, 16, 5120], P(None, 'gauss', 'view'), may hold values from 0 to 23
- skin_w: float32 [4, 16, 5120], P(None, 'gauss', 'view'), may hold values from 0.05 to 0.5
- canon_pos: float32 [3, 16, 5120], P(None, 'gauss', 'view'), may hold values from -5 to 5
- bone_tf: float32 [12, 192], replicated, may hold values from -4 to 4
- w_first: bfloat16 [256, 256], replicated, may hold values from -0.375 to 0.375
- w_second: bfloat16 [256, 256], replicated, may hold values from -0.375 to 0.375
- w_third: bfloat16 [256, 256], replicated, may hold values from -0.375 to 0.375
- biases: float32 [3, 256], replicated, may hold values from -3 to 3
- w_head: bfloat16 [3, 256], replicated, may hold values from -0.375 to 0.375
Outputs:
- attr_grads: float32 [59, 16, 5120], P(None, 'gauss', 'view')
- feat_grads: bfloat16 [256, 16, 5120], P(None, 'gauss', 'view')
- skin_grads: float32 [4, 16, 5120], P(None, 'gauss', 'view')
- first_grad: float32 [256, 256], replicated
- second_grad: float32 [256, 256], replicated
- third_grad: float32 [256, 256], replicated
- bias_grads: float32 [3, 256], replicated
- head_grad: float32 [3, 256], replicated
- code_grad: float32 [256, 8], replicated
- bone_grad: float32 [12, 192], replicated
All inputs are finite; a program needn't handle non-finite values.
Results may differ from a plain program's by a relative error of at most 0.024.
Values may be sent and summed in bfloat16 or wider, within the bound.
No kernel may reach another device: no remote copies, remote signals or barrier semaphores. Data moves between devices by JAX's collectives and lax.ppermute only.
A program may use at most 128 MiB of HBM per device.

v0:
```python
import math

import jax
import jax.numpy as jnp
from jax import lax
from jax.sharding import PartitionSpec as P

HIGH = lax.Precision.HIGHEST


def dsilu(value):
    sig = jax.nn.sigmoid(value)
    return sig * (1.0 + value * (1.0 - sig))


def over_rows(left, right):
    return lax.dot_general(
        left, right, (((1,), (1,)), ((), ())), preferred_element_type=jnp.float32
    )


def over_first(left, right):
    return lax.dot_general(
        left, right, (((0,), (0,)), ((), ())), preferred_element_type=jnp.float32
    )


def body(
    entry_grads,
    vis_ids,
    feats,
    code_tab,
    subj_ids,
    bone_ids,
    skin_w,
    canon_pos,
    bone_tf,
    w_first,
    w_second,
    w_third,
    biases,
    w_head,
):
    member_count = feats.shape[2]
    viewers = lax.axis_size("view")
    factor = 1.0 / math.sqrt(member_count * viewers * lax.axis_size("gauss"))
    partial_value = (
        jnp.zeros((entry_grads.shape[1], member_count * viewers), jnp.float32)
        .at[:, vis_ids[0]]
        .add(entry_grads[0].astype(jnp.float32))
    )
    position_gradient = lax.psum_scatter(
        partial_value[:3].astype(jnp.bfloat16), "view", scatter_dimension=1, tiled=True
    ).astype(jnp.float32)
    subjects = code_tab.shape[1]
    table_cols = bone_tf.shape[1]
    per_subject = table_cols // subjects
    subject = subj_ids[0]
    subj_hot = (subject[None, :] == jnp.arange(subjects, dtype=jnp.int32)[:, None]).astype(
        jnp.float32
    )
    code_sel = jnp.dot(code_tab, subj_hot, precision=HIGH)
    inputs = (feats[:, 0].astype(jnp.float32) + code_sel).astype(jnp.bfloat16)
    pre_one = jnp.dot(w_first, inputs, preferred_element_type=jnp.float32) + biases[0][:, None]
    act_one = jax.nn.silu(pre_one).astype(jnp.bfloat16)
    pre_two = jnp.dot(w_second, act_one, preferred_element_type=jnp.float32) + biases[1][:, None]
    act_two = jax.nn.silu(pre_two).astype(jnp.bfloat16)
    pre_three = jnp.dot(w_third, act_two, preferred_element_type=jnp.float32) + biases[2][:, None]
    act_three = jax.nn.silu(pre_three).astype(jnp.bfloat16)
    shifted_point = canon_pos[:, 0] + jnp.dot(w_head, act_three, preferred_element_type=jnp.float32)
    homogeneous_point = jnp.concatenate(
        [shifted_point, jnp.ones((1, member_count), jnp.float32)], axis=0
    )
    table_index = jnp.arange(table_cols, dtype=jnp.int32)[:, None]
    shift_acc = jnp.zeros((3, member_count), jnp.float32)
    bone_acc = jnp.zeros((12, table_cols), jnp.float32)
    skins = []
    for member_flag in range(bone_ids.shape[0]):
        column = subject * per_subject + bone_ids[member_flag, 0]
        onehot = (column[None, :] == table_index).astype(jnp.float32)
        blend_matrix = jnp.dot(bone_tf, onehot, precision=HIGH).reshape(3, 4, member_count)
        skinning_weight = skin_w[member_flag, 0]
        posed_point = jnp.sum(blend_matrix * homogeneous_point[None], axis=1)
        skins.append(jnp.sum(position_gradient * posed_point, axis=0))
        shift_acc = shift_acc + skinning_weight * jnp.sum(
            blend_matrix[:, :3] * position_gradient[:, None], axis=0
        )
        contribution = (
            (skinning_weight * position_gradient)[:, None] * homogeneous_point[None]
        ).reshape(12, member_count)
        bone_acc = bone_acc + lax.dot_general(
            contribution, onehot, (((1,), (1,)), ((), ())), precision=HIGH
        )
    shift_grad = shift_acc.astype(jnp.bfloat16)
    head = factor * over_rows(shift_grad, act_three)
    back_three = (over_first(w_head, shift_grad) * dsilu(pre_three)).astype(jnp.bfloat16)
    third = factor * over_rows(back_three, act_two)
    bias_three = factor * jnp.sum(back_three, axis=1, dtype=jnp.float32)
    bone_total = factor * bone_acc
    back_two = (over_first(w_third, back_three) * dsilu(pre_two)).astype(jnp.bfloat16)
    second = factor * over_rows(back_two, act_one)
    bias_two = factor * jnp.sum(back_two, axis=1, dtype=jnp.float32)
    back_one = (over_first(w_second, back_two) * dsilu(pre_one)).astype(jnp.bfloat16)
    first = factor * over_rows(back_one, inputs)
    bias_one = factor * jnp.sum(back_one, axis=1, dtype=jnp.float32)
    input_grad = over_first(w_first, back_one)
    code = factor * lax.dot_general(input_grad, subj_hot, (((1,), (1,)), ((), ())), precision=HIGH)
    first, second, third, bias_one, bias_two, bias_three, head, code, bone_total = lax.psum(
        (first, second, third, bias_one, bias_two, bias_three, head, code, bone_total),
        ("view", "gauss"),
    )
    others = lax.psum_scatter(
        partial_value[3:].astype(jnp.bfloat16), "view", scatter_dimension=1, tiled=True
    ).astype(jnp.float32)
    summed = jnp.concatenate([position_gradient, others], axis=0)
    bias_rows = jnp.stack([bias_one, bias_two, bias_three])
    return (
        summed[:, None, :],
        input_grad.astype(jnp.bfloat16)[:, None, :],
        jnp.stack(skins)[:, None, :],
        first,
        second,
        third,
        bias_rows,
        head,
        code,
        bone_total,
    )


def solution(mesh):
    placed = (
        P("view", None, "gauss"),
        P("view", "gauss"),
        P(None, "gauss", "view"),
        P(),
        P("gauss", "view"),
        P(None, "gauss", "view"),
        P(None, "gauss", "view"),
        P(None, "gauss", "view"),
        P(),
        P(),
        P(),
        P(),
        P(),
        P(),
    )
    return jax.shard_map(
        body,
        mesh=mesh,
        in_specs=placed,
        out_specs=(
            P(None, "gauss", "view"),
            P(None, "gauss", "view"),
            P(None, "gauss", "view"),
            P(),
            P(),
            P(),
            P(),
            P(),
            P(),
            P(),
        ),
        check_vma=False,
    )
```

profile of v0, /device:TPU:0, one launch (start us, length us, event | category | flops | bytes accessed | tf_op | source)
XLA Modules:
  0.0 231.1 jit_solution(535577359621695191)
XLA Ops:
  7.2 0.0 copy-start
  7.2 0.0 reduce-scatter.7.cloned.1.call-start
  7.2 1.2 convert_bitcast_fusion
  8.5 2.1 copy.65
  10.6 29.7 %scatter_custom_fusion = f32[59,5120]{0,1:T(8,128)} fusion(s32[5120]{0:T(1024)S(1)} %bitcast.121, f32[5120,59]{1,0:T(8,128)} %copy.65, f32[]{:T(128)} %constant.6.clone.1), kind=kCustom, calls=%fused_computation.46 | custom fusion | flops 302080 | bytes 1208832 | tf_op jit(solution)/shard_map/scatter-add | solution.py:50
  40.3 1.9 convert.6
  42.1 1.1 slice_bitcast_fusion
  43.3 0.0 reduce-scatter.7.cloned.1.call-update
  43.3 0.0 reduce-scatter.5.cloned.1.call-start
  43.4 1.6 slice.71
  45.0 0.0 reduce-scatter.5.cloned.1.call-update
  45.0 0.0 all-reduce.5.cloned.1.call-start
  45.1 0.1 fusion.43
  45.3 0.5 copy-done.24
  45.9 0.7 convolution_bitcast_fusion.4
  46.6 0.7 convolution_bitcast_fusion.7
  47.4 0.7 convolution_bitcast_fusion.6
  48.2 0.7 convolution_bitcast_fusion.5
  48.9 0.1 slice_reduce_fusion.3
  49.1 0.8 copy.68
  49.9 1.3 fusion.7
  51.2 2.3 %multiply_convert_fusion.2 = (bf16[256,2560]{0,1:T(8,128)(2,1)S(1)}, f32[256,2560]{0,1:T(8,128)}) fusion(f32[256]{0:T(256)S(1)} %bitcast.127, bf16[256,2560]{0,1:T(8,128)(2,1)S(1)} %fusion.7, bf16[256,256]{1,0:T(8,128)(2,1)S(1)} %copy-done.11), kind=kOutput, calls=%fused_computation.32 | convolution fusion | flops 339476480 | bytes 5374976 | tf_op jit(solution)/shard_map/dot_general | solution.py:64
  53.6 2.3 %multiply_convert_fusion.1 = (bf16[256,2560]{0,1:T(8,128)(2,1)S(1)}, f32[256,2560]{0,1:T(8,128)}) fusion(f32[256]{0:T(256)S(1)} %bitcast.126, bf16[256,2560]{0,1:T(8,128)(2,1)S(1)} %get-tuple-element.106, bf16[256,256]{1,0:T(8,128)(2,1)S(1)} %copy-done.30), kind=kOutput, calls=%fused_computation.30 | convolution fusion | flops 339476480 | bytes 5374976 | tf_op jit(solution)/shard_map/dot_general | solution.py:66
  55.9 2.3 %multiply_convert_fusion = (bf16[256,2560]{0,1:T(8,128)(2,1)S(1)}, f32[256,2560]{0,1:T(8,128)}) fusion(f32[256]{0:T(256)S(1)} %bitcast.125, bf16[256,2560]{0,1:T(8,128)(2,1)S(1)} %get-tuple-element.108, bf16[256,256]{1,0:T(8,128)(2,1)S(1)} %copy-done), kind=kOutput, calls=%fused_computation.28 | convolution fusion | flops 339476480 | bytes 5374976 | tf_op jit(solution)/shard_map/dot_general | solution.py:68
  58.2 0.4 fusion.11
  58.7 0.0 reduce-scatter.7.cloned.1.call-done
  58.7 1.3 copy.72
  60.1 0.1 fusion.33
  60.2 0.7 convert_multiply_fusion.3
  60.9 1.6 broadcast_multiply_fusion.3
  62.5 1.0 mul.335
  63.4 2.3 %fusion.12 = f32[12,192]{1,0:T(8,128)} fusion(f32[12,2560]{1,0:T(8,128)S(1)} %mul.335, s32[2560]{0:T(1024)} %copy-done.24), kind=kOutput, calls=%fused_computation.35 | convolution fusion | flops 71270400 | bytes 142336 | tf_op jit(solution)/shard_map/dot_general | solution.py:91
  65.7 1.0 mul.331
  66.7 2.3 fusion.13
  69.1 2.3 fusion.14
  71.4 0.3 convolution_multiply_fusion.4
  71.7 3.0 %convert_reduce_fusion = (f32[256]{0:T(256)S(1)}, bf16[256,2560]{0,1:T(8,128)(2,1)S(1)}) fusion(f32[256,2560]{0,1:T(8,128)} %get-tuple-element.111, bf16[3,2560]{1,0:T(4,128)(2,1)S(1)} %copy-done.15, bf16[3,256]{1,0:T(4,128)(2,1)S(1)} %copy-done.29), kind=kOutput, calls=%fused_computation.25 | convolution fusion | flops 11140864 | bytes 3950080 | tf_op jit(solution)/shard_map/dot_general | solution.py:23
  74.7 1.2 convolution_multiply_fusion
  76.0 0.6 copy-done.37
  76.6 1.1 convert_reduce_fusion.1
  77.7 1.3 convolution_multiply_fusion.1
  79.0 0.6 copy-done.36
  79.6 1.1 convert_reduce_fusion.2
  80.8 0.5 fusion.45
  81.2 0.2 copy-done.14
  81.5 0.2 copy-start.7
  81.7 1.0 convolution_multiply_fusion.3
  82.8 1.0 fusion.21
  83.8 0.1 fusion.34
  84.0 1.3 convolution_multiply_fusion.2
  85.3 1.2 convert_bitcast_fusion.1
  86.4 0.0 all-reduce.5.cloned.1.call-update
  86.5 43.1 %all-reduce.1 = (f32[1,256]{1,0:T(1,128)S(1)}, f32[1,256]{1,0:T(1,128)S(1)}, f32[1,256]{1,0:T(1,128)S(1)}, f32[3,256]{1,0:T(4,128)}, f32[256,8]{0,1:T(8,128)}, /*index=5*/f32[12,192]{1,0:T(8,128)}) all-reduce(f32[1,256]{1,0:T(1,128)S(1)} %bitcast.124, ...), channel_id=1, replica_groups=mesh['view'=2,'gauss'=16] {'view','gauss'}, use_global_device_ids=true, to_apply=%region_23.24 | all-reduce | flops 5888 | bytes 47104 | tf_op jit(solution)/shard_map/psum | solution.py:108
  129.6 0.6 pad_maximum_fusion.1
  130.2 0.3 copy.67
  130.5 0.6 broadcast_in_dim.11
  131.1 1.6 copy.70
  132.7 1.2 convert_element_type.67
  133.9 0.4 maximum_bitcast_fusion
  134.3 1.3 copy.69
  135.6 84.0 %all-reduce.5.cloned.1.call-done = (f32[256,256]{1,0:T(8,128)}, f32[256,256]{1,0:T(8,128)}, f32[256,256]{1,0:T(8,128)}) async-done(((f32[256,256]{1,0:T(8,128)}, f32[256,256]{1,0:T(8,128)}, f32[256,256]{1,0:T(8,128)}), (f32[256,256]{1,0:T(8,128)}, f32[256,256]{1,0:T(8,128)}, f32[256,256]{1,0:T(8,128)})) %all-reduce.5.cloned.1.call-update) | async-done | bytes 786448 | tf_op jit(solution)/shard_map/psum | solution.py:108
  219.6 1.7 copy.78
  221.3 1.7 copy.79
  222.9 1.7 copy.80
  (89 shorter events, 0.6 us)
Async XLA Ops:
  7.2 48.7 %copy-start = (bf16[256,256]{1,0:T(8,128)(2,1)S(1)}, bf16[256,256]{1,0:T(8,128)(2,1)}, u32[]{:S(2)}) copy-start(bf16[256,256]{1,0:T(8,128)(2,1)} %param.25) | copy-start | bytes 393220
  7.2 51.5 %reduce-scatter.7.cloned.1.call-start = ((), (), s32[]{:S(2)}) async-start(), calls=%async_computation.3 | async-start | bytes 1966080
  8.4 2.1 copy-start.19
  43.3 1.8 copy-start.17
  43.3 1.8 copy-start.25
  43.3 2.5 %copy-start.32 = (f32[12,192]{1,0:T(8,128)S(1)}, f32[12,192]{1,0:T(8,128)}, u32[]{:S(2)}) copy-start(f32[12,192]{1,0:T(8,128)} %param.22) | copy-start | bytes 27652
  43.3 89.4 %reduce-scatter.5.cloned.1.call-start = ((), (), s32[]{:S(2)}) async-start(), calls=%async_computation.2 | async-start | bytes 1966080 | tf_op jit(solution)/shard_map/reduce_scatter | solution.py:112
  45.0 3.9 %copy-start.18 = (f32[4,1,2560]{2,1,0:T(1,128)S(1)}, f32[4,1,2560]{2,1,0:T(1,128)}, u32[]{:S(2)}) copy-start(f32[4,1,2560]{2,1,0:T(1,128)} %param.20) | copy-start | bytes 122884
  45.0 4.0 %copy-start.4 = (bf16[256,1,2560]{2,0,1:T(8,128)(2,1)S(1)}, bf16[256,1,2560]{2,0,1:T(8,128)(2,1)}, u32[]{:S(2)}) copy-start(bf16[256,1,2560]{2,0,1:T(8,128)(2,1)} %param.16) | copy-start | bytes 3932164
  45.0 174.5 %all-reduce.5.cloned.1.call-start = ((), (), s32[]{:S(2)}) async-start(), calls=%async_computation.4 | async-start | bytes 1572864 | tf_op jit(solution)/shard_map/psum | solution.py:108
  45.3 0.6 copy-start.24
  45.3 2.1 copy-start.20
  45.3 2.9 %copy-start.22 = (s32[2560]{0:T(1024)}, s32[2560]{0:T(1024)S(1)}, u32[]{:S(2)}) copy-start(s32[2560]{0:T(1024)S(1)} %get-tuple-element.61) | copy-start | bytes 30724
  45.3 3.6 %copy-start.23 = (s32[2560]{0:T(1024)}, s32[2560]{0:T(1024)S(1)}, u32[]{:S(2)}) copy-start(s32[2560]{0:T(1024)S(1)} %get-tuple-element.63) | copy-start | bytes 30724
  45.3 4.6 %copy-start.13 = (s32[2560]{0:T(1024)}, s32[2560]{0:T(1024)S(1)}, u32[]{:S(2)}) copy-start(s32[2560]{0:T(1024)S(1)} %get-tuple-element.80) | copy-start | bytes 30724
  48.1 1.8 copy-start.27
  48.1 1.8 copy-start.26
  49.9 1.3 copy-start.11
  51.2 2.4 %copy-start.1 = (bf16[256,2560]{0,1:T(8,128)(2,1)}, bf16[256,2560]{0,1:T(8,128)(2,1)S(1)}, u32[]{:S(2)}) copy-start(bf16[256,2560]{0,1:T(8,128)(2,1)S(1)} %fusion.7) | copy-start | bytes 3932164
  51.2 2.3 %copy-start.30 = (bf16[256,256]{1,0:T(8,128)(2,1)S(1)}, bf16[256,256]{1,0:T(8,128)(2,1)}, u32[]{:S(2)}) copy-start(bf16[256,256]{1,0:T(8,128)(2,1)} %param.24) | copy-start | bytes 393220
  55.9 2.3 %copy-start.5 = (bf16[256,2560]{0,1:T(8,128)(2,1)}, bf16[256,2560]{0,1:T(8,128)(2,1)S(1)}, u32[]{:S(2)}) copy-start(bf16[256,2560]{0,1:T(8,128)(2,1)S(1)} %get-tuple-element.108) | copy-start | bytes 3932164
  55.9 2.3 %copy-start.16 = (f32[3,1,2560]{2,1,0:T(1,128)S(1)}, f32[3,1,2560]{2,1,0:T(1,128)}, u32[]{:S(2)}) copy-start(f32[3,1,2560]{2,1,0:T(1,128)} %param.21) | copy-start | bytes 92164
  55.9 2.3 %copy-start.28 = (bf16[3,256]{1,0:T(4,128)(2,1)S(1)}, bf16[3,256]{1,0:T(4,128)(2,1)}, u32[]{:S(2)}) copy-start(bf16[3,256]{1,0:T(4,128)(2,1)} %param.27) | copy-start | bytes 4612
  62.5 8.9 %copy-start.15 = (bf16[3,2560]{1,0:T(4,128)(2,1)S(1)}, bf16[3,2560]{1,0:T(4,128)(2,1)}, u32[]{:S(2)}) copy-start(bf16[3,2560]{1,0:T(4,128)(2,1)} %get-tuple-element.100) | copy-start | bytes 46084
  63.4 8.3 %copy-start.29 = (bf16[3,256]{1,0:T(4,128)(2,1)S(1)}, bf16[3,256]{1,0:T(4,128)(2,1)}, u32[]{:S(2)}) copy-start(bf16[3,256]{1,0:T(4,128)(2,1)} %param.27) | copy-start | bytes 4612
  71.7 3.0 %copy-start.6 = (bf16[256,2560]{0,1:T(8,128)(2,1)S(1)}, bf16[256,2560]{0,1:T(8,128)(2,1)}, u32[]{:S(2)}) copy-start(bf16[256,2560]{0,1:T(8,128)(2,1)} %copy-done.5) | copy-start | bytes 3932164
  74.7 1.8 copy-start.37
  77.7 1.3 copy-start.31
  77.7 1.9 copy-start.36
  79.6 1.1 copy-start.12
  80.7 0.7 copy-start.14
  81.4 1.3 copy-start.21
  81.5 1.3 copy-start.33
  81.5 1.3 copy-start.34
  81.5 1.3 copy-start.35
  81.5 2.3 copy-start.7
  81.7 2.1 copy-start.8
  81.7 2.1 copy-start.9
  81.7 2.1 copy-start.10
  81.7 2.3 copy-start.2
  86.4 44.7 %copy-start.3 = (bf16[256,1,2560]{0,2,1:T(8,128)(2,1)S(1)}, bf16[256,1,2560]{0,2,1:T(8,128)(2,1)}, u32[]{:S(2)}) copy-start(bf16[256,1,2560]{0,2,1:T(8,128)(2,1)} %convert_bitcast_fusion.1) | copy-start | bytes 3932164
Sparse Core Ops, SparseCore 0:
  43.4 11.4 reduce-scatter.6
  57.3 9.9 reduce-scatter.4
  86.6 132.9 all-reduce.4
where the time goes:
time: 232 us; the launch traced here: 231 us
  waiting for transfers between devices  84.1 us (36%)
  blocking collectives  43.1 us (19%)
  other arithmetic  38.9 us (17%)
  matrix products  30.2 us (13%)
  local copies, waits for them, and re-layouts  20.4 us (9%)
  between operations  14.4 us (6%)
    psum x1, waiting for transfers between devices, body(): lax.psum((first, second, third, bias_one, bias_two, bias_three, head, cod...  84 us
    psum x1, blocking collectives, body(): lax.psum((first, second, third, bias_one, bias_two, bias_three, head, cod...  43.1 us
    scatter-add x1, other arithmetic, body(): partial_value = jnp.zeros((entry_grads.shape[1], member_count * viewers),...  29.7 us
    unnamed x84, local copies, waits for them, and re-layouts  13.5 us
    dot_general x4, matrix products, body(): lax.dot_general(contribution, onehot, (((1,), (1,)), ((), ())), precision...  7.91 us
    dot_general x4, matrix products, over_first(): lax.dot_general(left, right, (((0,), (0,)), ((), ())), preferred_element_...  5.77 us
  transfers between devices with their start and end apart: 3, of which 1 were waited for; matrix products, arithmetic and copies ran while one was open for 20% of the time, Pallas kernels for 0%

commit v1 on v0

v1 whole, which is shorter than its diff:
```python
import functools
import math

import jax
import jax.numpy as jnp
from jax import lax
from jax.experimental import pallas as pl
from jax.experimental.pallas import tpu as pltpu
from jax.sharding import PartitionSpec as P

F32 = jnp.float32
BF16 = jnp.bfloat16
AXES = ("view", "gauss")
LOW = 256
GROUP = 16
NT = (((1,), (1,)), ((), ()))
TN = (((0,), (0,)), ((), ()))
VMEM = pl.BlockSpec(memory_space=pltpu.VMEM)
SMEM = pl.BlockSpec(memory_space=pltpu.SMEM)


def params():
    return pltpu.CompilerParams(vmem_limit_bytes=48 * 1024 * 1024)


def mm(left, right, dims=(((1,), (0,)), ((), ()))):
    return lax.dot_general(left, right, dims, preferred_element_type=F32)


def divisor(total, choices):
    for choice in choices:
        if total % choice == 0:
            return choice
    return total


def scatter_kernel(first_row, rows, viewers, view_ref, grads_ref, ids_ref, out_ref, acc_ref):
    entries = ids_ref.shape[1]
    blocks = acc_ref.shape[0]
    groups = acc_ref.shape[1] // GROUP
    step = divisor(entries, (1024, 512, 256, 128))
    low_rows = lax.broadcasted_iota(jnp.int32, (LOW, step), 0).astype(F32).astype(BF16)
    one = jnp.ones((), BF16)
    zero = jnp.zeros((), BF16)

    acc_ref[...] = jnp.zeros_like(acc_ref)

    def chunk(index, carry):
        spot = pl.ds(pl.multiple_of(index * step, step), step)
        ids = ids_ref[0:1, spot]
        high = lax.shift_right_logical(ids, 8).astype(F32).astype(BF16)
        low = lax.bitwise_and(ids, LOW - 1).astype(F32).astype(BF16)
        hot = jnp.where(low_rows == low, one, zero)
        values = []
        for group in range(groups):
            begin = first_row + group * GROUP
            count = min(GROUP, first_row + rows - begin)
            piece = grads_ref[0, begin : begin + count, spot]
            if count < GROUP:
                piece = jnp.concatenate(
                    [piece.astype(F32), jnp.zeros((GROUP - count, step), F32)], axis=0
                ).astype(BF16)
            values.append(piece)
        high = jnp.broadcast_to(high, (GROUP, step))
        for block in range(blocks):
            inside = high == jnp.asarray(block, BF16)
            left = jnp.concatenate([jnp.where(inside, v, zero) for v in values], axis=0)
            acc_ref[block] += mm(left, hot, NT)
        return carry

    lax.fori_loop(0, entries // step, chunk, 0)
    per = blocks // viewers
    for block in range(blocks):
        slot = lax.rem(block // per - view_ref[0] + viewers, viewers)
        out_ref[slot, :, (block % per) * LOW : (block % per + 1) * LOW] = acc_ref[block].astype(BF16)


def scatter(view, entry_grads, vis_ids, first_row, rows, members, viewers):
    groups = -(-rows // GROUP)
    blocks = members * viewers // LOW
    return pl.pallas_call(
        functools.partial(scatter_kernel, first_row, rows, viewers),
        out_shape=jax.ShapeDtypeStruct((viewers, groups * GROUP, members), BF16),
        in_specs=[SMEM, VMEM, VMEM],
        out_specs=VMEM,
        scratch_shapes=[pltpu.VMEM((blocks, groups * GROUP, LOW), F32)],
        compiler_params=params(),
    )(view, entry_grads, vis_ids)


def network_kernel(
    factor,
    side_ref,
    pos_ref,
    feats_ref,
    code_ref,
    subj_ref,
    bone_ids_ref,
    skin_ref,
    canon_ref,
    table_ref,
    first_ref,
    second_ref,
    third_ref,
    bias_ref,
    head_ref,
    feat_out,
    skin_out,
    mine_out,
    theirs_out,
    head_s,
    bias_s,
    table_s,
    total_s,
    sums_s,
    hots_s,
    x_s,
    act_s,
    slope_s,
    back_s,
):
    width, members = feats_ref.shape
    subjects = code_ref.shape[0]
    table_cols = table_ref.shape[1]
    per_subject = table_cols // subjects
    influence = bone_ids_ref.shape[0]
    half = mine_out.shape[0]
    step = divisor(members, (512, 256, 128))

    head_s[...] = jnp.zeros_like(head_s)
    head_s[0:3, :] = head_ref[...].astype(F32)
    head_w = head_s[...].astype(BF16)
    bias_s[...] = jnp.zeros_like(bias_s)
    bias_s[0:3, :] = bias_ref[...]
    bias_cols = bias_s[...].T
    table = table_ref[...]
    table_hi = table.astype(BF16).astype(F32)
    table_s[...] = jnp.zeros_like(table_s)
    table_s[0:12, :] = table_hi
    table_s[16:28, :] = table - table_hi
    table_w = table_s[...].astype(BF16)
    code = code_ref[...]
    code_hi = code.astype(BF16).astype(F32)
    code_mid = (code - code_hi).astype(BF16).astype(F32)
    code_lo = code - code_hi - code_mid
    code_w = jnp.concatenate([code_hi, code_mid, code_lo], axis=0).T.astype(BF16)
    total_s[...] = jnp.zeros_like(total_s)
    sums_s[...] = jnp.zeros_like(sums_s)
    hot_rows = lax.broadcasted_iota(jnp.int32, (3 * subjects, step), 0) % subjects
    table_rows = lax.broadcasted_iota(jnp.int32, (table_cols, step), 0).astype(F32).astype(BF16)
    entry_rows = lax.broadcasted_iota(jnp.int32, (16, step), 0)
    one = jnp.ones((), BF16)
    zero = jnp.zeros((), BF16)

    def lane_sums(slot, value):
        total = value[:, 0:128]
        for lane in range(128, value.shape[1], 128):
            total = total + value[:, lane : lane + 128]
        sums_s[slot] += total

    def chunk(index, carry):
        spot = pl.ds(pl.multiple_of(index * step, step), step)
        subject = subj_ref[0:1, spot]
        hot = (hot_rows == subject).astype(F32).astype(BF16)
        x = (feats_ref[:, spot].astype(F32) + mm(code_w, hot)).astype(BF16)
        x_s[:, spot] = x
        hots_s[:, spot] = hot[0:16]
        act = x
        for layer, weight in enumerate((first_ref, second_ref, third_ref)):
            pre = mm(weight[...], act) + bias_cols[:, layer : layer + 1]
            sig = 0.5 * jnp.tanh(0.5 * pre) + 0.5
            value = pre * sig
            slope_s[layer, :, :] = sig + value * (1.0 - sig)
            act = value.astype(BF16)
            act_s[layer, :, spot] = act
        moved = mm(head_w, act)
        point = [canon_ref[axis, :, spot] + moved[axis : axis + 1] for axis in range(3)]
        grad = pos_ref[0, :, spot].astype(F32)
        for slot in range(1, pos_ref.shape[0]):
            grad = grad + pos_ref[slot, :, spot].astype(F32)
        quarter = entry_rows // 4
        place = entry_rows % 4
        grad_rows = jnp.where(
            quarter == 0,
            grad[0:1],
            jnp.where(quarter == 1, grad[1:2], jnp.where(quarter == 2, grad[2:3], 0.0)),
        )
        point_rows = jnp.where(
            place == 0, point[0], jnp.where(place == 1, point[1], jnp.where(place == 2, point[2], 1.0))
        )
        outer = grad_rows * point_rows
        blend = jnp.zeros((16, step), F32)
        bones = jnp.zeros((32, table_cols), F32)
        for member in range(influence):
            column = (subject * per_subject + bone_ids_ref[member, :, spot]).astype(F32).astype(BF16)
            onehot = jnp.where(table_rows == column, one, zero)
            both = mm(table_w, onehot)
            matrix = both[0:16] + both[16:32]
            skin_out[member, :, spot] = jnp.sum(outer * matrix, axis=0, keepdims=True)
            weight = skin_ref[member, :, spot]
            blend = blend + weight * matrix
            share = weight * outer
            share_hi = share.astype(BF16).astype(F32)
            parts = jnp.concatenate([share_hi, share - share_hi], axis=0).astype(BF16)
            bones = bones + mm(parts, onehot, NT)
        total_s[2 * half - 16 : 2 * half, 0:table_cols] += bones[0:16] + bones[16:32]
        pulled = blend * grad_rows
        shift = pulled[0:4] + pulled[4:8] + pulled[8:12]
        shift = jnp.where(entry_rows[0:4] < 3, shift, 0.0)
        shift = jnp.concatenate([shift, jnp.zeros((12, step), F32)], axis=0).astype(BF16)
        total_s[half - 16 : half, :] += mm(shift, act, NT)
        back = mm(head_w, shift, TN) * slope_s[2, :, :]
        lane_sums(2, back)
        back = back.astype(BF16)
        back_s[2, :, spot] = back
        back = mm(third_ref[...], back, TN) * slope_s[1, :, :]
        lane_sums(1, back)
        back = back.astype(BF16)
        back_s[1, :, spot] = back
        back = mm(second_ref[...], back, TN) * slope_s[0, :, :]
        back = back.astype(BF16)
        back_s[0, :, spot] = back
        feat_out[:, spot] = mm(first_ref[...], back, TN).astype(BF16)
        return carry

    lax.fori_loop(0, members // step, chunk, 0)
    total_s[0:width, :] = mm(back_s[2], act_s[1], NT)
    second = mm(back_s[1], act_s[0], NT)
    total_s[width : half - 16, :] = second[0 : width // 2]
    total_s[half : half + width // 2, :] = second[width // 2 :]
    total_s[half + width // 2 : 2 * half - 16, :] = mm(back_s[0], x_s[...], NT)
    by_subject = mm(back_s[0], hots_s[...], NT)[:, 0:subjects]
    by_hi = by_subject.astype(BF16).astype(F32)
    by_mid = (by_subject - by_hi).astype(BF16).astype(F32)
    by_lo = by_subject - by_hi - by_mid
    code_total = (
        mm(first_ref[...], by_hi.astype(BF16), TN)
        + mm(first_ref[...], by_mid.astype(BF16), TN)
        + mm(first_ref[...], by_lo.astype(BF16), TN)
    )
    bias_one = jnp.sum(by_subject, axis=1, keepdims=True)
    bias_two = jnp.sum(sums_s[1], axis=1, keepdims=True)
    bias_three = jnp.sum(sums_s[2], axis=1, keepdims=True)
    tail = jnp.concatenate(
        [code_total, bias_one, bias_two, bias_three, jnp.zeros((width, 128 - subjects - 3), F32)], axis=1
    ).T
    total_s[half - 16 + 3 : half - 16 + 6, :] = tail[subjects : subjects + 3]
    total_s[half - 8 : half, :] = tail[0:subjects]
    side = side_ref[0]
    mine_out[...] = (total_s[pl.ds(pl.multiple_of(side * half, 16), half), :] * factor).astype(BF16)
    theirs_out[...] = (total_s[pl.ds(pl.multiple_of((1 - side) * half, 16), half), :] * factor).astype(BF16)


def network(side, position, feats, code, subj, bone_ids, skin, canon, table, w1, w2, w3, bias, head, factor):
    width, members = feats.shape
    half = width + width // 2 + 16
    influence = bone_ids.shape[0]
    table_cols = table.shape[1]
    step = divisor(members, (512, 256, 128))
    return pl.pallas_call(
        functools.partial(network_kernel, factor),
        out_shape=(
            jax.ShapeDtypeStruct((width, members), BF16),
            jax.ShapeDtypeStruct((influence, 1, members), F32),
            jax.ShapeDtypeStruct((half, width), BF16),
            jax.ShapeDtypeStruct((half, width), BF16),
        ),
        in_specs=[SMEM] + [VMEM] * 13,
        out_specs=(VMEM,) * 4,
        scratch_shapes=[
            pltpu.VMEM((16, width), F32),
            pltpu.VMEM((8, width), F32),
            pltpu.VMEM((32, table_cols), F32),
            pltpu.VMEM((2 * half, width), F32),
            pltpu.VMEM((3, width, 128), F32),
            pltpu.VMEM((16, members), BF16),
            pltpu.VMEM((width, members), BF16),
            pltpu.VMEM((3, width, members), BF16),
            pltpu.VMEM((3, width, step), F32),
            pltpu.VMEM((3, width, members), BF16),
        ],
        compiler_params=params(),
    )(side, position, feats, code, subj, bone_ids, skin, canon, table, w1, w2, w3, bias, head)


def finish_kernel(side_ref, mine_ref, theirs_ref, first_out, second_out, third_out, bias_out, head_out, code_out, bone_out):
    width = first_out.shape[0]
    half = mine_ref.shape[0]
    subjects = code_out.shape[0]
    table_cols = bone_out.shape[1]

    def write(top, bottom):
        third_out[...] = top[0:width, :].astype(F32)
        second_out[0 : width // 2, :] = top[width : half - 16, :].astype(F32)
        second_out[width // 2 :, :] = bottom[0 : width // 2, :].astype(F32)
        first_out[...] = bottom[width // 2 : half - 16, :].astype(F32)
        small = top[half - 16 : half, :].astype(F32)
        head_out[...] = small[0:3]
        bias_out[...] = small[3:6]
        code_out[...] = small[8 : 8 + subjects]
        bone_out[...] = bottom[half - 16 : half, :].astype(F32)[0:12, 0:table_cols]

    @pl.when(side_ref[0] == 0)
    def _():
        write(mine_ref, theirs_ref)

    @pl.when(side_ref[0] != 0)
    def _():
        write(theirs_ref, mine_ref)


def finish(side, mine, theirs, width, subjects, table_cols):
    square = jax.ShapeDtypeStruct((width, width), F32)
    rows = jax.ShapeDtypeStruct((3, width), F32)
    return pl.pallas_call(
        finish_kernel,
        out_shape=(
            square,
            square,
            square,
            rows,
            rows,
            jax.ShapeDtypeStruct((subjects, width), F32),
            jax.ShapeDtypeStruct((12, table_cols), F32),
        ),
        in_specs=[SMEM, VMEM, VMEM],
        out_specs=(VMEM,) * 7,
        compiler_params=params(),
    )(side, mine, theirs)


def add(left, right):
    return (left.astype(F32) + right.astype(F32)).astype(BF16)


def swap(value, mask, count):
    return lax.ppermute(value, AXES, [(place, place ^ mask) for place in range(count)])


def sum_over_devices(mine, theirs, viewers, shards):
    count = viewers * shards
    pair = shards
    mine = add(mine, swap(theirs, pair, count))
    masks = []
    mask = 1
    while mask < count:
        if mask != pair:
            masks.append(mask)
        mask *= 2
    shift = len(masks) // 2
    rows = mine.shape[0]
    cut = rows // 32 * 16
    parts = [mine[:cut], mine[cut:]]
    orders = [masks, masks[shift:] + masks[:shift]]
    for stage in range(len(masks)):
        got = [swap(part, order[stage], count) for part, order in zip(parts, orders)]
        parts = [add(part, other) for part, other in zip(parts, got)]
    mine = jnp.concatenate(parts, axis=0)
    return mine, swap(mine, pair, count)


def to_owner(parts, viewers):
    got = [parts[0]]
    for away in range(1, viewers):
        perm = [(place, (place + away) % viewers) for place in range(viewers)]
        got.append(lax.ppermute(parts[away], "view", perm))
    return jnp.stack(got)


def body(
    entry_grads,
    vis_ids,
    feats,
    code_tab,
    subj_ids,
    bone_ids,
    skin_w,
    canon_pos,
    bone_tf,
    w_first,
    w_second,
    w_third,
    biases,
    w_head,
):
    width, _, members = feats.shape
    viewers = lax.axis_size("view")
    shards = lax.axis_size("gauss")
    attrs = entry_grads.shape[1]
    factor = 1.0 / math.sqrt(members * viewers * shards)
    view = lax.axis_index("view").astype(jnp.int32).reshape(1)
    side = view % 2
    position = scatter(view, entry_grads, vis_ids, 0, GROUP, members, viewers)
    position = to_owner(position, viewers)
    others = scatter(view, entry_grads, vis_ids, GROUP, attrs - GROUP, members, viewers)
    others = to_owner(others, viewers)
    feat_grads, skin_grads, mine, theirs = network(
        side,
        position,
        feats[:, 0],
        code_tab.T,
        subj_ids,
        bone_ids,
        skin_w,
        canon_pos,
        bone_tf,
        w_first,
        w_second,
        w_third,
        biases,
        w_head,
        factor,
    )
    mine, theirs = sum_over_devices(mine, theirs, viewers, shards)
    first, second, third, bias, head, code, bone = finish(
        side, mine, theirs, width, code_tab.shape[1], bone_tf.shape[1]
    )
    attr = jnp.concatenate(
        [jnp.sum(position.astype(F32), axis=0), jnp.sum(others.astype(F32), axis=0)[: attrs - GROUP]], axis=0
    )
    return (
        attr[:, None, :],
        feat_grads[:, None, :],
        skin_grads,
        first,
        second,
        third,
        bias,
        head,
        code.T,
        bone,
    )


def solution(mesh):
    placed = (
        P("view", None, "gauss"),
        P("view", "gauss"),
        P(None, "gauss", "view"),
        P(),
        P("gauss", "view"),
        P(None, "gauss", "view"),
        P(None, "gauss", "view"),
        P(None, "gauss", "view"),
        P(),
        P(),
        P(),
        P(),
        P(),
        P(),
    )
    return jax.shard_map(
        body,
        mesh=mesh,
        in_specs=placed,
        out_specs=(
            P(None, "gauss", "view"),
            P(None, "gauss", "view"),
            P(None, "gauss", "view"),
            P(),
            P(),
            P(),
            P(),
            P(),
            P(),
            P(),
        ),
        check_vma=False,
    )
```

time: 232 us -> 75 us (0.32)
  waiting for transfers between devices: 84.1 us -> 10.2 us
  Pallas kernels: 0 us -> 43.3 us
  blocking collectives: 43.1 us -> 0 us
  other arithmetic: 38.9 us -> 0.45 us
  matrix products: 30.2 us -> 0 us
  local copies, waits for them, and re-layouts: 20.4 us -> 3.15 us
  starting transfers between devices: 0.12 us -> 16.7 us
  between operations: 14.4 us -> 0.98 us
    psum x1 -> x0, waiting for transfers between devices: 84 us -> none  [body(): lax.psum((first, second, third, bias_one, bias_two, bias_three, head, cod...]
    pallas_call x0 -> x4, Pallas kernels: none -> 43.3 us  [the longest x2 29.8 us: scatter(): pl.pallas_call(functools.partial(scatter_kernel, first_row, rows, viewers...]
    psum x1 -> x0, blocking collectives: 43.1 us -> none  [body(): lax.psum((first, second, third, bias_one, bias_two, bias_three, head, cod...]
    dot_general x22 -> x0, matrix products: 30.2 us -> none  [the longest x4 7.91 us: body(): lax.dot_general(contribution, onehot, (((1,), (1,)), ((), ())), precision...]
    scatter-add x1 -> x0, other arithmetic: 29.7 us -> none  [body(): partial_value = jnp.zeros((entry_grads.shape[1], member_count * viewers),...]
    ppermute x0 -> x12, starting transfers between devices: none -> 16.7 us  [the longest x10 15.7 us: swap(): lax.ppermute(value, AXES, [(place, place ^ mask) for place in range(count)])]
    unnamed x84 -> x28, local copies, waits for them, and re-layouts: 13.5 us -> 1.86 us
    ppermute x0 -> x12, waiting for transfers between devices: none -> 10.2 us  [the longest x10 10.2 us: swap(): lax.ppermute(value, AXES, [(place, place ^ mask) for place in range(count)])]
  transfers between devices with their start and end apart: 3 -> 12, of which waited for: 1 -> 8; matrix products, arithmetic and copies ran while one was open for 20% -> 2% of each run, Pallas kernels for 0% -> 21%
where the time goes in v1:
time: 75 us; the launch traced here: 74.8 us
  Pallas kernels  43.3 us (58%)
  starting transfers between devices  16.7 us (22%)
  waiting for transfers between devices  10.2 us (14%)
  local copies, waits for them, and re-layouts  3.15 us (4%)
  between operations  0.98 us (1%)
    pallas_call x2, Pallas kernels, scatter(): pl.pallas_call(functools.partial(scatter_kernel, first_row, rows, viewers...  29.8 us
    ppermute x10, starting transfers between devices, swap(): lax.ppermute(value, AXES, [(place, place ^ mask) for place in range(count)])  15.7 us
    pallas_call x1, Pallas kernels, network(): pl.pallas_call(functools.partial(network_kernel, factor), out_shape=(jax....  12.5 us
    ppermute x10, waiting for transfers between devices, swap(): lax.ppermute(value, AXES, [(place, place ^ mask) for place in range(count)])  10.2 us
    unnamed x28, local copies, waits for them, and re-layouts  1.86 us
  transfers between devices with their start and end apart: 12, of which 8 were waited for; matrix products, arithmetic and copies ran while one was open for 2% of the time, Pallas kernels for 21%

profile of v1, /device:TPU:0, one launch (start us, length us, event | category | flops | bytes accessed | tf_op | source)
XLA Modules:
  0.0 74.8 jit_solution(9469689569632745398)
XLA Ops:
  0.7 0.0 copy-start
  0.7 1.1 %copy-done = bf16[1,59,5120]{2,1,0:T(8,128)(2,1)S(1)} copy-done((bf16[1,59,5120]{2,1,0:T(8,128)(2,1)S(1)}, bf16[1,59,5120]{2,1,0:T(8,128)(2,1)}, u32[]{:S(2)}) %copy-start) | copy-done | bytes 604184
  1.7 0.0 copy-start.5
  1.7 0.7 copy-done.5
  2.5 0.0 copy-start.1
  2.5 0.0 copy-start.2
  2.5 0.0 copy-start.3
  2.5 0.0 copy-start.4
  2.5 0.0 copy-start.6
  2.5 0.0 copy-start.7
  2.5 0.0 copy-start.8
  2.5 0.0 copy-start.9
  2.5 0.0 copy-start.10
  2.5 0.0 copy-start.11
  2.5 0.0 copy-start.12
  2.6 0.0 copy-start.13
  2.6 14.2 %shard_map.213 = bf16[2,16,2560]{2,1,0:T(8,128)(2,1)S(1)} custom-call(s32[1]{0:T(128)} %bitcast.view_ref, bf16[1,59,5120]{2,1,0:T(8,128)(2,1)S(1)} %copy-done, s32[1,5120]{1,0:T(1,128)S(1)} %copy-done.5), custom_call_target="tpu_custom_call" | custom-call | tf_op jit(solution)/shard_map/pallas_call | solution.py:81
  16.8 0.5 collective-permute-start
  17.3 15.6 %shard_map.214 = bf16[2,48,2560]{2,1,0:T(8,128)(2,1)S(1)} custom-call(s32[1]{0:T(128)} %bitcast.view_ref, bf16[1,59,5120]{2,1,0:T(8,128)(2,1)S(1)} %copy-done, s32[1,5120]{1,0:T(1,128)S(1)} %copy-done.5), custom_call_target="tpu_custom_call" | custom-call | tf_op jit(solution)/shard_map/pallas_call | solution.py:81
  32.9 0.0 collective-permute-done
  33.0 0.0 copy-done.1
  33.0 0.0 copy-done.2
  33.0 0.0 copy-done.3
  33.0 0.0 copy-done.4
  33.0 0.0 copy-done.6
  33.0 0.0 copy-done.7
  33.0 0.0 copy-done.8
  33.1 0.0 copy-done.9
  33.1 0.0 copy-done.10
  33.1 0.0 copy-done.11
  33.1 0.0 copy-done.12
  33.1 0.0 copy-done.13
  33.1 12.5 %shard_map.215 = (bf16[256,2560]{1,0:T(8,128)(2,1)}, f32[4,1,2560]{2,1,0:T(1,128)}, bf16[400,256]{1,0:T(8,128)(2,1)S(1)}, bf16[400,256]{1,0:T(8,128)(2,1)S(1)}) custom-call(s32[1]{0:T(128)S(6)} %select_n.7.side_ref, bf16[2,16,2560]{2,1,0:T(8,128)(2,1)S(1)} %pad_maximum_fusion.2.pos_ref, bf16[256,2560]{1,0:T(8,128)(2,1)S(1)} %bitcast.12, ...), custom_call_target="tpu_custom_call" | custom-call | tf_op jit(solution)/shard_map/pallas_call | solution.py:260
  45.6 0.1 collective-permute-start.2
  45.8 0.5 collective-permute-start.1
  46.3 0.8 %collective-permute-done.2 = bf16[400,256]{1,0:T(8,128)(2,1)S(1)} collective-permute-done((bf16[400,256]{1,0:T(8,128)(2,1)S(1)}, bf16[400,256]{1,0:T(8,128)(2,1)S(1)}, u32[]{:S(2)}, u32[]{:S(2)}) %collective-permute-start.2) | collective-permute-done | bytes 204832 | tf_op jit(solution)/shard_map/ppermute | solution.py:337
  47.1 0.1 add_convert_fusion
  47.2 2.7 %collective-permute-start.3 = (bf16[192,256]{1,0:T(8,128)(2,1)S(1)}, bf16[192,256]{1,0:T(8,128)(2,1)S(1)}, u32[]{:S(2)}, u32[]{:S(2)}) collective-permute-start(bf16[192,256]{1,0:T(8,128)(2,1)S(1)} %slice.33), channel_id=1, source_target_pairs={{0,1},{1,0},{2,3},{3,2},{4,5},{5,4},{6,7},{7,6},{8,9},{9,8},{10,11... | collective-permute-start | bytes 294920 | tf_op jit(solution)/shard_map/ppermute | solution.py:337
  49.9 0.0 collective-permute-done.1
  49.9 0.1 convert_reduce_fusion
  50.0 1.6 %collective-permute-start.7 = (bf16[208,256]{1,0:T(8,128)(2,1)S(1)}, bf16[208,256]{1,0:T(8,128)(2,1)S(1)}, u32[]{:S(2)}, u32[]{:S(2)}) collective-permute-start(bf16[208,256]{1,0:T(8,128)(2,1)S(1)} %slice.34), channel_id=1, source_target_pairs={{0,4},{1,5},{2,6},{3,7},{4,0},{5,1},{6,2},{7,3},{8,12},{9,13},{10,... | collective-permute-start | bytes 319496 | tf_op jit(solution)/shard_map/ppermute | solution.py:337
  51.7 1.5 %collective-permute-done.3 = bf16[192,256]{1,0:T(8,128)(2,1)S(1)} collective-permute-done((bf16[192,256]{1,0:T(8,128)(2,1)S(1)}, bf16[192,256]{1,0:T(8,128)(2,1)S(1)}, u32[]{:S(2)}, u32[]{:S(2)}) %collective-permute-start.3) | collective-permute-done | bytes 98336 | tf_op jit(solution)/shard_map/ppermute | solution.py:337
  53.3 1.8 %collective-permute-start.4 = (bf16[192,256]{1,0:T(8,128)(2,1)S(1)}, bf16[192,256]{1,0:T(8,128)(2,1)S(1)}, u32[]{:S(2)}, u32[]{:S(2)}) collective-permute-start(bf16[192,256]{1,0:T(8,128)(2,1)S(1)} %add_convert_fusion.8), channel_id=1, source_target_pairs={{0,2},{1,3},{2,0},{3,1},{4,6},{5,7},{6,4},{7,5},{8,10},{9,11},{10,... | collective-permute-start | bytes 294920 | tf_op jit(solution)/shard_map/ppermute | solution.py:337
  55.1 0.0 collective-permute-done.7
  55.1 2.7 %collective-permute-start.8 = (bf16[208,256]{1,0:T(8,128)(2,1)S(1)}, bf16[208,256]{1,0:T(8,128)(2,1)S(1)}, u32[]{:S(2)}, u32[]{:S(2)}) collective-permute-start(bf16[208,256]{1,0:T(8,128)(2,1)S(1)} %add_convert_fusion.4), channel_id=1, source_target_pairs={{0,8},{1,9},{2,10},{3,11},{4,12},{5,13},{6,14},{7,15},{8,0},{9,1},... | collective-permute-start | bytes 319496 | tf_op jit(solution)/shard_map/ppermute | solution.py:337
  57.8 0.2 collective-permute-done.4
  58.0 1.9 %collective-permute-start.5 = (bf16[192,256]{1,0:T(8,128)(2,1)S(1)}, bf16[192,256]{1,0:T(8,128)(2,1)S(1)}, u32[]{:S(2)}, u32[]{:S(2)}) collective-permute-start(bf16[192,256]{1,0:T(8,128)(2,1)S(1)} %add_convert_fusion.7), channel_id=1, source_target_pairs={{0,4},{1,5},{2,6},{3,7},{4,0},{5,1},{6,2},{7,3},{8,12},{9,13},{10,... | collective-permute-start | bytes 294920 | tf_op jit(solution)/shard_map/ppermute | solution.py:337
  59.9 2.8 %collective-permute-done.8 = bf16[208,256]{1,0:T(8,128)(2,1)S(1)} collective-permute-done((bf16[208,256]{1,0:T(8,128)(2,1)S(1)}, bf16[208,256]{1,0:T(8,128)(2,1)S(1)}, u32[]{:S(2)}, u32[]{:S(2)}) %collective-permute-start.8) | collective-permute-done | bytes 106528 | tf_op jit(solution)/shard_map/ppermute | solution.py:337
  62.7 1.6 %collective-permute-start.9 = (bf16[208,256]{1,0:T(8,128)(2,1)S(1)}, bf16[208,256]{1,0:T(8,128)(2,1)S(1)}, u32[]{:S(2)}, u32[]{:S(2)}) collective-permute-start(bf16[208,256]{1,0:T(8,128)(2,1)S(1)} %add_convert_fusion.3), channel_id=1, source_target_pairs={{0,1},{1,0},{2,3},{3,2},{4,5},{5,4},{6,7},{7,6},{8,9},{9,8},{10,11... | collective-permute-start | bytes 319496 | tf_op jit(solution)/shard_map/ppermute | solution.py:337
  64.2 0.0 collective-permute-done.5
  64.3 1.7 %collective-permute-start.6 = (bf16[192,256]{1,0:T(8,128)(2,1)S(1)}, bf16[192,256]{1,0:T(8,128)(2,1)S(1)}, u32[]{:S(2)}, u32[]{:S(2)}) collective-permute-start(bf16[192,256]{1,0:T(8,128)(2,1)S(1)} %add_convert_fusion.6), channel_id=1, source_target_pairs={{0,8},{1,9},{2,10},{3,11},{4,12},{5,13},{6,14},{7,15},{8,0},{9,1},... | collective-permute-start | bytes 294920 | tf_op jit(solution)/shard_map/ppermute | solution.py:337
  65.9 1.5 %collective-permute-done.9 = bf16[208,256]{1,0:T(8,128)(2,1)S(1)} collective-permute-done((bf16[208,256]{1,0:T(8,128)(2,1)S(1)}, bf16[208,256]{1,0:T(8,128)(2,1)S(1)}, u32[]{:S(2)}, u32[]{:S(2)}) %collective-permute-start.9) | collective-permute-done | bytes 106528 | tf_op jit(solution)/shard_map/ppermute | solution.py:337
  67.5 1.5 %collective-permute-start.10 = (bf16[208,256]{1,0:T(8,128)(2,1)S(1)}, bf16[208,256]{1,0:T(8,128)(2,1)S(1)}, u32[]{:S(2)}, u32[]{:S(2)}) collective-permute-start(bf16[208,256]{1,0:T(8,128)(2,1)S(1)} %add_convert_fusion.2), channel_id=1, source_target_pairs={{0,2},{1,3},{2,0},{3,1},{4,6},{5,7},{6,4},{7,5},{8,10},{9,11},{10,... | collective-permute-start | bytes 319496 | tf_op jit(solution)/shard_map/ppermute | solution.py:337
  69.0 1.9 %collective-permute-done.6 = bf16[192,256]{1,0:T(8,128)(2,1)S(1)} collective-permute-done((bf16[192,256]{1,0:T(8,128)(2,1)S(1)}, bf16[192,256]{1,0:T(8,128)(2,1)S(1)}, u32[]{:S(2)}, u32[]{:S(2)}) %collective-permute-start.6) | collective-permute-done | bytes 98336 | tf_op jit(solution)/shard_map/ppermute | solution.py:337
  70.9 1.3 %collective-permute-done.10 = bf16[208,256]{1,0:T(8,128)(2,1)S(1)} collective-permute-done((bf16[208,256]{1,0:T(8,128)(2,1)S(1)}, bf16[208,256]{1,0:T(8,128)(2,1)S(1)}, u32[]{:S(2)}, u32[]{:S(2)}) %collective-permute-start.10) | collective-permute-done | bytes 106528 | tf_op jit(solution)/shard_map/ppermute | solution.py:337
  72.3 0.1 collective-permute-start.11
  72.4 1.2 %broadcast_in_dim.6 = f32[59,1,2560]{2,1,0:T(1,128)} reshape(f32[59,2560]{1,0:T(8,128)S(1)} %pad_maximum_fusion) | data formatting | bytes 1208320 | tf_op jit(solution)/shard_map/broadcast_in_dim | solution.py:422
  73.7 0.2 collective-permute-done.11.theirs_ref
  73.8 0.9 %shard_map.216 = (f32[256,256]{1,0:T(8,128)}, f32[256,256]{1,0:T(8,128)}, f32[256,256]{1,0:T(8,128)}, f32[3,256]{1,0:T(4,128)}, f32[3,256]{1,0:T(4,128)}, /*index=5*/f32[8,256]{1,0:T(8,128)}, f32[12,192]{1,0:T(8,128)}) custom-call(s32[1]{0:T(128)S(6)} %select_n.7.side_ref, bf16[400,256]{1,0:T(8,128)(2,1)S(1)} %pad_maximum_fusion.1.mine_ref, ...), custom_call_target="tpu_custom_call" | custom-call | tf_op jit(solution)/shard_map/pallas_call | solution.py:315
  (16 shorter events, 0.4 us)
Async XLA Ops:
  0.7 1.1 %copy-start = (bf16[1,59,5120]{2,1,0:T(8,128)(2,1)S(1)}, bf16[1,59,5120]{2,1,0:T(8,128)(2,1)}, u32[]{:S(2)}) copy-start(bf16[1,59,5120]{2,1,0:T(8,128)(2,1)} %grads_ref.3) | copy-start | bytes 1812484
  1.7 0.7 copy-start.5
  2.5 30.5 %copy-start.1 = (bf16[256,1,2560]{2,0,1:T(8,128)(2,1)S(1)}, bf16[256,1,2560]{2,0,1:T(8,128)(2,1)}, u32[]{:S(2)}) copy-start(bf16[256,1,2560]{2,0,1:T(8,128)(2,1)} %param.16) | copy-start | bytes 3932164
  2.5 30.5 %copy-start.2 = (bf16[256,256]{1,0:T(8,128)(2,1)S(1)}, bf16[256,256]{1,0:T(8,128)(2,1)}, u32[]{:S(2)}) copy-start(bf16[256,256]{1,0:T(8,128)(2,1)} %first_ref.1) | copy-start | bytes 393220
  2.5 30.5 %copy-start.3 = (bf16[256,256]{1,0:T(8,128)(2,1)S(1)}, bf16[256,256]{1,0:T(8,128)(2,1)}, u32[]{:S(2)}) copy-start(bf16[256,256]{1,0:T(8,128)(2,1)} %second_ref.1) | copy-start | bytes 393220
  2.5 30.5 %copy-start.4 = (bf16[256,256]{1,0:T(8,128)(2,1)S(1)}, bf16[256,256]{1,0:T(8,128)(2,1)}, u32[]{:S(2)}) copy-start(bf16[256,256]{1,0:T(8,128)(2,1)} %third_ref.1) | copy-start | bytes 393220
  2.5 30.5 %copy-start.6 = (s32[4,1,2560]{2,1,0:T(1,128)S(1)}, s32[4,1,2560]{2,1,0:T(1,128)}, u32[]{:S(2)}) copy-start(s32[4,1,2560]{2,1,0:T(1,128)} %bone_ids_ref.1) | copy-start | bytes 122884
  2.5 30.5 %copy-start.7 = (f32[4,1,2560]{2,1,0:T(1,128)S(1)}, f32[4,1,2560]{2,1,0:T(1,128)}, u32[]{:S(2)}) copy-start(f32[4,1,2560]{2,1,0:T(1,128)} %skin_ref.1) | copy-start | bytes 122884
  2.5 30.5 %copy-start.8 = (f32[3,1,2560]{2,1,0:T(1,128)S(1)}, f32[3,1,2560]{2,1,0:T(1,128)}, u32[]{:S(2)}) copy-start(f32[3,1,2560]{2,1,0:T(1,128)} %canon_ref.1) | copy-start | bytes 92164
  2.5 30.5 %copy-start.9 = (f32[12,192]{1,0:T(8,128)S(1)}, f32[12,192]{1,0:T(8,128)}, u32[]{:S(2)}) copy-start(f32[12,192]{1,0:T(8,128)} %table_ref.1) | copy-start | bytes 27652
  2.5 30.5 %copy-start.10 = (s32[1,2560]{1,0:T(1,128)S(1)}, s32[1,2560]{1,0:T(1,128)}, u32[]{:S(2)}) copy-start(s32[1,2560]{1,0:T(1,128)} %subj_ref.1) | copy-start | bytes 30724
  2.5 30.5 %copy-start.11 = (f32[256,8]{0,1:T(8,128)S(1)}, f32[256,8]{0,1:T(8,128)}, u32[]{:S(2)}) copy-start(f32[256,8]{0,1:T(8,128)} %param.17) | copy-start | bytes 24580
  2.5 30.5 %copy-start.12 = (f32[3,256]{1,0:T(4,128)S(1)}, f32[3,256]{1,0:T(4,128)}, u32[]{:S(2)}) copy-start(f32[3,256]{1,0:T(4,128)} %bias_ref.1) | copy-start | bytes 9220
  2.6 30.5 %copy-start.13 = (bf16[3,256]{1,0:T(4,128)(2,1)S(1)}, bf16[3,256]{1,0:T(4,128)(2,1)}, u32[]{:S(2)}) copy-start(bf16[3,256]{1,0:T(4,128)(2,1)} %head_ref.1) | copy-start | bytes 4612
  16.8 16.1 %collective-permute-start = (bf16[16,2560]{1,0:T(8,128)(2,1)S(1)}, bf16[16,2560]{1,0:T(8,128)(2,1)S(1)}, u32[]{:S(2)}, u32[]{:S(2)}) collective-permute-start(bf16[16,2560]{1,0:T(8,128)(2,1)S(1)} %get-tuple-element.35), channel_id=1, source_target_pairs={{0,16},{16,0},{1,17},{17,1},{2,18},{18,2},{3,19},{19,3},{4,20},{20... | collective-permute-start | bytes 245768 | tf_op jit(solution)/shard_map/ppermute | solution.py:366
  45.6 1.5 %collective-permute-start.2 = (bf16[400,256]{1,0:T(8,128)(2,1)S(1)}, bf16[400,256]{1,0:T(8,128)(2,1)S(1)}, u32[]{:S(2)}, u32[]{:S(2)}) collective-permute-start(bf16[400,256]{1,0:T(8,128)(2,1)S(1)} %get-tuple-element.24), channel_id=1, source_target_pairs={{0,16},{1,17},{2,18},{3,19},{4,20},{5,21},{6,22},{7,23},{8,24},{9,... | collective-permute-start | bytes 614408 | tf_op jit(solution)/shard_map/ppermute | solution.py:337
  45.8 4.2 %collective-permute-start.1 = (bf16[48,2560]{1,0:T(8,128)(2,1)S(1)}, bf16[48,2560]{1,0:T(8,128)(2,1)S(1)}, u32[]{:S(2)}, u32[]{:S(2)}) collective-permute-start(bf16[48,2560]{1,0:T(8,128)(2,1)S(1)} %get-tuple-element.33), channel_id=1, source_target_pairs={{0,16},{16,0},{1,17},{17,1},{2,18},{18,2},{3,19},{19,3},{4,20},{20... | collective-permute-start | bytes 737288 | tf_op jit(solution)/shard_map/ppermute | solution.py:366
  47.2 6.0 %collective-permute-start.3 = (bf16[192,256]{1,0:T(8,128)(2,1)S(1)}, bf16[192,256]{1,0:T(8,128)(2,1)S(1)}, u32[]{:S(2)}, u32[]{:S(2)}) collective-permute-start(bf16[192,256]{1,0:T(8,128)(2,1)S(1)} %slice.33), channel_id=1, source_target_pairs={{0,1},{1,0},{2,3},{3,2},{4,5},{5,4},{6,7},{7,6},{8,9},{9,8},{10,11... | collective-permute-start | bytes 294920 | tf_op jit(solution)/shard_map/ppermute | solution.py:337
  50.0 5.1 %collective-permute-start.7 = (bf16[208,256]{1,0:T(8,128)(2,1)S(1)}, bf16[208,256]{1,0:T(8,128)(2,1)S(1)}, u32[]{:S(2)}, u32[]{:S(2)}) collective-permute-start(bf16[208,256]{1,0:T(8,128)(2,1)S(1)} %slice.34), channel_id=1, source_target_pairs={{0,4},{1,5},{2,6},{3,7},{4,0},{5,1},{6,2},{7,3},{8,12},{9,13},{10,... | collective-permute-start | bytes 319496 | tf_op jit(solution)/shard_map/ppermute | solution.py:337
  53.3 4.7 %collective-permute-start.4 = (bf16[192,256]{1,0:T(8,128)(2,1)S(1)}, bf16[192,256]{1,0:T(8,128)(2,1)S(1)}, u32[]{:S(2)}, u32[]{:S(2)}) collective-permute-start(bf16[192,256]{1,0:T(8,128)(2,1)S(1)} %add_convert_fusion.8), channel_id=1, source_target_pairs={{0,2},{1,3},{2,0},{3,1},{4,6},{5,7},{6,4},{7,5},{8,10},{9,11},{10,... | collective-permute-start | bytes 294920 | tf_op jit(solution)/shard_map/ppermute | solution.py:337
  55.1 7.5 %collective-permute-start.8 = (bf16[208,256]{1,0:T(8,128)(2,1)S(1)}, bf16[208,256]{1,0:T(8,128)(2,1)S(1)}, u32[]{:S(2)}, u32[]{:S(2)}) collective-permute-start(bf16[208,256]{1,0:T(8,128)(2,1)S(1)} %add_convert_fusion.4), channel_id=1, source_target_pairs={{0,8},{1,9},{2,10},{3,11},{4,12},{5,13},{6,14},{7,15},{8,0},{9,1},... | collective-permute-start | bytes 319496 | tf_op jit(solution)/shard_map/ppermute | solution.py:337
  58.0 6.3 %collective-permute-start.5 = (bf16[192,256]{1,0:T(8,128)(2,1)S(1)}, bf16[192,256]{1,0:T(8,128)(2,1)S(1)}, u32[]{:S(2)}, u32[]{:S(2)}) collective-permute-start(bf16[192,256]{1,0:T(8,128)(2,1)S(1)} %add_convert_fusion.7), channel_id=1, source_target_pairs={{0,4},{1,5},{2,6},{3,7},{4,0},{5,1},{6,2},{7,3},{8,12},{9,13},{10,... | collective-permute-start | bytes 294920 | tf_op jit(solution)/shard_map/ppermute | solution.py:337
  62.7 4.8 %collective-permute-start.9 = (bf16[208,256]{1,0:T(8,128)(2,1)S(1)}, bf16[208,256]{1,0:T(8,128)(2,1)S(1)}, u32[]{:S(2)}, u32[]{:S(2)}) collective-permute-start(bf16[208,256]{1,0:T(8,128)(2,1)S(1)} %add_convert_fusion.3), channel_id=1, source_target_pairs={{0,1},{1,0},{2,3},{3,2},{4,5},{5,4},{6,7},{7,6},{8,9},{9,8},{10,11... | collective-permute-start | bytes 319496 | tf_op jit(solution)/shard_map/ppermute | solution.py:337
  64.3 6.6 %collective-permute-start.6 = (bf16[192,256]{1,0:T(8,128)(2,1)S(1)}, bf16[192,256]{1,0:T(8,128)(2,1)S(1)}, u32[]{:S(2)}, u32[]{:S(2)}) collective-permute-start(bf16[192,256]{1,0:T(8,128)(2,1)S(1)} %add_convert_fusion.6), channel_id=1, source_target_pairs={{0,8},{1,9},{2,10},{3,11},{4,12},{5,13},{6,14},{7,15},{8,0},{9,1},... | collective-permute-start | bytes 294920 | tf_op jit(solution)/shard_map/ppermute | solution.py:337
  67.5 4.8 %collective-permute-start.10 = (bf16[208,256]{1,0:T(8,128)(2,1)S(1)}, bf16[208,256]{1,0:T(8,128)(2,1)S(1)}, u32[]{:S(2)}, u32[]{:S(2)}) collective-permute-start(bf16[208,256]{1,0:T(8,128)(2,1)S(1)} %add_convert_fusion.2), channel_id=1, source_target_pairs={{0,2},{1,3},{2,0},{3,1},{4,6},{5,7},{6,4},{7,5},{8,10},{9,11},{10,... | collective-permute-start | bytes 319496 | tf_op jit(solution)/shard_map/ppermute | solution.py:337
  72.3 1.5 %collective-permute-start.11 = (bf16[400,256]{1,0:T(8,128)(2,1)S(1)}, bf16[400,256]{1,0:T(8,128)(2,1)S(1)}, u32[]{:S(2)}, u32[]{:S(2)}) collective-permute-start(bf16[400,256]{1,0:T(8,128)(2,1)S(1)} %pad_maximum_fusion.1.mine_ref), channel_id=1, source_target_pairs={{0,16},{1,17},{2,18},{3,19},{4,20},{5,21},{6,22},{7,23},{8,24},{9,... | collective-permute-start | bytes 614408 | tf_op jit(solution)/shard_map/ppermute | solution.py:337

commit v2 on v1

--- a/solution.py
+++ b/solution.py
@@ -34,16 +34,15 @@
     return total
 
 
-def scatter_kernel(first_row, rows, viewers, view_ref, grads_ref, ids_ref, out_ref, acc_ref):
+def scatter_kernel(first_row, rows, viewers, view_ref, grads_ref, ids_ref, out_ref, acc_ref, left_ref):
     entries = ids_ref.shape[1]
-    blocks = acc_ref.shape[0]
-    groups = acc_ref.shape[1] // GROUP
-    step = divisor(entries, (1024, 512, 256, 128))
+    step = left_ref.shape[1]
+    height = out_ref.shape[1]
+    blocks = acc_ref.shape[0] // height
+    groups = height // GROUP
     low_rows = lax.broadcasted_iota(jnp.int32, (LOW, step), 0).astype(F32).astype(BF16)
     one = jnp.ones((), BF16)
     zero = jnp.zeros((), BF16)
-
-    acc_ref[...] = jnp.zeros_like(acc_ref)
 
     def chunk(index, carry):
         spot = pl.ds(pl.multiple_of(index * step, step), step)
@@ -51,7 +50,7 @@
         high = lax.shift_right_logical(ids, 8).astype(F32).astype(BF16)
         low = lax.bitwise_and(ids, LOW - 1).astype(F32).astype(BF16)
         hot = jnp.where(low_rows == low, one, zero)
-        values = []
+        high = jnp.broadcast_to(high, (GROUP, step))
         for group in range(groups):
             begin = first_row + group * GROUP
             count = min(GROUP, first_row + rows - begin)
@@ -60,30 +59,40 @@
                 piece = jnp.concatenate(
                     [piece.astype(F32), jnp.zeros((GROUP - count, step), F32)], axis=0
                 ).astype(BF16)
-            values.append(piece)
-        high = jnp.broadcast_to(high, (GROUP, step))
-        for block in range(blocks):
-            inside = high == jnp.asarray(block, BF16)
-            left = jnp.concatenate([jnp.where(inside, v, zero) for v in values], axis=0)
-            acc_ref[block] += mm(left, hot, NT)
+            for block in range(blocks):
+                place = block * height + group * GROUP
+                left_ref[place : place + GROUP, :] = jnp.where(high == jnp.asarray(block, BF16), piece, zero)
+        product = mm(left_ref[...], hot, NT)
+
+        @pl.when(index == 0)
+        def _():
+            acc_ref[...] = product
+
+        @pl.when(index != 0)
+        def _():
+            acc_ref[...] += product
+
         return carry
 
     lax.fori_loop(0, entries // step, chunk, 0)
     per = blocks // viewers
     for block in range(blocks):
         slot = lax.rem(block // per - view_ref[0] + viewers, viewers)
-        out_ref[slot, :, (block % per) * LOW : (block % per + 1) * LOW] = acc_ref[block].astype(BF16)
+        out_ref[slot, :, (block % per) * LOW : (block % per + 1) * LOW] = acc_ref[
+            block * height : (block + 1) * height, :
+        ].astype(BF16)
 
 
 def scatter(view, entry_grads, vis_ids, first_row, rows, members, viewers):
-    groups = -(-rows // GROUP)
+    height = -(-rows // GROUP) * GROUP
     blocks = members * viewers // LOW
+    step = divisor(vis_ids.shape[1], (2560, 2048, 1024, 512, 256, 128))
     return pl.pallas_call(
         functools.partial(scatter_kernel, first_row, rows, viewers),
-        out_shape=jax.ShapeDtypeStruct((viewers, groups * GROUP, members), BF16),
+        out_shape=jax.ShapeDtypeStruct((viewers, height, members), BF16),
         in_specs=[SMEM, VMEM, VMEM],
         out_specs=VMEM,
-        scratch_shapes=[pltpu.VMEM((blocks, groups * GROUP, LOW), F32)],
+        scratch_shapes=[pltpu.VMEM((blocks * height, LOW), F32), pltpu.VMEM((blocks * height, step), BF16)],
         compiler_params=params(),
     )(view, entry_grads, vis_ids)
 

time: 75 us -> 49.6 us (0.66)
  Pallas kernels: 43.3 us -> 17.9 us
    pallas_call x2, Pallas kernels: 29.8 us -> 4.5 us  [scatter(): pl.pallas_call(functools.partial(scatter_kernel, first_row, rows, viewers...]
  transfers between devices with their start and end apart: 12 -> 12, of which waited for: 8 -> 8; matrix products, arithmetic and copies ran while one was open for 2% -> 3% of each run, Pallas kernels for 21% -> 6%
where the time goes in v2:
time: 49.6 us; the launch traced here: 49.4 us
  Pallas kernels  17.9 us (36%)
  starting transfers between devices  16.7 us (34%)
  waiting for transfers between devices  10.2 us (21%)
  local copies, waits for them, and re-layouts  3.15 us (6%)
  between operations  0.98 us (2%)
    ppermute x10, starting transfers between devices, swap(): lax.ppermute(value, AXES, [(place, place ^ mask) for place in range(count)])  15.7 us
    pallas_call x1, Pallas kernels, network(): pl.pallas_call(functools.partial(network_kernel, factor), out_shape=(jax....  12.5 us
    ppermute x10, waiting for transfers between devices, swap(): lax.ppermute(value, AXES, [(place, place ^ mask) for place in range(count)])  10.2 us
    pallas_call x2, Pallas kernels, scatter(): pl.pallas_call(functools.partial(scatter_kernel, first_row, rows, viewers...  4.5 us
    unnamed x28, local copies, waits for them, and re-layouts  1.86 us
    broadcast_in_dim x1, local copies, waits for them, and re-layouts, body(): attr[:, None, :]  1.23 us
    ppermute x2, starting transfers between devices, to_owner(): got.append(lax.ppermute(parts[away], 'view', perm))  1.06 us
  transfers between devices with their start and end apart: 12, of which 8 were waited for; matrix products, arithmetic and copies ran while one was open for 3% of the time, Pallas kernels for 6%

profile of v2, /device:TPU:0, one launch (start us, length us, event | category | flops | bytes accessed | tf_op | source)
XLA Modules:
  0.0 49.4 jit_solution(8817629687252133973)
XLA Ops:
  0.7 0.0 copy-start
  0.7 1.1 %copy-done = bf16[1,59,5120]{2,1,0:T(8,128)(2,1)S(1)} copy-done((bf16[1,59,5120]{2,1,0:T(8,128)(2,1)S(1)}, bf16[1,59,5120]{2,1,0:T(8,128)(2,1)}, u32[]{:S(2)}) %copy-start) | copy-done | bytes 604184
  1.7 0.0 copy-start.5
  1.7 0.7 %copy-done.5 = s32[1,5120]{1,0:T(1,128)S(1)} copy-done((s32[1,5120]{1,0:T(1,128)S(1)}, s32[1,5120]{1,0:T(1,128)}, u32[]{:S(2)}) %copy-start.5) | copy-done | bytes 20504
  2.5 0.0 copy-start.1
  2.5 0.0 copy-start.2
  2.5 0.0 copy-start.3
  2.5 0.0 copy-start.4
  2.5 0.0 copy-start.6
  2.5 0.0 copy-start.7
  2.5 0.0 copy-start.8
  2.5 0.0 copy-start.9
  2.5 0.0 copy-start.10
  2.5 0.0 copy-start.11
  2.5 0.0 copy-start.12
  2.6 0.0 copy-start.13
  2.6 1.3 %shard_map.213 = bf16[2,16,2560]{2,1,0:T(8,128)(2,1)S(1)} custom-call(s32[1]{0:T(128)} %bitcast.view_ref, bf16[1,59,5120]{2,1,0:T(8,128)(2,1)S(1)} %copy-done, s32[1,5120]{1,0:T(1,128)S(1)} %copy-done.5), custom_call_target="tpu_custom_call" | custom-call | tf_op jit(solution)/shard_map/pallas_call | solution.py:90
  3.9 0.5 %collective-permute-start = (bf16[16,2560]{1,0:T(8,128)(2,1)S(1)}, bf16[16,2560]{1,0:T(8,128)(2,1)S(1)}, u32[]{:S(2)}, u32[]{:S(2)}) collective-permute-start(bf16[16,2560]{1,0:T(8,128)(2,1)S(1)} %get-tuple-element.35), channel_id=1, source_target_pairs={{0,16},{16,0},{1,17},{17,1},{2,18},{18,2},{3,19},{19,3},{4,20},{20... | collective-permute-start | bytes 245768 | tf_op jit(solution)/shard_map/ppermute | solution.py:375
  4.5 3.2 %shard_map.214 = bf16[2,48,2560]{2,1,0:T(8,128)(2,1)S(1)} custom-call(s32[1]{0:T(128)} %bitcast.view_ref, bf16[1,59,5120]{2,1,0:T(8,128)(2,1)S(1)} %copy-done, s32[1,5120]{1,0:T(1,128)S(1)} %copy-done.5), custom_call_target="tpu_custom_call" | custom-call | tf_op jit(solution)/shard_map/pallas_call | solution.py:90
  7.6 0.0 collective-permute-done
  7.7 0.0 copy-done.1
  7.7 0.0 copy-done.2
  7.7 0.0 copy-done.3
  7.7 0.0 copy-done.4
  7.7 0.0 copy-done.6
  7.7 0.0 copy-done.7
  7.7 0.0 copy-done.8
  7.7 0.0 copy-done.9
  7.7 0.0 copy-done.10
  7.8 0.0 copy-done.11
  7.8 0.0 copy-done.12
  7.8 0.0 copy-done.13
  7.8 12.5 %shard_map.215 = (bf16[256,2560]{1,0:T(8,128)(2,1)}, f32[4,1,2560]{2,1,0:T(1,128)}, bf16[400,256]{1,0:T(8,128)(2,1)S(1)}, bf16[400,256]{1,0:T(8,128)(2,1)S(1)}) custom-call(s32[1]{0:T(128)S(6)} %select_n.7.side_ref, bf16[2,16,2560]{2,1,0:T(8,128)(2,1)S(1)} %pad_maximum_fusion.2.pos_ref, bf16[256,2560]{1,0:T(8,128)(2,1)S(1)} %bitcast.12, ...), custom_call_target="tpu_custom_call" | custom-call | tf_op jit(solution)/shard_map/pallas_call | solution.py:269
  20.3 0.1 collective-permute-start.2
  20.4 0.5 %collective-permute-start.1 = (bf16[48,2560]{1,0:T(8,128)(2,1)S(1)}, bf16[48,2560]{1,0:T(8,128)(2,1)S(1)}, u32[]{:S(2)}, u32[]{:S(2)}) collective-permute-start(bf16[48,2560]{1,0:T(8,128)(2,1)S(1)} %get-tuple-element.33), channel_id=1, source_target_pairs={{0,16},{16,0},{1,17},{17,1},{2,18},{18,2},{3,19},{19,3},{4,20},{20... | collective-permute-start | bytes 737288 | tf_op jit(solution)/shard_map/ppermute | solution.py:375
  21.0 0.8 %collective-permute-done.2 = bf16[400,256]{1,0:T(8,128)(2,1)S(1)} collective-permute-done((bf16[400,256]{1,0:T(8,128)(2,1)S(1)}, bf16[400,256]{1,0:T(8,128)(2,1)S(1)}, u32[]{:S(2)}, u32[]{:S(2)}) %collective-permute-start.2) | collective-permute-done | bytes 204832 | tf_op jit(solution)/shard_map/ppermute | solution.py:346
  21.8 0.1 add_convert_fusion
  21.9 2.7 %collective-permute-start.3 = (bf16[192,256]{1,0:T(8,128)(2,1)S(1)}, bf16[192,256]{1,0:T(8,128)(2,1)S(1)}, u32[]{:S(2)}, u32[]{:S(2)}) collective-permute-start(bf16[192,256]{1,0:T(8,128)(2,1)S(1)} %slice.33), channel_id=1, source_target_pairs={{0,1},{1,0},{2,3},{3,2},{4,5},{5,4},{6,7},{7,6},{8,9},{9,8},{10,11... | collective-permute-start | bytes 294920 | tf_op jit(solution)/shard_map/ppermute | solution.py:346
  24.6 0.0 collective-permute-done.1
  24.6 0.1 convert_reduce_fusion
  24.7 1.6 %collective-permute-start.7 = (bf16[208,256]{1,0:T(8,128)(2,1)S(1)}, bf16[208,256]{1,0:T(8,128)(2,1)S(1)}, u32[]{:S(2)}, u32[]{:S(2)}) collective-permute-start(bf16[208,256]{1,0:T(8,128)(2,1)S(1)} %slice.34), channel_id=1, source_target_pairs={{0,4},{1,5},{2,6},{3,7},{4,0},{5,1},{6,2},{7,3},{8,12},{9,13},{10,... | collective-permute-start | bytes 319496 | tf_op jit(solution)/shard_map/ppermute | solution.py:346
  26.3 1.6 %collective-permute-done.3 = bf16[192,256]{1,0:T(8,128)(2,1)S(1)} collective-permute-done((bf16[192,256]{1,0:T(8,128)(2,1)S(1)}, bf16[192,256]{1,0:T(8,128)(2,1)S(1)}, u32[]{:S(2)}, u32[]{:S(2)}) %collective-permute-start.3) | collective-permute-done | bytes 98336 | tf_op jit(solution)/shard_map/ppermute | solution.py:346
  27.9 1.8 %collective-permute-start.4 = (bf16[192,256]{1,0:T(8,128)(2,1)S(1)}, bf16[192,256]{1,0:T(8,128)(2,1)S(1)}, u32[]{:S(2)}, u32[]{:S(2)}) collective-permute-start(bf16[192,256]{1,0:T(8,128)(2,1)S(1)} %add_convert_fusion.8), channel_id=1, source_target_pairs={{0,2},{1,3},{2,0},{3,1},{4,6},{5,7},{6,4},{7,5},{8,10},{9,11},{10,... | collective-permute-start | bytes 294920 | tf_op jit(solution)/shard_map/ppermute | solution.py:346
  29.8 0.0 collective-permute-done.7
  29.8 2.7 %collective-permute-start.8 = (bf16[208,256]{1,0:T(8,128)(2,1)S(1)}, bf16[208,256]{1,0:T(8,128)(2,1)S(1)}, u32[]{:S(2)}, u32[]{:S(2)}) collective-permute-start(bf16[208,256]{1,0:T(8,128)(2,1)S(1)} %add_convert_fusion.4), channel_id=1, source_target_pairs={{0,8},{1,9},{2,10},{3,11},{4,12},{5,13},{6,14},{7,15},{8,0},{9,1},... | collective-permute-start | bytes 319496 | tf_op jit(solution)/shard_map/ppermute | solution.py:346
  32.5 0.1 collective-permute-done.4
  32.7 1.9 %collective-permute-start.5 = (bf16[192,256]{1,0:T(8,128)(2,1)S(1)}, bf16[192,256]{1,0:T(8,128)(2,1)S(1)}, u32[]{:S(2)}, u32[]{:S(2)}) collective-permute-start(bf16[192,256]{1,0:T(8,128)(2,1)S(1)} %add_convert_fusion.7), channel_id=1, source_target_pairs={{0,4},{1,5},{2,6},{3,7},{4,0},{5,1},{6,2},{7,3},{8,12},{9,13},{10,... | collective-permute-start | bytes 294920 | tf_op jit(solution)/shard_map/ppermute | solution.py:346
  34.6 2.7 %collective-permute-done.8 = bf16[208,256]{1,0:T(8,128)(2,1)S(1)} collective-permute-done((bf16[208,256]{1,0:T(8,128)(2,1)S(1)}, bf16[208,256]{1,0:T(8,128)(2,1)S(1)}, u32[]{:S(2)}, u32[]{:S(2)}) %collective-permute-start.8) | collective-permute-done | bytes 106528 | tf_op jit(solution)/shard_map/ppermute | solution.py:346
  37.3 1.6 %collective-permute-start.9 = (bf16[208,256]{1,0:T(8,128)(2,1)S(1)}, bf16[208,256]{1,0:T(8,128)(2,1)S(1)}, u32[]{:S(2)}, u32[]{:S(2)}) collective-permute-start(bf16[208,256]{1,0:T(8,128)(2,1)S(1)} %add_convert_fusion.3), channel_id=1, source_target_pairs={{0,1},{1,0},{2,3},{3,2},{4,5},{5,4},{6,7},{7,6},{8,9},{9,8},{10,11... | collective-permute-start | bytes 319496 | tf_op jit(solution)/shard_map/ppermute | solution.py:346
  38.9 0.0 collective-permute-done.5
  38.9 1.7 %collective-permute-start.6 = (bf16[192,256]{1,0:T(8,128)(2,1)S(1)}, bf16[192,256]{1,0:T(8,128)(2,1)S(1)}, u32[]{:S(2)}, u32[]{:S(2)}) collective-permute-start(bf16[192,256]{1,0:T(8,128)(2,1)S(1)} %add_convert_fusion.6), channel_id=1, source_target_pairs={{0,8},{1,9},{2,10},{3,11},{4,12},{5,13},{6,14},{7,15},{8,0},{9,1},... | collective-permute-start | bytes 294920 | tf_op jit(solution)/shard_map/ppermute | solution.py:346
  40.6 1.5 %collective-permute-done.9 = bf16[208,256]{1,0:T(8,128)(2,1)S(1)} collective-permute-done((bf16[208,256]{1,0:T(8,128)(2,1)S(1)}, bf16[208,256]{1,0:T(8,128)(2,1)S(1)}, u32[]{:S(2)}, u32[]{:S(2)}) %collective-permute-start.9) | collective-permute-done | bytes 106528 | tf_op jit(solution)/shard_map/ppermute | solution.py:346
  42.1 1.5 %collective-permute-start.10 = (bf16[208,256]{1,0:T(8,128)(2,1)S(1)}, bf16[208,256]{1,0:T(8,128)(2,1)S(1)}, u32[]{:S(2)}, u32[]{:S(2)}) collective-permute-start(bf16[208,256]{1,0:T(8,128)(2,1)S(1)} %add_convert_fusion.2), channel_id=1, source_target_pairs={{0,2},{1,3},{2,0},{3,1},{4,6},{5,7},{6,4},{7,5},{8,10},{9,11},{10,... | collective-permute-start | bytes 319496 | tf_op jit(solution)/shard_map/ppermute | solution.py:346
  43.7 1.9 %collective-permute-done.6 = bf16[192,256]{1,0:T(8,128)(2,1)S(1)} collective-permute-done((bf16[192,256]{1,0:T(8,128)(2,1)S(1)}, bf16[192,256]{1,0:T(8,128)(2,1)S(1)}, u32[]{:S(2)}, u32[]{:S(2)}) %collective-permute-start.6) | collective-permute-done | bytes 98336 | tf_op jit(solution)/shard_map/ppermute | solution.py:346
  45.6 1.3 %collective-permute-done.10 = bf16[208,256]{1,0:T(8,128)(2,1)S(1)} collective-permute-done((bf16[208,256]{1,0:T(8,128)(2,1)S(1)}, bf16[208,256]{1,0:T(8,128)(2,1)S(1)}, u32[]{:S(2)}, u32[]{:S(2)}) %collective-permute-start.10) | collective-permute-done | bytes 106528 | tf_op jit(solution)/shard_map/ppermute | solution.py:346
  47.0 0.1 collective-permute-start.11
  47.1 1.2 %broadcast_in_dim.6 = f32[59,1,2560]{2,1,0:T(1,128)} reshape(f32[59,2560]{1,0:T(8,128)S(1)} %pad_maximum_fusion) | data formatting | bytes 1208320 | tf_op jit(solution)/shard_map/broadcast_in_dim | solution.py:431
  48.3 0.2 collective-permute-done.11.theirs_ref
  48.5 0.9 %shard_map.216 = (f32[256,256]{1,0:T(8,128)}, f32[256,256]{1,0:T(8,128)}, f32[256,256]{1,0:T(8,128)}, f32[3,256]{1,0:T(4,128)}, f32[3,256]{1,0:T(4,128)}, /*index=5*/f32[8,256]{1,0:T(8,128)}, f32[12,192]{1,0:T(8,128)}) custom-call(s32[1]{0:T(128)S(6)} %select_n.7.side_ref, bf16[400,256]{1,0:T(8,128)(2,1)S(1)} %pad_maximum_fusion.1.mine_ref, ...), custom_call_target="tpu_custom_call" | custom-call | tf_op jit(solution)/shard_map/pallas_call | solution.py:324
  (16 shorter events, 0.4 us)
Async XLA Ops:
  0.7 1.1 %copy-start = (bf16[1,59,5120]{2,1,0:T(8,128)(2,1)S(1)}, bf16[1,59,5120]{2,1,0:T(8,128)(2,1)}, u32[]{:S(2)}) copy-start(bf16[1,59,5120]{2,1,0:T(8,128)(2,1)} %grads_ref.3) | copy-start | bytes 1812484
  1.7 0.7 %copy-start.5 = (s32[1,5120]{1,0:T(1,128)S(1)}, s32[1,5120]{1,0:T(1,128)}, u32[]{:S(2)}) copy-start(s32[1,5120]{1,0:T(1,128)} %ids_ref.3) | copy-start | bytes 61444
  2.5 5.2 %copy-start.1 = (bf16[256,1,2560]{2,0,1:T(8,128)(2,1)S(1)}, bf16[256,1,2560]{2,0,1:T(8,128)(2,1)}, u32[]{:S(2)}) copy-start(bf16[256,1,2560]{2,0,1:T(8,128)(2,1)} %param.16) | copy-start | bytes 3932164
  2.5 5.2 %copy-start.2 = (bf16[256,256]{1,0:T(8,128)(2,1)S(1)}, bf16[256,256]{1,0:T(8,128)(2,1)}, u32[]{:S(2)}) copy-start(bf16[256,256]{1,0:T(8,128)(2,1)} %first_ref.1) | copy-start | bytes 393220
  2.5 5.2 %copy-start.3 = (bf16[256,256]{1,0:T(8,128)(2,1)S(1)}, bf16[256,256]{1,0:T(8,128)(2,1)}, u32[]{:S(2)}) copy-start(bf16[256,256]{1,0:T(8,128)(2,1)} %second_ref.1) | copy-start | bytes 393220
  2.5 5.2 %copy-start.4 = (bf16[256,256]{1,0:T(8,128)(2,1)S(1)}, bf16[256,256]{1,0:T(8,128)(2,1)}, u32[]{:S(2)}) copy-start(bf16[256,256]{1,0:T(8,128)(2,1)} %third_ref.1) | copy-start | bytes 393220
  2.5 5.2 %copy-start.6 = (s32[4,1,2560]{2,1,0:T(1,128)S(1)}, s32[4,1,2560]{2,1,0:T(1,128)}, u32[]{:S(2)}) copy-start(s32[4,1,2560]{2,1,0:T(1,128)} %bone_ids_ref.1) | copy-start | bytes 122884
  2.5 5.2 %copy-start.7 = (f32[4,1,2560]{2,1,0:T(1,128)S(1)}, f32[4,1,2560]{2,1,0:T(1,128)}, u32[]{:S(2)}) copy-start(f32[4,1,2560]{2,1,0:T(1,128)} %skin_ref.1) | copy-start | bytes 122884
  2.5 5.2 %copy-start.8 = (f32[3,1,2560]{2,1,0:T(1,128)S(1)}, f32[3,1,2560]{2,1,0:T(1,128)}, u32[]{:S(2)}) copy-start(f32[3,1,2560]{2,1,0:T(1,128)} %canon_ref.1) | copy-start | bytes 92164
  2.5 5.2 %copy-start.9 = (f32[12,192]{1,0:T(8,128)S(1)}, f32[12,192]{1,0:T(8,128)}, u32[]{:S(2)}) copy-start(f32[12,192]{1,0:T(8,128)} %table_ref.1) | copy-start | bytes 27652
  2.5 5.2 %copy-start.10 = (s32[1,2560]{1,0:T(1,128)S(1)}, s32[1,2560]{1,0:T(1,128)}, u32[]{:S(2)}) copy-start(s32[1,2560]{1,0:T(1,128)} %subj_ref.1) | copy-start | bytes 30724
  2.5 5.2 %copy-start.11 = (f32[256,8]{0,1:T(8,128)S(1)}, f32[256,8]{0,1:T(8,128)}, u32[]{:S(2)}) copy-start(f32[256,8]{0,1:T(8,128)} %param.17) | copy-start | bytes 24580
  2.5 5.2 %copy-start.12 = (f32[3,256]{1,0:T(4,128)S(1)}, f32[3,256]{1,0:T(4,128)}, u32[]{:S(2)}) copy-start(f32[3,256]{1,0:T(4,128)} %bias_ref.1) | copy-start | bytes 9220
  2.6 5.2 %copy-start.13 = (bf16[3,256]{1,0:T(4,128)(2,1)S(1)}, bf16[3,256]{1,0:T(4,128)(2,1)}, u32[]{:S(2)}) copy-start(bf16[3,256]{1,0:T(4,128)(2,1)} %head_ref.1) | copy-start | bytes 4612
  3.9 3.7 %collective-permute-start = (bf16[16,2560]{1,0:T(8,128)(2,1)S(1)}, bf16[16,2560]{1,0:T(8,128)(2,1)S(1)}, u32[]{:S(2)}, u32[]{:S(2)}) collective-permute-start(bf16[16,2560]{1,0:T(8,128)(2,1)S(1)} %get-tuple-element.35), channel_id=1, source_target_pairs={{0,16},{16,0},{1,17},{17,1},{2,18},{18,2},{3,19},{19,3},{4,20},{20... | collective-permute-start | bytes 245768 | tf_op jit(solution)/shard_map/ppermute | solution.py:375
  20.3 1.5 %collective-permute-start.2 = (bf16[400,256]{1,0:T(8,128)(2,1)S(1)}, bf16[400,256]{1,0:T(8,128)(2,1)S(1)}, u32[]{:S(2)}, u32[]{:S(2)}) collective-permute-start(bf16[400,256]{1,0:T(8,128)(2,1)S(1)} %get-tuple-element.24), channel_id=1, source_target_pairs={{0,16},{1,17},{2,18},{3,19},{4,20},{5,21},{6,22},{7,23},{8,24},{9,... | collective-permute-start | bytes 614408 | tf_op jit(solution)/shard_map/ppermute | solution.py:346
  20.4 4.2 %collective-permute-start.1 = (bf16[48,2560]{1,0:T(8,128)(2,1)S(1)}, bf16[48,2560]{1,0:T(8,128)(2,1)S(1)}, u32[]{:S(2)}, u32[]{:S(2)}) collective-permute-start(bf16[48,2560]{1,0:T(8,128)(2,1)S(1)} %get-tuple-element.33), channel_id=1, source_target_pairs={{0,16},{16,0},{1,17},{17,1},{2,18},{18,2},{3,19},{19,3},{4,20},{20... | collective-permute-start | bytes 737288 | tf_op jit(solution)/shard_map/ppermute | solution.py:375
  21.9 6.0 %collective-permute-start.3 = (bf16[192,256]{1,0:T(8,128)(2,1)S(1)}, bf16[192,256]{1,0:T(8,128)(2,1)S(1)}, u32[]{:S(2)}, u32[]{:S(2)}) collective-permute-start(bf16[192,256]{1,0:T(8,128)(2,1)S(1)} %slice.33), channel_id=1, source_target_pairs={{0,1},{1,0},{2,3},{3,2},{4,5},{5,4},{6,7},{7,6},{8,9},{9,8},{10,11... | collective-permute-start | bytes 294920 | tf_op jit(solution)/shard_map/ppermute | solution.py:346
  24.7 5.0 %collective-permute-start.7 = (bf16[208,256]{1,0:T(8,128)(2,1)S(1)}, bf16[208,256]{1,0:T(8,128)(2,1)S(1)}, u32[]{:S(2)}, u32[]{:S(2)}) collective-permute-start(bf16[208,256]{1,0:T(8,128)(2,1)S(1)} %slice.34), channel_id=1, source_target_pairs={{0,4},{1,5},{2,6},{3,7},{4,0},{5,1},{6,2},{7,3},{8,12},{9,13},{10,... | collective-permute-start | bytes 319496 | tf_op jit(solution)/shard_map/ppermute | solution.py:346
  27.9 4.7 %collective-permute-start.4 = (bf16[192,256]{1,0:T(8,128)(2,1)S(1)}, bf16[192,256]{1,0:T(8,128)(2,1)S(1)}, u32[]{:S(2)}, u32[]{:S(2)}) collective-permute-start(bf16[192,256]{1,0:T(8,128)(2,1)S(1)} %add_convert_fusion.8), channel_id=1, source_target_pairs={{0,2},{1,3},{2,0},{3,1},{4,6},{5,7},{6,4},{7,5},{8,10},{9,11},{10,... | collective-permute-start | bytes 294920 | tf_op jit(solution)/shard_map/ppermute | solution.py:346
  29.8 7.5 %collective-permute-start.8 = (bf16[208,256]{1,0:T(8,128)(2,1)S(1)}, bf16[208,256]{1,0:T(8,128)(2,1)S(1)}, u32[]{:S(2)}, u32[]{:S(2)}) collective-permute-start(bf16[208,256]{1,0:T(8,128)(2,1)S(1)} %add_convert_fusion.4), channel_id=1, source_target_pairs={{0,8},{1,9},{2,10},{3,11},{4,12},{5,13},{6,14},{7,15},{8,0},{9,1},... | collective-permute-start | bytes 319496 | tf_op jit(solution)/shard_map/ppermute | solution.py:346
  32.7 6.3 %collective-permute-start.5 = (bf16[192,256]{1,0:T(8,128)(2,1)S(1)}, bf16[192,256]{1,0:T(8,128)(2,1)S(1)}, u32[]{:S(2)}, u32[]{:S(2)}) collective-permute-start(bf16[192,256]{1,0:T(8,128)(2,1)S(1)} %add_convert_fusion.7), channel_id=1, source_target_pairs={{0,4},{1,5},{2,6},{3,7},{4,0},{5,1},{6,2},{7,3},{8,12},{9,13},{10,... | collective-permute-start | bytes 294920 | tf_op jit(solution)/shard_map/ppermute | solution.py:346
  37.3 4.8 %collective-permute-start.9 = (bf16[208,256]{1,0:T(8,128)(2,1)S(1)}, bf16[208,256]{1,0:T(8,128)(2,1)S(1)}, u32[]{:S(2)}, u32[]{:S(2)}) collective-permute-start(bf16[208,256]{1,0:T(8,128)(2,1)S(1)} %add_convert_fusion.3), channel_id=1, source_target_pairs={{0,1},{1,0},{2,3},{3,2},{4,5},{5,4},{6,7},{7,6},{8,9},{9,8},{10,11... | collective-permute-start | bytes 319496 | tf_op jit(solution)/shard_map/ppermute | solution.py:346
  38.9 6.6 %collective-permute-start.6 = (bf16[192,256]{1,0:T(8,128)(2,1)S(1)}, bf16[192,256]{1,0:T(8,128)(2,1)S(1)}, u32[]{:S(2)}, u32[]{:S(2)}) collective-permute-start(bf16[192,256]{1,0:T(8,128)(2,1)S(1)} %add_convert_fusion.6), channel_id=1, source_target_pairs={{0,8},{1,9},{2,10},{3,11},{4,12},{5,13},{6,14},{7,15},{8,0},{9,1},... | collective-permute-start | bytes 294920 | tf_op jit(solution)/shard_map/ppermute | solution.py:346
  42.1 4.8 %collective-permute-start.10 = (bf16[208,256]{1,0:T(8,128)(2,1)S(1)}, bf16[208,256]{1,0:T(8,128)(2,1)S(1)}, u32[]{:S(2)}, u32[]{:S(2)}) collective-permute-start(bf16[208,256]{1,0:T(8,128)(2,1)S(1)} %add_convert_fusion.2), channel_id=1, source_target_pairs={{0,2},{1,3},{2,0},{3,1},{4,6},{5,7},{6,4},{7,5},{8,10},{9,11},{10,... | collective-permute-start | bytes 319496 | tf_op jit(solution)/shard_map/ppermute | solution.py:346
  47.0 1.5 %collective-permute-start.11 = (bf16[400,256]{1,0:T(8,128)(2,1)S(1)}, bf16[400,256]{1,0:T(8,128)(2,1)S(1)}, u32[]{:S(2)}, u32[]{:S(2)}) collective-permute-start(bf16[400,256]{1,0:T(8,128)(2,1)S(1)} %pad_maximum_fusion.1.mine_ref), channel_id=1, source_target_pairs={{0,16},{1,17},{2,18},{3,19},{4,20},{5,21},{6,22},{7,23},{8,24},{9,... | collective-permute-start | bytes 614408 | tf_op jit(solution)/shard_map/ppermute | solution.py:346

commit v3 on v2

v3 whole, which is shorter than its diff:
```python
import functools
import math

import jax
import jax.numpy as jnp
from jax import lax
from jax.experimental import pallas as pl
from jax.experimental.pallas import tpu as pltpu
from jax.sharding import PartitionSpec as P

F32 = jnp.float32
BF16 = jnp.bfloat16
AXES = ("view", "gauss")
LOW = 256
GROUP = 16
NT = (((1,), (1,)), ((), ()))
TN = (((0,), (0,)), ((), ()))
HBM = pl.BlockSpec(memory_space=pltpu.HBM)
VMEM = pl.BlockSpec(memory_space=pltpu.VMEM)
SMEM = pl.BlockSpec(memory_space=pltpu.SMEM)


def params(mebibytes):
    return pltpu.CompilerParams(vmem_limit_bytes=mebibytes * 1024 * 1024)


def mm(left, right, dims=(((1,), (0,)), ((), ()))):
    return lax.dot_general(left, right, dims, preferred_element_type=F32)


def divisor(total, choices):
    for choice in choices:
        if total % choice == 0:
            return choice
    return total


def scatter_kernel(first_row, rows, viewers, view_ref, grads_ref, ids_ref, out_ref, acc_ref, left_ref):
    entries = ids_ref.shape[1]
    step = left_ref.shape[1]
    height = out_ref.shape[1]
    blocks = acc_ref.shape[0] // height
    groups = height // GROUP
    low_rows = lax.broadcasted_iota(jnp.int32, (LOW, step), 0).astype(F32).astype(BF16)
    one = jnp.ones((), BF16)
    zero = jnp.zeros((), BF16)

    def chunk(index, carry):
        spot = pl.ds(pl.multiple_of(index * step, step), step)
        ids = ids_ref[0:1, spot]
        high = lax.shift_right_logical(ids, 8).astype(F32).astype(BF16)
        low = lax.bitwise_and(ids, LOW - 1).astype(F32).astype(BF16)
        hot = jnp.where(low_rows == low, one, zero)
        high = jnp.broadcast_to(high, (GROUP, step))
        for group in range(groups):
            begin = first_row + group * GROUP
            count = min(GROUP, first_row + rows - begin)
            piece = grads_ref[0, begin : begin + count, spot]
            if count < GROUP:
                piece = jnp.concatenate(
                    [piece.astype(F32), jnp.zeros((GROUP - count, step), F32)], axis=0
                ).astype(BF16)
            for block in range(blocks):
                place = block * height + group * GROUP
                left_ref[place : place + GROUP, :] = jnp.where(high == jnp.asarray(block, BF16), piece, zero)
        product = mm(left_ref[...], hot, NT)

        @pl.when(index == 0)
        def _():
            acc_ref[...] = product

        @pl.when(index != 0)
        def _():
            acc_ref[...] += product

        return carry

    lax.fori_loop(0, entries // step, chunk, 0)
    per = blocks // viewers
    for block in range(blocks):
        slot = lax.rem(block // per - view_ref[0] + viewers, viewers)
        out_ref[slot, :, (block % per) * LOW : (block % per + 1) * LOW] = acc_ref[
            block * height : (block + 1) * height, :
        ].astype(BF16)


def scatter(view, entry_grads, vis_ids, first_row, rows, members, viewers):
    height = -(-rows // GROUP) * GROUP
    blocks = members * viewers // LOW
    step = divisor(vis_ids.shape[1], (2560, 2048, 1024, 512, 256, 128))
    return pl.pallas_call(
        functools.partial(scatter_kernel, first_row, rows, viewers),
        out_shape=jax.ShapeDtypeStruct((viewers, height, members), BF16),
        in_specs=[SMEM, VMEM, VMEM],
        out_specs=VMEM,
        scratch_shapes=[pltpu.VMEM((blocks * height, LOW), F32), pltpu.VMEM((blocks * height, step), BF16)],
        compiler_params=params(16),
    )(view, entry_grads, vis_ids)


def entry_kernel(viewers, count, view_ref, *refs):
    sources, out_ref, targets = refs[:count], refs[count], refs[count + 1 : 2 * count + 1]
    acc_ref, left_ref, rows_ref, sems = refs[2 * count + 1 :]
    copies = [
        pltpu.make_async_copy(source, target, sems.at[index])
        for index, (source, target) in enumerate(zip(sources, targets))
    ]
    early = pltpu.make_async_copy(sources[1].at[:, 0:GROUP, :], rows_ref, sems.at[count])
    copies[0].start()
    early.start()
    for copy in copies[1:]:
        copy.start()
    copies[0].wait()
    early.wait()
    scatter_kernel(0, GROUP, viewers, view_ref, rows_ref, targets[0], out_ref, acc_ref, left_ref)
    for copy in copies[1:]:
        copy.wait()


def entry(view, arrays, members, viewers):
    blocks = members * viewers // LOW
    step = divisor(arrays[0].shape[1], (2560, 2048, 1024, 512, 256, 128))
    count = len(arrays)
    results = pl.pallas_call(
        functools.partial(entry_kernel, viewers, count),
        out_shape=(
            jax.ShapeDtypeStruct((viewers, GROUP, members), BF16),
            *(jax.ShapeDtypeStruct(value.shape, value.dtype) for value in arrays),
        ),
        in_specs=[SMEM] + [HBM] * count,
        out_specs=(VMEM,) * (count + 1),
        scratch_shapes=[
            pltpu.VMEM((blocks * GROUP, LOW), F32),
            pltpu.VMEM((blocks * GROUP, step), BF16),
            pltpu.VMEM((1, GROUP, arrays[0].shape[1]), BF16),
            pltpu.SemaphoreType.DMA((count + 1,)),
        ],
        compiler_params=params(16),
    )(view, *(pltpu.with_memory_space_constraint(value, pltpu.HBM) for value in arrays))
    return results[0], results[1:]


def two_parts(value):
    top = value.astype(BF16)
    return top, value - top.astype(F32)


def forward_kernel(
    feats_ref,
    code_ref,
    subj_ref,
    bone_ids_ref,
    skin_ref,
    canon_ref,
    table_ref,
    first_ref,
    second_ref,
    third_ref,
    bias_ref,
    head_ref,
    inputs_out,
    act_one_out,
    act_two_out,
    act_three_out,
    slope_one_out,
    slope_two_out,
    slope_three_out,
    point_out,
    matrix_out,
    blend_out,
    bone_out,
    head_s,
    bias_s,
    table_s,
):
    width, members = feats_ref.shape
    subjects = code_ref.shape[0]
    table_cols = table_ref.shape[1]
    per_subject = table_cols // subjects
    influence = bone_ids_ref.shape[0]
    padded = bone_out.shape[0] // 2
    pieces = table_s.shape[1] // 128

    head_s[...] = jnp.zeros_like(head_s)
    head_s[0:3, :] = head_ref[...].astype(F32)
    head_w = head_s[...].astype(BF16)
    bias_s[...] = jnp.zeros_like(bias_s)
    bias_s[0:3, :] = bias_ref[...]
    bias_cols = bias_s[...].T
    table_s[...] = jnp.zeros_like(table_s)
    table_s[0:12, 0:table_cols] = table_ref[...]
    code = code_ref[...]
    code_hi, code_rest = two_parts(code)
    code_mid, code_lo = two_parts(code_rest)
    code_w = jnp.concatenate([code_hi.astype(F32), code_mid.astype(F32), code_lo], axis=0).T.astype(BF16)

    subject = subj_ref[0:1, :]
    hot_rows = lax.broadcasted_iota(jnp.int32, (3 * subjects, members), 0) % subjects
    hot = (hot_rows == subject).astype(F32).astype(BF16)
    x = (feats_ref[...].astype(F32) + mm(code_w, hot)).astype(BF16)
    inputs_out[0:width, :] = x
    inputs_out[width : width + 16, :] = hot[0:16]
    act = x
    layers = (
        (first_ref, act_one_out, slope_one_out),
        (second_ref, act_two_out, slope_two_out),
        (third_ref, act_three_out, slope_three_out),
    )
    for layer, (weight, act_out, slope_out) in enumerate(layers):
        pre = mm(weight[...], act) + bias_cols[:, layer : layer + 1]
        sig = 0.5 * jnp.tanh(0.5 * pre) + 0.5
        value = pre * sig
        slope_out[...] = sig + value * (1.0 - sig)
        act = value.astype(BF16)
        act_out[...] = act
    moved = mm(head_w, act)
    for axis in range(3):
        point_out[axis : axis + 1, :] = canon_ref[axis] + moved[axis : axis + 1]
    point_out[3:4, :] = jnp.ones((1, members), F32)

    bone_rows = lax.broadcasted_iota(jnp.int32, (padded, members), 0)
    spread = jnp.zeros((padded, members), F32)
    for member in range(influence):
        chosen = bone_ids_ref[member]
        spread = spread + jnp.where(bone_rows == chosen, skin_ref[member], 0.0)
    spread_hi, spread_lo = two_parts(spread)
    bone_out[0:padded, :] = spread_hi
    bone_out[padded : 2 * padded, :] = spread_lo.astype(BF16)

    for tile in range(members // 128):
        lanes = slice(tile * 128, (tile + 1) * 128)
        base = subj_ref[0:1, lanes] * per_subject
        blend = [jnp.zeros((8, 128), F32), jnp.zeros((8, 128), F32)]
        for member in range(influence):
            column = jnp.broadcast_to(base + bone_ids_ref[member, :, lanes], (8, 128))
            within = lax.bitwise_and(column, 127)
            weight = skin_ref[member, :, lanes]
            for part in range(2):
                rows = slice(part * 8, part * 8 + 8)
                matrix = jnp.take_along_axis(table_s[rows, 0:128], within, axis=1, mode="promise_in_bounds")
                for piece in range(1, pieces):
                    other = jnp.take_along_axis(
                        table_s[rows, piece * 128 : (piece + 1) * 128], within, axis=1, mode="promise_in_bounds"
                    )
                    matrix = jnp.where(column >= piece * 128, other, matrix)
                matrix_out[member, rows, lanes] = matrix
                blend[part] = blend[part] + weight * matrix
        blend_out[0:8, lanes] = blend[0]
        blend_out[8:16, lanes] = blend[1]


def forward(feats, code, subj, bone_ids, skin, canon, table, w1, w2, w3, bias, head):
    width, members = feats.shape
    influence = bone_ids.shape[0]
    subjects = code.shape[0]
    table_cols = table.shape[1]
    padded = -(-(table_cols // subjects) // 16) * 16
    act = jax.ShapeDtypeStruct((width, members), BF16)
    slope = jax.ShapeDtypeStruct((width, members), F32)
    return pl.pallas_call(
        forward_kernel,
        out_shape=(
            jax.ShapeDtypeStruct((width + 16, members), BF16),
            act,
            act,
            act,
            slope,
            slope,
            slope,
            jax.ShapeDtypeStruct((4, members), F32),
            jax.ShapeDtypeStruct((influence, 16, members), F32),
            jax.ShapeDtypeStruct((16, members), F32),
            jax.ShapeDtypeStruct((2 * padded, members), BF16),
        ),
        in_specs=[VMEM] * 12,
        out_specs=(VMEM,) * 11,
        scratch_shapes=[
            pltpu.VMEM((16, width), F32),
            pltpu.VMEM((8, width), F32),
            pltpu.VMEM((16, -(-table_cols // 128) * 128), F32),
        ],
        compiler_params=params(16),
    )(feats, code, subj, bone_ids, skin, canon, table, w1, w2, w3, bias, head)


def split_halves(side, total_s, mine_out, theirs_out, factor):
    half = mine_out.shape[0]
    mine_out[...] = (total_s[pl.ds(pl.multiple_of(side * half, 16), half), :] * factor).astype(BF16)
    theirs_out[...] = (total_s[pl.ds(pl.multiple_of((1 - side) * half, 16), half), :] * factor).astype(BF16)


def lane_sums(value):
    total = value[:, 0:128]
    for lane in range(128, value.shape[1], 128):
        total = total + value[:, lane : lane + 128]
    return jnp.sum(total.T, axis=0, keepdims=True)


def upper_kernel(factor, subjects, per_subject, got, *refs):
    (side_ref, pos_ref), refs = refs[:2], refs[2:]
    got_refs, refs = refs[:got], refs[got:]
    (
        point_ref,
        blend_ref,
        bone_ref,
        subj_ref,
        act_one_ref,
        act_two_ref,
        act_three_ref,
        slope_two_ref,
        slope_three_ref,
        third_ref,
        head_ref,
        outer_out,
        back_out,
        rest_out,
        mine_out,
        theirs_out,
        total_s,
        head_s,
        masked_s,
    ) = refs
    width, members = act_one_ref.shape
    lead = width // 2
    padded = bone_ref.shape[0] // 2
    half = mine_out.shape[0]

    head_s[...] = jnp.zeros_like(head_s)
    head_s[0:3, :] = head_ref[...].astype(F32)
    head_w = head_s[...].astype(BF16)
    grad = pos_ref[0].astype(F32)
    for ref in got_refs:
        grad = grad + ref[...].astype(F32)
    rows = lax.broadcasted_iota(jnp.int32, (16, members), 0)
    quarter = rows // 4
    place = rows % 4
    grad_rows = jnp.where(
        quarter == 0,
        grad[0:1],
        jnp.where(quarter == 1, grad[1:2], jnp.where(quarter == 2, grad[2:3], 0.0)),
    )
    point = point_ref[...]
    point_rows = jnp.where(
        place == 0, point[0:1], jnp.where(place == 1, point[1:2], jnp.where(place == 2, point[2:3], point[3:4]))
    )
    outer = grad_rows * point_rows
    outer_out[...] = outer
    pulled = blend_ref[...] * grad_rows
    shift = pulled[0:4] + pulled[4:8] + pulled[8:12]
    shift = jnp.where(rows[0:4] < 3, shift, 0.0)
    shift = jnp.concatenate([shift, jnp.zeros((12, members), F32)], axis=0).astype(BF16)
    back = mm(head_w, shift, TN) * slope_three_ref[...]
    bias_three = lane_sums(back)
    back = back.astype(BF16)
    total_s[0:width, :] = mm(back, act_two_ref[...], NT)
    small = half + half - 32
    total_s[small : small + 3, :] = mm(shift, act_three_ref[...], NT)[0:3]
    back = mm(third_ref[...], back, TN) * slope_two_ref[...]
    total_s[small + 3 : small + 4, :] = lane_sums(back)
    total_s[small + 4 : small + 5, :] = bias_three
    total_s[small + 5 : small + 16, :] = jnp.zeros((11, width), F32)
    back = back.astype(BF16)
    back_out[...] = back
    second = mm(back, act_one_ref[...], NT)
    total_s[width : width + lead, :] = second[0:lead]
    rest_out[...] = second[lead:width]

    outer_hi, outer_lo = two_parts(outer)
    outer_lo = outer_lo.astype(BF16)
    subject = jnp.broadcast_to(subj_ref[...].astype(F32).astype(BF16), (16, members))
    zero = jnp.zeros((), BF16)
    for s in range(subjects):
        inside = subject == jnp.asarray(s, BF16)
        masked_s[32 * s : 32 * s + 16, :] = jnp.where(inside, outer_hi, zero)
        masked_s[32 * s + 16 : 32 * s + 32, :] = jnp.where(inside, outer_lo, zero)
    product = mm(masked_s[...], bone_ref[...], NT)
    total_s[small + 16 : small + 32, :] = jnp.zeros((16, width), F32)
    for s in range(subjects):
        both = product[32 * s : 32 * s + 16] + product[32 * s + 16 : 32 * s + 32]
        columns = slice(s * per_subject, (s + 1) * per_subject)
        total_s[small + 16 : small + 32, columns] = both[:, 0:per_subject] + both[:, padded : padded + per_subject]
    split_halves(side_ref[0], total_s, mine_out, theirs_out, factor)


def upper(side, pos, got, forwarded, subj, w3, head, factor, subjects, per_subject):
    _, act_one, act_two, act_three, _, slope_two, slope_three, point, _, blend, bone = forwarded
    width, members = act_one.shape
    half = (width + width // 2 + 32) // 2
    part = jax.ShapeDtypeStruct((half, width), BF16)
    return pl.pallas_call(
        functools.partial(upper_kernel, factor, subjects, per_subject, len(got)),
        out_shape=(
            jax.ShapeDtypeStruct((16, members), F32),
            jax.ShapeDtypeStruct((width, members), BF16),
            jax.ShapeDtypeStruct((width // 2, width), F32),
            part,
            part,
        ),
        in_specs=[SMEM] + [VMEM] * (12 + len(got)),
        out_specs=(VMEM,) * 5,
        scratch_shapes=[
            pltpu.VMEM((2 * half, width), F32),
            pltpu.VMEM((16, width), F32),
            pltpu.VMEM((32 * subjects, members), BF16),
        ],
        compiler_params=params(16),
    )(
        side,
        pos,
        *got,
        point,
        blend,
        bone,
        subj,
        act_one,
        act_two,
        act_three,
        slope_two,
        slope_three,
        w3,
        head,
    )


def lower_kernel(
    factor,
    subjects,
    side_ref,
    back_ref,
    rest_ref,
    inputs_ref,
    slope_ref,
    second_ref,
    first_ref,
    back_out,
    mine_out,
    theirs_out,
    total_s,
):
    width = back_out.shape[0]
    half = mine_out.shape[0]
    lead = width // 2
    back = (mm(second_ref[...], back_ref[...], TN) * slope_ref[...]).astype(BF16)
    back_out[...] = back
    product = mm(inputs_ref[...], back, NT)
    by_subject = product[width : width + subjects]
    by_hi, by_rest = two_parts(by_subject)
    by_mid, by_lo = two_parts(by_rest)
    by_parts = jnp.concatenate([by_hi.astype(F32), by_mid.astype(F32), by_lo], axis=0).astype(BF16)
    code = mm(by_parts, first_ref[...])
    total_s[0:width, :] = product[0:width].T
    total_s[width : width + lead, :] = rest_ref[...]
    small = width + lead
    total_s[small : small + subjects, :] = (
        code[0:subjects] + code[subjects : 2 * subjects] + code[2 * subjects : 3 * subjects]
    )
    total_s[small + subjects : small + 16, :] = jnp.broadcast_to(
        jnp.sum(by_subject, axis=0, keepdims=True), (16 - subjects, width)
    )
    total_s[small + 16 : small + 32, :] = jnp.zeros((16, width), F32)
    split_halves(side_ref[0], total_s, mine_out, theirs_out, factor)


def lower(side, back, rest, inputs, slope, w2, w1, factor, subjects):
    width, members = back.shape
    half = (width + width // 2 + 32) // 2
    part = jax.ShapeDtypeStruct((half, width), BF16)
    return pl.pallas_call(
        functools.partial(lower_kernel, factor, subjects),
        out_shape=(jax.ShapeDtypeStruct((width, members), BF16), part, part),
        in_specs=[SMEM] + [VMEM] * 6,
        out_specs=(VMEM,) * 3,
        scratch_shapes=[pltpu.VMEM((2 * half, width), F32)],
        compiler_params=params(16),
    )(side, back, rest, inputs, slope, w2, w1)


def gaussian_kernel(back_ref, first_ref, outer_ref, matrix_ref, feat_out, skin_out):
    feat_out[...] = mm(first_ref[...], back_ref[...], TN).astype(BF16)
    outer = outer_ref[...]
    for member in range(matrix_ref.shape[0]):
        skin_out[member] = jnp.sum(outer * matrix_ref[member], axis=0, keepdims=True)


def gaussian_grads(back, w1, outer, matrix):
    width, members = back.shape
    influence = matrix.shape[0]
    return pl.pallas_call(
        gaussian_kernel,
        out_shape=(
            jax.ShapeDtypeStruct((width, members), BF16),
            jax.ShapeDtypeStruct((influence, 1, members), F32),
        ),
        in_specs=[VMEM] * 4,
        out_specs=(VMEM,) * 2,
        compiler_params=params(16),
    )(back, w1, outer, matrix)


def finish_kernel(
    side_ref,
    upper_mine,
    upper_theirs,
    lower_mine,
    lower_theirs,
    first_out,
    second_out,
    third_out,
    bias_out,
    head_out,
    code_out,
    bone_out,
):
    width = third_out.shape[0]
    half = upper_mine.shape[0]
    lead = width // 2
    table_cols = bone_out.shape[1]
    subjects = code_out.shape[0]

    def write(up, low):
        def rows(pair, begin, end):
            pieces = []
            if begin < half:
                pieces.append(pair[0][begin : min(end, half), :].astype(F32))
            if end > half:
                pieces.append(pair[1][max(begin, half) - half : end - half, :].astype(F32))
            return pieces

        def store(out, pair, begin, end, place=0):
            for piece in rows(pair, begin, end):
                out[place : place + piece.shape[0], :] = piece
                place += piece.shape[0]

        small = width + lead
        store(third_out, up, 0, width)
        store(second_out, up, width, small)
        store(second_out, low, small - lead, small, lead)
        store(first_out, low, 0, width)
        (values,) = rows(up, small, small + 16)
        head_out[...] = values[0:3]
        bias_out[1:3, :] = values[3:5]
        (values,) = rows(up, small + 16, small + 32)
        bone_out[...] = values[0:12, 0:table_cols]
        (values,) = rows(low, small, small + 16)
        code_out[...] = values[0:subjects]
        bias_out[0:1, :] = values[subjects : subjects + 1]

    @pl.when(side_ref[0] == 0)
    def _():
        write((upper_mine, upper_theirs), (lower_mine, lower_theirs))

    @pl.when(side_ref[0] != 0)
    def _():
        write((upper_theirs, upper_mine), (lower_theirs, lower_mine))


def finish(side, upper_both, lower_both, subjects, table_cols):
    width = upper_both[0].shape[1]
    square = jax.ShapeDtypeStruct((width, width), F32)
    rows = jax.ShapeDtypeStruct((3, width), F32)
    return pl.pallas_call(
        finish_kernel,
        out_shape=(
            square,
            square,
            square,
            rows,
            rows,
            jax.ShapeDtypeStruct((subjects, width), F32),
            jax.ShapeDtypeStruct((12, table_cols), F32),
        ),
        in_specs=[SMEM] + [VMEM] * 4,
        out_specs=(VMEM,) * 7,
        compiler_params=params(16),
    )(side, *upper_both, *lower_both)


def attr_kernel(count, *refs):
    out_ref = refs[-1]
    attrs = out_ref.shape[0]
    row = 0
    for start in (0, count):
        total = refs[start][0].astype(F32)
        for ref in refs[start + 1 : start + count]:
            total = total + ref[...].astype(F32)
        for place in range(min(total.shape[0], attrs - row)):
            out_ref[row + place] = total[place : place + 1]
        row += total.shape[0]


def attr_sum(position, position_got, others, others_got, attrs):
    members = position.shape[2]
    count = 1 + len(position_got)
    return pl.pallas_call(
        functools.partial(attr_kernel, count),
        out_shape=jax.ShapeDtypeStruct((attrs, 1, members), F32),
        in_specs=[VMEM] * (2 * count),
        out_specs=VMEM,
        compiler_params=params(16),
    )(position, *position_got, others, *others_got)


def add(left, right):
    return (left.astype(F32) + right.astype(F32)).astype(BF16)


def swap(value, mask, count):
    return lax.ppermute(value, AXES, [(place, place ^ mask) for place in range(count)])


def tied(values, others):
    held = lax.optimization_barrier((tuple(values), tuple(others)))
    return list(held[0]), list(held[1])


def sum_over_devices(halves, viewers, shards, between):
    count = viewers * shards
    pair = shards
    masks = [1 << bit for bit in range(count.bit_length() - 1) if 1 << bit != pair]
    orders = [[masks[0], *masks[2:], masks[1]], [masks[1], masks[0], *masks[2:]]]
    parts = [add(mine, swap(theirs, pair, count)) for mine, theirs in halves]
    for stage in range(len(masks)):
        got = [swap(part, order[stage], count) for part, order in zip(parts, orders)]
        for work in between.get(stage, ()):
            got[0] = work(parts[0], got[0])
        parts = [add(part, other) for part, other in zip(parts, got)]
    return [(part, swap(part, pair, count)) for part in parts]


class Work:
    def __init__(self, call, *operands):
        self.call = call
        self.operands = operands
        self.results = None

    def __call__(self, after, before):
        operands, _ = tied(self.operands, [after])
        results = self.call(*operands)
        self.results, held = tied(results, [before])
        return held[0]


def received(parts, viewers):
    got = []
    for away in range(1, viewers):
        perm = [(place, (place + away) % viewers) for place in range(viewers)]
        got.append(lax.ppermute(parts[away], "view", perm))
    return got


def body(
    entry_grads,
    vis_ids,
    feats,
    code_tab,
    subj_ids,
    bone_ids,
    skin_w,
    canon_pos,
    bone_tf,
    w_first,
    w_second,
    w_third,
    biases,
    w_head,
):
    members = feats.shape[2]
    viewers = lax.axis_size("view")
    shards = lax.axis_size("gauss")
    attrs = entry_grads.shape[1]
    subjects = code_tab.shape[1]
    table_cols = bone_tf.shape[1]
    factor = 1.0 / math.sqrt(members * viewers * shards)
    view = lax.axis_index("view").astype(jnp.int32).reshape(1)
    side = lax.bitwise_and(view, 1)
    position, arrays = entry(
        view,
        (
            vis_ids,
            entry_grads,
            feats[:, 0],
            code_tab.T,
            subj_ids,
            bone_ids,
            skin_w,
            canon_pos,
            bone_tf,
            w_first,
            w_second,
            w_third,
            biases,
            w_head,
        ),
        members,
        viewers,
    )
    vis_ids, entry_grads, *arrays = arrays
    subj_ids, (w_first, w_second, w_third), w_head = arrays[2], arrays[7:10], arrays[11]
    position_got = received(position, viewers)
    forwarded = forward(*arrays)
    outer, back_two, second_rest, *upper_halves = upper(
        side, position, position_got, forwarded, subj_ids, w_third, w_head, factor, subjects, table_cols // subjects
    )
    back_one, *lower_halves = lower(
        side, back_two, second_rest, forwarded[0], forwarded[4], w_second, w_first, factor, subjects
    )

    def scatter_rows(row):
        def call(grads, ids):
            return [scatter(view, grads, ids, row, min(GROUP, attrs - row), members, viewers)]

        return Work(call, entry_grads, vis_ids)

    works = [scatter_rows(row) for row in range(GROUP, attrs, GROUP)]
    per_gaussian = Work(gaussian_grads, back_one, w_first, outer, forwarded[8])

    def exchange(_):
        others = jnp.concatenate([work.results[0] for work in works], axis=1)
        others_got = received(others, viewers)
        return [attr_sum(position, position_got, others, others_got, attrs)]

    last = Work(exchange, view)
    between = {0: [works[0]], 1: [works[1]], 2: [works[2], per_gaussian], 3: [last]}
    upper_both, lower_both = sum_over_devices([upper_halves, lower_halves], viewers, shards, between)
    attr = last.results[0]
    feat_grads, skin_grads = per_gaussian.results
    first, second, third, bias, head, code, bone = finish(side, upper_both, lower_both, subjects, table_cols)
    return (
        attr,
        feat_grads[:, None, :],
        skin_grads,
        first,
        second,
        third,
        bias,
        head,
        code.T,
        bone,
    )


def solution(mesh):
    placed = (
        P("view", None, "gauss"),
        P("view", "gauss"),
        P(None, "gauss", "view"),
        P(),
        P("gauss", "view"),
        P(None, "gauss", "view"),
        P(None, "gauss", "view"),
        P(None, "gauss", "view"),
        P(),
        P(),
        P(),
        P(),
        P(),
        P(),
    )
    return jax.shard_map(
        body,
        mesh=mesh,
        in_specs=placed,
        out_specs=(
            P(None, "gauss", "view"),
            P(None, "gauss", "view"),
            P(None, "gauss", "view"),
            P(),
            P(),
            P(),
            P(),
            P(),
            P(),
            P(),
        ),
        check_vma=False,
    )
```

time: 49.6 us -> 43.1 us (0.87)
  the two profiles are of different devices: /device:TPU:0 before, /device:TPU:25 now
where the time goes in v3:
time: 43.1 us; the launch traced here: 42.9 us
  Pallas kernels  18 us (42%)
  starting transfers between devices  17.7 us (41%)
  waiting for transfers between devices  6.06 us (14%)
  between operations  0.78 us (2%)
    ppermute x12, starting transfers between devices, swap(): lax.ppermute(value, AXES, [(place, place ^ mask) for place in range(count)])  10.3 us
    ppermute x2, starting transfers between devices, received(): got.append(lax.ppermute(parts[away], 'view', perm))  7.44 us
    ppermute x12, waiting for transfers between devices, swap(): lax.ppermute(value, AXES, [(place, place ^ mask) for place in range(count)])  6.06 us
    pallas_call x1, Pallas kernels, forward(): pl.pallas_call(forward_kernel, out_shape=(jax.ShapeDtypeStruct((width + 1...  4.08 us
    pallas_call x3, Pallas kernels, scatter(): pl.pallas_call(functools.partial(scatter_kernel, first_row, rows, viewers...  4.06 us
    pallas_call x1, Pallas kernels, upper(): pl.pallas_call(functools.partial(upper_kernel, factor, subjects, per_subj...  2.75 us
    pallas_call x1, Pallas kernels, entry(): pl.pallas_call(functools.partial(entry_kernel, viewers, count), out_shape...  2.46 us
    pallas_call x1, Pallas kernels, gaussian_grads(): pl.pallas_call(gaussian_kernel, out_shape=(jax.ShapeDtypeStruct((width, m...  1.6 us
  transfers between devices with their start and end apart: 14, of which 7 were waited for; matrix products, arithmetic and copies ran while one was open for 1% of the time, Pallas kernels for 25%

profile of v3, /device:TPU:25, one launch (start us, length us, event | category | flops | bytes accessed | tf_op | source)
XLA Modules:
  0.0 42.9 jit_solution(4883753121099779189)
XLA Ops:
  0.7 2.5 %shard_map.213 = (bf16[2,16,2560]{2,1,0:T(8,128)(2,1)S(1)}, s32[1,5120]{1,0:T(1,128)S(1)}, bf16[1,59,5120]{2,1,0:T(8,128)(2,1)S(1)}, bf16[256,2560]{1,0:T(8,128)...) custom-call(s32[1]{0:T(128)} %bitcast.view_ref, ...), custom_call_target="tpu_custom_call" | custom-call | tf_op jit(solution)/shard_map/pallas_call | solution.py:124
  3.1 0.7 %collective-permute-start = (bf16[16,2560]{1,0:T(8,128)(2,1)S(1)}, bf16[16,2560]{1,0:T(8,128)(2,1)S(1)}, u32[]{:S(2)}, u32[]{:S(2)}) collective-permute-start(bf16[16,2560]{1,0:T(8,128)(2,1)S(1)} %slice_bitcast_fusion.1), channel_id=1, source_target_pairs={{0,16},{16,0},{1,17},{17,1},{2,18},{18,2},{3,19},{19,3},{4,20},{20... | collective-permute-start | bytes 245768 | tf_op jit(solution)/shard_map/ppermute | solution.py:647
  3.9 4.1 %shard_map.214 = (bf16[272,2560]{1,0:T(8,128)(2,1)S(1)}, bf16[256,2560]{1,0:T(8,128)(2,1)S(1)}, bf16[256,2560]{1,0:T(8,128)(2,1)S(1)}, bf16[256,2560]{1,0:T(8,12...) custom-call(bf16[256,2560]{1,0:T(8,128)(2,1)S(1)} %get-tuple-element, ...), custom_call_target="tpu_custom_call" | custom-call | tf_op jit(solution)/shard_map/pallas_call | solution.py:260
  8.0 0.0 collective-permute-done.refs_2_.refs_1_
  8.0 2.7 %shard_map.215 = (f32[16,2560]{1,0:T(8,128)S(1)}, bf16[256,2560]{1,0:T(8,128)(2,1)S(1)}, f32[128,256]{1,0:T(8,128)S(1)}, bf16[208,256]{1,0:T(8,128)(2,1)S(1)}, bf16[208,256]{1,0:T(8,128)(2,1)S(1)}) custom-call(s32[1]{0:T(128)S(6)} %and.4.refs_0_.side_ref, bf16[2,16,2560]{2,1,0:T(8,128)(2,1)S(1)} %get-tuple-element.74.refs_1_.refs_0_, ...), custom_call_target="tpu_custom_call" | custom-call | tf_op jit(solution)/shard_map/pallas_call | solution.py:390
  10.7 1.1 %shard_map.220 = (bf16[256,2560]{1,0:T(8,128)(2,1)S(1)}, bf16[208,256]{1,0:T(8,128)(2,1)S(1)}, bf16[208,256]{1,0:T(8,128)(2,1)S(1)}) custom-call(s32[1]{0:T(128)S(6)} %and.4.refs_0_.side_ref, bf16[256,2560]{1,0:T(8,128)(2,1)S(1)} %get-tuple-element.110.back_ref, f32[128,256]{1,0:T(8,128)S(1)} %get-tuple-element.111.rest_ref, ...), custom_call_target="tpu_custom_call" | custom-call | tf_op jit(solution)/shard_map/pallas_call | solution.py:468
  11.9 0.1 collective-permute-start.8
  11.9 0.5 %collective-permute-start.1 = (bf16[208,256]{1,0:T(8,128)(2,1)S(1)}, bf16[208,256]{1,0:T(8,128)(2,1)S(1)}, u32[]{:S(2)}, u32[]{:S(2)}) collective-permute-start(bf16[208,256]{1,0:T(8,128)(2,1)S(1)} %get-tuple-element.98), channel_id=1, source_target_pairs={{0,16},{1,17},{2,18},{3,19},{4,20},{5,21},{6,22},{7,23},{8,24},{9,... | collective-permute-start | bytes 319496 | tf_op jit(solution)/shard_map/ppermute | solution.py:608
  12.4 0.8 %collective-permute-done.8 = bf16[208,256]{1,0:T(8,128)(2,1)S(1)} collective-permute-done((bf16[208,256]{1,0:T(8,128)(2,1)S(1)}, bf16[208,256]{1,0:T(8,128)(2,1)S(1)}, u32[]{:S(2)}, u32[]{:S(2)}) %collective-permute-start.8) | collective-permute-done | bytes 106528 | tf_op jit(solution)/shard_map/ppermute | solution.py:608
  13.3 1.3 %collective-permute-start.9 = (bf16[208,256]{1,0:T(8,128)(2,1)S(1)}, bf16[208,256]{1,0:T(8,128)(2,1)S(1)}, u32[]{:S(2)}, u32[]{:S(2)}) collective-permute-start(bf16[208,256]{1,0:T(8,128)(2,1)S(1)} %add_convert_fusion.4), channel_id=1, source_target_pairs={{0,2},{1,3},{2,0},{3,1},{4,6},{5,7},{6,4},{7,5},{8,10},{9,11},{10,... | collective-permute-start | bytes 319496 | tf_op jit(solution)/shard_map/ppermute | solution.py:608
  14.6 0.0 collective-permute-done.1
  14.6 1.3 %collective-permute-start.2 = (bf16[208,256]{1,0:T(8,128)(2,1)S(1)}, bf16[208,256]{1,0:T(8,128)(2,1)S(1)}, u32[]{:S(2)}, u32[]{:S(2)}) collective-permute-start(bf16[208,256]{1,0:T(8,128)(2,1)S(1)} %add_convert_fusion.9), channel_id=1, source_target_pairs={{0,1},{1,0},{2,3},{3,2},{4,5},{5,4},{6,7},{7,6},{8,9},{9,8},{10,11... | collective-permute-start | bytes 319496 | tf_op jit(solution)/shard_map/ppermute | solution.py:608
  15.9 1.4 %shard_map.216 = bf16[2,16,2560]{2,1,0:T(8,128)(2,1)S(1)} custom-call(s32[1]{0:T(128)} %bitcast.view_ref, bf16[1,59,5120]{2,1,0:T(8,128)(2,1)S(1)} %get-tuple-element.107.grads_ref, s32[1,5120]{1,0:T(1,128)S(1)} %get-tuple-element.108.ids_ref), custom_call_target="tpu_custom_call" | custom-call | tf_op jit(solution)/shard_map/pallas_call | solution.py:91
  17.2 0.5 %collective-permute-done.9 = bf16[208,256]{1,0:T(8,128)(2,1)S(1)} collective-permute-done((bf16[208,256]{1,0:T(8,128)(2,1)S(1)}, bf16[208,256]{1,0:T(8,128)(2,1)S(1)}, u32[]{:S(2)}, u32[]{:S(2)}) %collective-permute-start.9) | collective-permute-done | bytes 106528 | tf_op jit(solution)/shard_map/ppermute | solution.py:608
  17.8 1.3 %collective-permute-start.10 = (bf16[208,256]{1,0:T(8,128)(2,1)S(1)}, bf16[208,256]{1,0:T(8,128)(2,1)S(1)}, u32[]{:S(2)}, u32[]{:S(2)}) collective-permute-start(bf16[208,256]{1,0:T(8,128)(2,1)S(1)} %add_convert_fusion.3), channel_id=1, source_target_pairs={{0,1},{1,0},{2,3},{3,2},{4,5},{5,4},{6,7},{7,6},{8,9},{9,8},{10,11... | collective-permute-start | bytes 319496 | tf_op jit(solution)/shard_map/ppermute | solution.py:608
  19.1 0.0 collective-permute-done.2
  19.1 0.2 collective-permute-start.3
  19.3 1.4 %shard_map.217 = bf16[2,16,2560]{2,1,0:T(8,128)(2,1)S(1)} custom-call(s32[1]{0:T(128)} %bitcast.view_ref, bf16[1,59,5120]{2,1,0:T(8,128)(2,1)S(1)} %get-tuple-element.107.grads_ref, s32[1,5120]{1,0:T(1,128)S(1)} %get-tuple-element.108.ids_ref), custom_call_target="tpu_custom_call" | custom-call | tf_op jit(solution)/shard_map/pallas_call | solution.py:91
  20.7 0.7 %collective-permute-done.10 = bf16[208,256]{1,0:T(8,128)(2,1)S(1)} collective-permute-done((bf16[208,256]{1,0:T(8,128)(2,1)S(1)}, bf16[208,256]{1,0:T(8,128)(2,1)S(1)}, u32[]{:S(2)}, u32[]{:S(2)}) %collective-permute-start.10) | collective-permute-done | bytes 106528 | tf_op jit(solution)/shard_map/ppermute | solution.py:608
  21.4 0.7 %collective-permute-start.11 = (bf16[208,256]{1,0:T(8,128)(2,1)S(1)}, bf16[208,256]{1,0:T(8,128)(2,1)S(1)}, u32[]{:S(2)}, u32[]{:S(2)}) collective-permute-start(bf16[208,256]{1,0:T(8,128)(2,1)S(1)} %add_convert_fusion.2), channel_id=1, source_target_pairs={{0,4},{1,5},{2,6},{3,7},{4,0},{5,1},{6,2},{7,3},{8,12},{9,13},{10,... | collective-permute-start | bytes 319496 | tf_op jit(solution)/shard_map/ppermute | solution.py:608
  22.1 0.9 %collective-permute-done.3 = bf16[208,256]{1,0:T(8,128)(2,1)S(1)} collective-permute-done((bf16[208,256]{1,0:T(8,128)(2,1)S(1)}, bf16[208,256]{1,0:T(8,128)(2,1)S(1)}, u32[]{:S(2)}, u32[]{:S(2)}) %collective-permute-start.3) | collective-permute-done | bytes 106528 | tf_op jit(solution)/shard_map/ppermute | solution.py:608
  23.0 0.1 collective-permute-start.4
  23.2 1.4 %shard_map.218 = bf16[2,16,2560]{2,1,0:T(8,128)(2,1)S(1)} custom-call(s32[1]{0:T(128)} %bitcast.view_ref, bf16[1,59,5120]{2,1,0:T(8,128)(2,1)S(1)} %get-tuple-element.107.grads_ref, s32[1,5120]{1,0:T(1,128)S(1)} %get-tuple-element.108.ids_ref), custom_call_target="tpu_custom_call" | custom-call | tf_op jit(solution)/shard_map/pallas_call | solution.py:91
  24.5 1.6 %shard_map.221 = (bf16[256,2560]{1,0:T(8,128)(2,1)}, f32[4,1,2560]{2,1,0:T(1,128)}) custom-call(bf16[256,2560]{1,0:T(8,128)(2,1)S(1)} %get-tuple-element.117.back_ref, bf16[256,256]{1,0:T(8,128)(2,1)S(1)} %get-tuple-element.118.first_ref, f32[16,2560]{1,0:T(8,128)S(1)} %get-tuple-element.119.outer_ref, f32[4,16,2560]{2,1,0:T(8,128)S(1)} %get-tuple-element.120.matrix_ref), custom_call_target="tpu_custom_call" | custom-call | tf_op jit(solution)/shard_map/pallas_call | solution.py:488
  26.1 0.0 collective-permute-done.11
  26.2 2.4 %collective-permute-start.12 = (bf16[208,256]{1,0:T(8,128)(2,1)S(1)}, bf16[208,256]{1,0:T(8,128)(2,1)S(1)}, u32[]{:S(2)}, u32[]{:S(2)}) collective-permute-start(bf16[208,256]{1,0:T(8,128)(2,1)S(1)} %add_convert_fusion.1), channel_id=1, source_target_pairs={{0,8},{1,9},{2,10},{3,11},{4,12},{5,13},{6,14},{7,15},{8,0},{9,1},... | collective-permute-start | bytes 319496 | tf_op jit(solution)/shard_map/ppermute | solution.py:608
  28.5 0.2 collective-permute-done.4
  28.8 6.7 %collective-permute-start.5 = (bf16[48,2560]{1,0:T(8,128)(2,1)S(1)}, bf16[48,2560]{1,0:T(8,128)(2,1)S(1)}, u32[]{:S(2)}, u32[]{:S(2)}) collective-permute-start(bf16[48,2560]{1,0:T(8,128)(2,1)S(1)} %slice_bitcast_fusion), channel_id=1, source_target_pairs={{0,16},{16,0},{1,17},{17,1},{2,18},{18,2},{3,19},{19,3},{4,20},{20... | collective-permute-start | bytes 737288 | tf_op jit(solution)/shard_map/ppermute | solution.py:647
  35.5 1.3 %collective-permute-start.6 = (bf16[208,256]{1,0:T(8,128)(2,1)S(1)}, bf16[208,256]{1,0:T(8,128)(2,1)S(1)}, u32[]{:S(2)}, u32[]{:S(2)}) collective-permute-start(bf16[208,256]{1,0:T(8,128)(2,1)S(1)} %add_convert_fusion.6), channel_id=1, source_target_pairs={{0,2},{1,3},{2,0},{3,1},{4,6},{5,7},{6,4},{7,5},{8,10},{9,11},{10,... | collective-permute-start | bytes 319496 | tf_op jit(solution)/shard_map/ppermute | solution.py:608
  36.8 0.0 collective-permute-done.12
  36.8 0.4 collective-permute-start.13
  37.2 0.0 collective-permute-done.5.refs_3_
  37.2 1.0 %shard_map.219 = f32[59,1,2560]{2,1,0:T(1,128)} custom-call(bf16[2,16,2560]{2,1,0:T(8,128)(2,1)S(1)} %get-tuple-element.74.refs_1_.refs_0_, bf16[16,2560]{1,0:T(8,128)(2,1)S(1)} %collective-permute-done.refs_2_.refs_1_, bf16[2,48,2560]{2,1,0:T(8,128)(2,1)S(1)} %constant_dynamic-update-slice_fusion.refs_2_, bf16[48,2560]{1,0:T(8,128)(2,1)S(1)} %collective-permute-done.5.refs_3_), custom_call_target="tpu_custom_call" | custom-call | tf_op jit(solution)/shard_map/pallas_call | solution.py:594
  38.2 2.0 %collective-permute-done.6 = bf16[208,256]{1,0:T(8,128)(2,1)S(1)} collective-permute-done((bf16[208,256]{1,0:T(8,128)(2,1)S(1)}, bf16[208,256]{1,0:T(8,128)(2,1)S(1)}, u32[]{:S(2)}, u32[]{:S(2)}) %collective-permute-start.6) | collective-permute-done | bytes 106528 | tf_op jit(solution)/shard_map/ppermute | solution.py:608
  40.2 0.9 %collective-permute-start.7 = (bf16[208,256]{1,0:T(8,128)(2,1)S(1)}, bf16[208,256]{1,0:T(8,128)(2,1)S(1)}, u32[]{:S(2)}, u32[]{:S(2)}) collective-permute-start(bf16[208,256]{1,0:T(8,128)(2,1)S(1)} %add_convert_fusion.5.upper_mine), channel_id=1, source_target_pairs={{0,16},{1,17},{2,18},{3,19},{4,20},{5,21},{6,22},{7,23},{8,24},{9,... | collective-permute-start | bytes 319496 | tf_op jit(solution)/shard_map/ppermute | solution.py:608
  41.0 0.0 collective-permute-done.13.lower_theirs
  41.0 1.0 %collective-permute-done.7.upper_theirs = bf16[208,256]{1,0:T(8,128)(2,1)S(1)} collective-permute-done((bf16[208,256]{1,0:T(8,128)(2,1)S(1)}, bf16[208,256]{1,0:T(8,128)(2,1)S(1)}, u32[]{:S(2)}, u32[]{:S(2)}) %collective-permute-start.7) | collective-permute-done | bytes 106528 | tf_op jit(solution)/shard_map/ppermute | solution.py:608
  42.0 0.9 %shard_map.222 = (f32[256,256]{1,0:T(8,128)}, f32[256,256]{1,0:T(8,128)}, f32[256,256]{1,0:T(8,128)}, f32[3,256]{1,0:T(4,128)}, f32[3,256]{1,0:T(4,128)}, /*index=5*/f32[8,256]{1,0:T(8,128)}, f32[12,192]{1,0:T(8,128)}) custom-call(s32[1]{0:T(128)S(6)} %and.4.refs_0_.side_ref, bf16[208,256]{1,0:T(8,128)(2,1)S(1)} %add_convert_fusion.5.upper_mine, ...), custom_call_target="tpu_custom_call" | custom-call | tf_op jit(solution)/shard_map/pallas_call | solution.py:561
  (15 shorter events, 0.3 us)
Async XLA Ops:
  3.1 4.8 %collective-permute-start = (bf16[16,2560]{1,0:T(8,128)(2,1)S(1)}, bf16[16,2560]{1,0:T(8,128)(2,1)S(1)}, u32[]{:S(2)}, u32[]{:S(2)}) collective-permute-start(bf16[16,2560]{1,0:T(8,128)(2,1)S(1)} %slice_bitcast_fusion.1), channel_id=1, source_target_pairs={{0,16},{16,0},{1,17},{17,1},{2,18},{18,2},{3,19},{19,3},{4,20},{20... | collective-permute-start | bytes 245768 | tf_op jit(solution)/shard_map/ppermute | solution.py:647
  11.9 1.4 %collective-permute-start.8 = (bf16[208,256]{1,0:T(8,128)(2,1)S(1)}, bf16[208,256]{1,0:T(8,128)(2,1)S(1)}, u32[]{:S(2)}, u32[]{:S(2)}) collective-permute-start(bf16[208,256]{1,0:T(8,128)(2,1)S(1)} %get-tuple-element.130), channel_id=1, source_target_pairs={{0,16},{1,17},{2,18},{3,19},{4,20},{5,21},{6,22},{7,23},{8,24},{9,... | collective-permute-start | bytes 319496 | tf_op jit(solution)/shard_map/ppermute | solution.py:608
  11.9 2.6 %collective-permute-start.1 = (bf16[208,256]{1,0:T(8,128)(2,1)S(1)}, bf16[208,256]{1,0:T(8,128)(2,1)S(1)}, u32[]{:S(2)}, u32[]{:S(2)}) collective-permute-start(bf16[208,256]{1,0:T(8,128)(2,1)S(1)} %get-tuple-element.98), channel_id=1, source_target_pairs={{0,16},{1,17},{2,18},{3,19},{4,20},{5,21},{6,22},{7,23},{8,24},{9,... | collective-permute-start | bytes 319496 | tf_op jit(solution)/shard_map/ppermute | solution.py:608
  13.3 4.5 %collective-permute-start.9 = (bf16[208,256]{1,0:T(8,128)(2,1)S(1)}, bf16[208,256]{1,0:T(8,128)(2,1)S(1)}, u32[]{:S(2)}, u32[]{:S(2)}) collective-permute-start(bf16[208,256]{1,0:T(8,128)(2,1)S(1)} %add_convert_fusion.4), channel_id=1, source_target_pairs={{0,2},{1,3},{2,0},{3,1},{4,6},{5,7},{6,4},{7,5},{8,10},{9,11},{10,... | collective-permute-start | bytes 319496 | tf_op jit(solution)/shard_map/ppermute | solution.py:608
  14.6 4.5 %collective-permute-start.2 = (bf16[208,256]{1,0:T(8,128)(2,1)S(1)}, bf16[208,256]{1,0:T(8,128)(2,1)S(1)}, u32[]{:S(2)}, u32[]{:S(2)}) collective-permute-start(bf16[208,256]{1,0:T(8,128)(2,1)S(1)} %add_convert_fusion.9), channel_id=1, source_target_pairs={{0,1},{1,0},{2,3},{3,2},{4,5},{5,4},{6,7},{7,6},{8,9},{9,8},{10,11... | collective-permute-start | bytes 319496 | tf_op jit(solution)/shard_map/ppermute | solution.py:608
  17.8 3.6 %collective-permute-start.10 = (bf16[208,256]{1,0:T(8,128)(2,1)S(1)}, bf16[208,256]{1,0:T(8,128)(2,1)S(1)}, u32[]{:S(2)}, u32[]{:S(2)}) collective-permute-start(bf16[208,256]{1,0:T(8,128)(2,1)S(1)} %add_convert_fusion.3), channel_id=1, source_target_pairs={{0,1},{1,0},{2,3},{3,2},{4,5},{5,4},{6,7},{7,6},{8,9},{9,8},{10,11... | collective-permute-start | bytes 319496 | tf_op jit(solution)/shard_map/ppermute | solution.py:608
  19.1 3.9 %collective-permute-start.3 = (bf16[208,256]{1,0:T(8,128)(2,1)S(1)}, bf16[208,256]{1,0:T(8,128)(2,1)S(1)}, u32[]{:S(2)}, u32[]{:S(2)}) collective-permute-start(bf16[208,256]{1,0:T(8,128)(2,1)S(1)} %add_convert_fusion.8), channel_id=1, source_target_pairs={{0,4},{1,5},{2,6},{3,7},{4,0},{5,1},{6,2},{7,3},{8,12},{9,13},{10,... | collective-permute-start | bytes 319496 | tf_op jit(solution)/shard_map/ppermute | solution.py:608
  21.4 4.7 %collective-permute-start.11 = (bf16[208,256]{1,0:T(8,128)(2,1)S(1)}, bf16[208,256]{1,0:T(8,128)(2,1)S(1)}, u32[]{:S(2)}, u32[]{:S(2)}) collective-permute-start(bf16[208,256]{1,0:T(8,128)(2,1)S(1)} %add_convert_fusion.2), channel_id=1, source_target_pairs={{0,4},{1,5},{2,6},{3,7},{4,0},{5,1},{6,2},{7,3},{8,12},{9,13},{10,... | collective-permute-start | bytes 319496 | tf_op jit(solution)/shard_map/ppermute | solution.py:608
  23.0 5.7 %collective-permute-start.4 = (bf16[208,256]{1,0:T(8,128)(2,1)S(1)}, bf16[208,256]{1,0:T(8,128)(2,1)S(1)}, u32[]{:S(2)}, u32[]{:S(2)}) collective-permute-start(bf16[208,256]{1,0:T(8,128)(2,1)S(1)} %add_convert_fusion.7), channel_id=1, source_target_pairs={{0,8},{1,9},{2,10},{3,11},{4,12},{5,13},{6,14},{7,15},{8,0},{9,1},... | collective-permute-start | bytes 319496 | tf_op jit(solution)/shard_map/ppermute | solution.py:608
  26.2 10.6 %collective-permute-start.12 = (bf16[208,256]{1,0:T(8,128)(2,1)S(1)}, bf16[208,256]{1,0:T(8,128)(2,1)S(1)}, u32[]{:S(2)}, u32[]{:S(2)}) collective-permute-start(bf16[208,256]{1,0:T(8,128)(2,1)S(1)} %add_convert_fusion.1), channel_id=1, source_target_pairs={{0,8},{1,9},{2,10},{3,11},{4,12},{5,13},{6,14},{7,15},{8,0},{9,1},... | collective-permute-start | bytes 319496 | tf_op jit(solution)/shard_map/ppermute | solution.py:608
  28.8 8.4 %collective-permute-start.5 = (bf16[48,2560]{1,0:T(8,128)(2,1)S(1)}, bf16[48,2560]{1,0:T(8,128)(2,1)S(1)}, u32[]{:S(2)}, u32[]{:S(2)}) collective-permute-start(bf16[48,2560]{1,0:T(8,128)(2,1)S(1)} %slice_bitcast_fusion), channel_id=1, source_target_pairs={{0,16},{16,0},{1,17},{17,1},{2,18},{18,2},{3,19},{19,3},{4,20},{20... | collective-permute-start | bytes 737288 | tf_op jit(solution)/shard_map/ppermute | solution.py:647
  35.5 4.7 %collective-permute-start.6 = (bf16[208,256]{1,0:T(8,128)(2,1)S(1)}, bf16[208,256]{1,0:T(8,128)(2,1)S(1)}, u32[]{:S(2)}, u32[]{:S(2)}) collective-permute-start(bf16[208,256]{1,0:T(8,128)(2,1)S(1)} %add_convert_fusion.6), channel_id=1, source_target_pairs={{0,2},{1,3},{2,0},{3,1},{4,6},{5,7},{6,4},{7,5},{8,10},{9,11},{10,... | collective-permute-start | bytes 319496 | tf_op jit(solution)/shard_map/ppermute | solution.py:608
  36.8 4.2 %collective-permute-start.13 = (bf16[208,256]{1,0:T(8,128)(2,1)S(1)}, bf16[208,256]{1,0:T(8,128)(2,1)S(1)}, u32[]{:S(2)}, u32[]{:S(2)}) collective-permute-start(bf16[208,256]{1,0:T(8,128)(2,1)S(1)} %add_convert_fusion.lower_mine), channel_id=1, source_target_pairs={{0,16},{1,17},{2,18},{3,19},{4,20},{5,21},{6,22},{7,23},{8,24},{9,... | collective-permute-start | bytes 319496 | tf_op jit(solution)/shard_map/ppermute | solution.py:608
  40.2 1.8 %collective-permute-start.7 = (bf16[208,256]{1,0:T(8,128)(2,1)S(1)}, bf16[208,256]{1,0:T(8,128)(2,1)S(1)}, u32[]{:S(2)}, u32[]{:S(2)}) collective-permute-start(bf16[208,256]{1,0:T(8,128)(2,1)S(1)} %add_convert_fusion.5.upper_mine), channel_id=1, source_target_pairs={{0,16},{1,17},{2,18},{3,19},{4,20},{5,21},{6,22},{7,23},{8,24},{9,... | collective-permute-start | bytes 319496 | tf_op jit(solution)/shard_map/ppermute | solution.py:608

commit v4 on v3

--- a/solution.py
+++ b/solution.py
@@ -13,6 +13,7 @@
 AXES = ("view", "gauss")
 LOW = 256
 GROUP = 16
+FAN = 4
 NT = (((1,), (1,)), ((), ()))
 TN = (((0,), (0,)), ((), ()))
 HBM = pl.BlockSpec(memory_space=pltpu.HBM)
@@ -283,10 +284,16 @@
     )(feats, code, subj, bone_ids, skin, canon, table, w1, w2, w3, bias, head)
 
 
-def split_halves(side, total_s, mine_out, theirs_out, factor):
-    half = mine_out.shape[0]
-    mine_out[...] = (total_s[pl.ds(pl.multiple_of(side * half, 16), half), :] * factor).astype(BF16)
-    theirs_out[...] = (total_s[pl.ds(pl.multiple_of((1 - side) * half, 16), half), :] * factor).astype(BF16)
+def block_rows(width):
+    return -(-(3 * width + 48) // (2 * FAN * 16)) * 16
+
+
+def split_blocks(side, quarter, total_s, mine_out, theirs_out, factor):
+    rows = mine_out.shape[1]
+    for core, out in ((side, mine_out), (1 - side, theirs_out)):
+        for slot in range(FAN):
+            place = (core * FAN + lax.bitwise_xor(quarter, slot)) * rows
+            out[slot] = (total_s[pl.ds(pl.multiple_of(place, 16), rows), :] * factor).astype(BF16)
 
 
 def lane_sums(value):
@@ -296,24 +303,27 @@
     return jnp.sum(total.T, axis=0, keepdims=True)
 
 
-def upper_kernel(factor, subjects, per_subject, got, *refs):
-    (side_ref, pos_ref), refs = refs[:2], refs[2:]
+def backward_kernel(factor, subjects, per_subject, got, *refs):
+    (side_ref, quarter_ref, pos_ref), refs = refs[:3], refs[3:]
     got_refs, refs = refs[:got], refs[got:]
     (
         point_ref,
         blend_ref,
         bone_ref,
         subj_ref,
+        inputs_ref,
         act_one_ref,
         act_two_ref,
         act_three_ref,
+        slope_one_ref,
         slope_two_ref,
         slope_three_ref,
+        first_ref,
+        second_ref,
         third_ref,
         head_ref,
         outer_out,
         back_out,
-        rest_out,
         mine_out,
         theirs_out,
         total_s,
@@ -321,13 +331,13 @@
         masked_s,
     ) = refs
     width, members = act_one_ref.shape
-    lead = width // 2
     padded = bone_ref.shape[0] // 2
-    half = mine_out.shape[0]
+    small = 3 * width
 
     head_s[...] = jnp.zeros_like(head_s)
     head_s[0:3, :] = head_ref[...].astype(F32)
     head_w = head_s[...].astype(BF16)
+    total_s[small:, :] = jnp.zeros((total_s.shape[0] - small, width), F32)
     grad = pos_ref[0].astype(F32)
     for ref in got_refs:
         grad = grad + ref[...].astype(F32)
@@ -349,21 +359,29 @@
     shift = pulled[0:4] + pulled[4:8] + pulled[8:12]
     shift = jnp.where(rows[0:4] < 3, shift, 0.0)
     shift = jnp.concatenate([shift, jnp.zeros((12, members), F32)], axis=0).astype(BF16)
+
     back = mm(head_w, shift, TN) * slope_three_ref[...]
-    bias_three = lane_sums(back)
+    total_s[small + 5 : small + 6, :] = lane_sums(back)
     back = back.astype(BF16)
     total_s[0:width, :] = mm(back, act_two_ref[...], NT)
-    small = half + half - 32
     total_s[small : small + 3, :] = mm(shift, act_three_ref[...], NT)[0:3]
     back = mm(third_ref[...], back, TN) * slope_two_ref[...]
-    total_s[small + 3 : small + 4, :] = lane_sums(back)
-    total_s[small + 4 : small + 5, :] = bias_three
-    total_s[small + 5 : small + 16, :] = jnp.zeros((11, width), F32)
+    total_s[small + 4 : small + 5, :] = lane_sums(back)
     back = back.astype(BF16)
+    total_s[width : 2 * width, :] = mm(back, act_one_ref[...], NT)
+    back = (mm(second_ref[...], back, TN) * slope_one_ref[...]).astype(BF16)
     back_out[...] = back
-    second = mm(back, act_one_ref[...], NT)
-    total_s[width : width + lead, :] = second[0:lead]
-    rest_out[...] = second[lead:width]
+    product = mm(inputs_ref[...], back, NT)
+    total_s[2 * width : 3 * width, :] = product[0:width].T
+    by_subject = product[width : width + subjects]
+    total_s[small + 3 : small + 4, :] = jnp.sum(by_subject, axis=0, keepdims=True)
+    by_hi, by_rest = two_parts(by_subject)
+    by_mid, by_lo = two_parts(by_rest)
+    by_parts = jnp.concatenate([by_hi.astype(F32), by_mid.astype(F32), by_lo], axis=0).astype(BF16)
+    code = mm(by_parts, first_ref[...])
+    total_s[small + 32 : small + 32 + subjects, :] = (
+        code[0:subjects] + code[subjects : 2 * subjects] + code[2 * subjects : 3 * subjects]
+    )
 
     outer_hi, outer_lo = two_parts(outer)
     outer_lo = outer_lo.astype(BF16)
@@ -374,105 +392,51 @@
         masked_s[32 * s : 32 * s + 16, :] = jnp.where(inside, outer_hi, zero)
         masked_s[32 * s + 16 : 32 * s + 32, :] = jnp.where(inside, outer_lo, zero)
     product = mm(masked_s[...], bone_ref[...], NT)
-    total_s[small + 16 : small + 32, :] = jnp.zeros((16, width), F32)
     for s in range(subjects):
         both = product[32 * s : 32 * s + 16] + product[32 * s + 16 : 32 * s + 32]
         columns = slice(s * per_subject, (s + 1) * per_subject)
         total_s[small + 16 : small + 32, columns] = both[:, 0:per_subject] + both[:, padded : padded + per_subject]
-    split_halves(side_ref[0], total_s, mine_out, theirs_out, factor)
-
-
-def upper(side, pos, got, forwarded, subj, w3, head, factor, subjects, per_subject):
-    _, act_one, act_two, act_three, _, slope_two, slope_three, point, _, blend, bone = forwarded
+    split_blocks(side_ref[0], quarter_ref[0], total_s, mine_out, theirs_out, factor)
+
+
+def backward(side, quarter, pos, got, forwarded, subj, weights, head, factor, subjects, per_subject):
+    inputs, act_one, act_two, act_three, *slopes, point, _, blend, bone = forwarded
     width, members = act_one.shape
-    half = (width + width // 2 + 32) // 2
-    part = jax.ShapeDtypeStruct((half, width), BF16)
+    rows = block_rows(width)
+    part = jax.ShapeDtypeStruct((FAN, rows, width), BF16)
     return pl.pallas_call(
-        functools.partial(upper_kernel, factor, subjects, per_subject, len(got)),
+        functools.partial(backward_kernel, factor, subjects, per_subject, len(got)),
         out_shape=(
             jax.ShapeDtypeStruct((16, members), F32),
             jax.ShapeDtypeStruct((width, members), BF16),
-            jax.ShapeDtypeStruct((width // 2, width), F32),
             part,
             part,
         ),
-        in_specs=[SMEM] + [VMEM] * (12 + len(got)),
-        out_specs=(VMEM,) * 5,
+        in_specs=[SMEM] * 2 + [VMEM] * (16 + len(got)),
+        out_specs=(VMEM,) * 4,
         scratch_shapes=[
-            pltpu.VMEM((2 * half, width), F32),
+            pltpu.VMEM((2 * FAN * rows, width), F32),
             pltpu.VMEM((16, width), F32),
             pltpu.VMEM((32 * subjects, members), BF16),
         ],
-        compiler_params=params(16),
+        compiler_params=params(24),
     )(
         side,
+        quarter,
         pos,
         *got,
         point,
         blend,
         bone,
         subj,
+        inputs,
         act_one,
         act_two,
         act_three,
-        slope_two,
-        slope_three,
-        w3,
+        *slopes,
+        *weights,
         head,
     )
-
-
-def lower_kernel(
-    factor,
-    subjects,
-    side_ref,
-    back_ref,
-    rest_ref,
-    inputs_ref,
-    slope_ref,
-    second_ref,
-    first_ref,
-    back_out,
-    mine_out,
-    theirs_out,
-    total_s,
-):
-    width = back_out.shape[0]
-    half = mine_out.shape[0]
-    lead = width // 2
-    back = (mm(second_ref[...], back_ref[...], TN) * slope_ref[...]).astype(BF16)
-    back_out[...] = back
-    product = mm(inputs_ref[...], back, NT)
-    by_subject = product[width : width + subjects]
-    by_hi, by_rest = two_parts(by_subject)
-    by_mid, by_lo = two_parts(by_rest)
-    by_parts = jnp.concatenate([by_hi.astype(F32), by_mid.astype(F32), by_lo], axis=0).astype(BF16)
-    code = mm(by_parts, first_ref[...])
-    total_s[0:width, :] = product[0:width].T
-    total_s[width : width + lead, :] = rest_ref[...]
-    small = width + lead
-    total_s[small : small + subjects, :] = (
-        code[0:subjects] + code[subjects : 2 * subjects] + code[2 * subjects : 3 * subjects]
-    )
-    total_s[small + subjects : small + 16, :] = jnp.broadcast_to(
-        jnp.sum(by_subject, axis=0, keepdims=True), (16 - subjects, width)
-    )
-    total_s[small + 16 : small + 32, :] = jnp.zeros((16, width), F32)
-    split_halves(side_ref[0], total_s, mine_out, theirs_out, factor)
-
-
-def lower(side, back, rest, inputs, slope, w2, w1, factor, subjects):
-    width, members = back.shape
-    half = (width + width // 2 + 32) // 2
-    part = jax.ShapeDtypeStruct((half, width), BF16)
-    return pl.pallas_call(
-        functools.partial(lower_kernel, factor, subjects),
-        out_shape=(jax.ShapeDtypeStruct((width, members), BF16), part, part),
-        in_specs=[SMEM] + [VMEM] * 6,
-        out_specs=(VMEM,) * 3,
-        scratch_shapes=[pltpu.VMEM((2 * half, width), F32)],
-        compiler_params=params(16),
-    )(side, back, rest, inputs, slope, w2, w1)
 
 
 def gaussian_kernel(back_ref, first_ref, outer_ref, matrix_ref, feat_out, skin_out):
@@ -497,82 +461,50 @@
     )(back, w1, outer, matrix)
 
 
-def finish_kernel(
-    side_ref,
-    upper_mine,
-    upper_theirs,
-    lower_mine,
-    lower_theirs,
-    first_out,
-    second_out,
-    third_out,
-    bias_out,
-    head_out,
-    code_out,
-    bone_out,
-):
+def finish_kernel(side_ref, quarter_ref, *refs):
+    mine_refs, refs = refs[:FAN], refs[FAN:]
+    theirs_ref, first_out, second_out, third_out, bias_out, head_out, code_out, bone_out, total_s = refs
     width = third_out.shape[0]
-    half = upper_mine.shape[0]
-    lead = width // 2
     table_cols = bone_out.shape[1]
     subjects = code_out.shape[0]
-
-    def write(up, low):
-        def rows(pair, begin, end):
-            pieces = []
-            if begin < half:
-                pieces.append(pair[0][begin : min(end, half), :].astype(F32))
-            if end > half:
-                pieces.append(pair[1][max(begin, half) - half : end - half, :].astype(F32))
-            return pieces
-
-        def store(out, pair, begin, end, place=0):
-            for piece in rows(pair, begin, end):
-                out[place : place + piece.shape[0], :] = piece
-                place += piece.shape[0]
-
-        small = width + lead
-        store(third_out, up, 0, width)
-        store(second_out, up, width, small)
-        store(second_out, low, small - lead, small, lead)
-        store(first_out, low, 0, width)
-        (values,) = rows(up, small, small + 16)
-        head_out[...] = values[0:3]
-        bias_out[1:3, :] = values[3:5]
-        (values,) = rows(up, small + 16, small + 32)
-        bone_out[...] = values[0:12, 0:table_cols]
-        (values,) = rows(low, small, small + 16)
-        code_out[...] = values[0:subjects]
-        bias_out[0:1, :] = values[subjects : subjects + 1]
-
-    @pl.when(side_ref[0] == 0)
-    def _():
-        write((upper_mine, upper_theirs), (lower_mine, lower_theirs))
-
-    @pl.when(side_ref[0] != 0)
-    def _():
-        write((upper_theirs, upper_mine), (lower_theirs, lower_mine))
-
-
-def finish(side, upper_both, lower_both, subjects, table_cols):
-    width = upper_both[0].shape[1]
+    rows = mine_refs[0].shape[0]
+    side = side_ref[0]
+    for slot in range(FAN):
+        place = lax.bitwise_xor(quarter_ref[0], slot)
+        mine = pl.multiple_of((side * FAN + place) * rows, 16)
+        theirs = pl.multiple_of(((1 - side) * FAN + place) * rows, 16)
+        total_s[pl.ds(mine, rows), :] = mine_refs[slot][...].astype(F32)
+        total_s[pl.ds(theirs, rows), :] = theirs_ref[slot * rows : (slot + 1) * rows, :].astype(F32)
+    third_out[...] = total_s[0:width, :]
+    second_out[...] = total_s[width : 2 * width, :]
+    first_out[...] = total_s[2 * width : 3 * width, :]
+    small = total_s[3 * width : 3 * width + 48, :]
+    head_out[...] = small[0:3]
+    bias_out[...] = small[3:6]
+    bone_out[...] = small[16:28, 0:table_cols]
+    code_out[...] = small[32 : 32 + subjects]
+
+
+def finish(side, quarter, mine, theirs, subjects, table_cols):
+    rows, width = mine[0].shape
     square = jax.ShapeDtypeStruct((width, width), F32)
-    rows = jax.ShapeDtypeStruct((3, width), F32)
+    lines = jax.ShapeDtypeStruct((3, width), F32)
     return pl.pallas_call(
         finish_kernel,
         out_shape=(
             square,
             square,
             square,
-            rows,
-            rows,
+            lines,
+            lines,
             jax.ShapeDtypeStruct((subjects, width), F32),
             jax.ShapeDtypeStruct((12, table_cols), F32),
         ),
-        in_specs=[SMEM] + [VMEM] * 4,
+        in_specs=[SMEM] * 2 + [VMEM] * (FAN + 1),
         out_specs=(VMEM,) * 7,
+        scratch_shapes=[pltpu.VMEM((2 * FAN * rows, width), F32)],
         compiler_params=params(16),
-    )(side, *upper_both, *lower_both)
+    )(side, quarter, *mine, theirs)
 
 
 def attr_kernel(count, *refs):
@@ -613,18 +545,30 @@
     return list(held[0]), list(held[1])
 
 
-def sum_over_devices(halves, viewers, shards, between):
+def sum_over_devices(mine, theirs, viewers, shards, between):
     count = viewers * shards
     pair = shards
-    masks = [1 << bit for bit in range(count.bit_length() - 1) if 1 << bit != pair]
-    orders = [[masks[0], *masks[2:], masks[1]], [masks[1], masks[0], *masks[2:]]]
-    parts = [add(mine, swap(theirs, pair, count)) for mine, theirs in halves]
-    for stage in range(len(masks)):
-        got = [swap(part, order[stage], count) for part, order in zip(parts, orders)]
-        for work in between.get(stage, ()):
-            got[0] = work(parts[0], got[0])
-        parts = [add(part, other) for part, other in zip(parts, got)]
-    return [(part, swap(part, pair, count)) for part in parts]
+    rows, width = mine.shape[1:]
+    masks = [1 << bit for bit in range(count.bit_length() - 1) if 1 << bit >= FAN and 1 << bit != pair]
+
+    def work(stage, after, got):
+        for item in between.get(stage, ()):
+            got[0] = item(after, got[0])
+        return got
+
+    arrived = swap(theirs, pair, count)
+    blocks = [add(mine[slot], arrived[slot]) for slot in range(FAN)]
+    got = [swap(blocks[slot], slot, count) for slot in range(1, FAN)]
+    got = work("scatter", blocks[0], got)
+    total = sum((value.astype(F32) for value in got), blocks[0].astype(F32)).astype(BF16)
+    for stage, mask in enumerate(masks):
+        got = work(stage, total, [swap(total, mask, count)])
+        total = add(total, got[0])
+    got = [swap(total, slot, count) for slot in range(1, FAN)]
+    got = work("gather", total, got)
+    mine = [total, *got]
+    theirs = swap(jnp.concatenate(mine, axis=0), pair, count)
+    return mine, theirs
 
 
 class Work:
@@ -673,6 +617,7 @@
     factor = 1.0 / math.sqrt(members * viewers * shards)
     view = lax.axis_index("view").astype(jnp.int32).reshape(1)
     side = lax.bitwise_and(view, 1)
+    quarter = lax.bitwise_and(lax.axis_index("gauss").astype(jnp.int32).reshape(1), FAN - 1)
     position, arrays = entry(
         view,
         (
@@ -695,14 +640,21 @@
         viewers,
     )
     vis_ids, entry_grads, *arrays = arrays
-    subj_ids, (w_first, w_second, w_third), w_head = arrays[2], arrays[7:10], arrays[11]
+    subj_ids, weights, w_head = arrays[2], arrays[7:10], arrays[11]
     position_got = received(position, viewers)
     forwarded = forward(*arrays)
-    outer, back_two, second_rest, *upper_halves = upper(
-        side, position, position_got, forwarded, subj_ids, w_third, w_head, factor, subjects, table_cols // subjects
-    )
-    back_one, *lower_halves = lower(
-        side, back_two, second_rest, forwarded[0], forwarded[4], w_second, w_first, factor, subjects
+    outer, back_one, mine, theirs = backward(
+        side,
+        quarter,
+        position,
+        position_got,
+        forwarded,
+        subj_ids,
+        weights,
+        w_head,
+        factor,
+        subjects,
+        table_cols // subjects,
     )
 
     def scatter_rows(row):
@@ -712,19 +664,19 @@
         return Work(call, entry_grads, vis_ids)
 
     works = [scatter_rows(row) for row in range(GROUP, attrs, GROUP)]
-    per_gaussian = Work(gaussian_grads, back_one, w_first, outer, forwarded[8])
-
-    def exchange(_):
+    per_gaussian = Work(gaussian_grads, back_one, weights[0], outer, forwarded[8])
+
+    def attributes(_):
         others = jnp.concatenate([work.results[0] for work in works], axis=1)
         others_got = received(others, viewers)
         return [attr_sum(position, position_got, others, others_got, attrs)]
 
-    last = Work(exchange, view)
-    between = {0: [works[0]], 1: [works[1]], 2: [works[2], per_gaussian], 3: [last]}
-    upper_both, lower_both = sum_over_devices([upper_halves, lower_halves], viewers, shards, between)
+    last = Work(attributes, view)
+    between = {"scatter": works[:2], 0: works[2:], 1: [per_gaussian], "gather": [last]}
+    mine, theirs = sum_over_devices(mine, theirs, viewers, shards, between)
     attr = last.results[0]
     feat_grads, skin_grads = per_gaussian.results
-    first, second, third, bias, head, code, bone = finish(side, upper_both, lower_both, subjects, table_cols)
+    first, second, third, bias, head, code, bone = finish(side, quarter, mine, theirs, subjects, table_cols)
     return (
         attr,
         feat_grads[:, None, :],

time: 43.1 us -> 41.3 us (0.958)
  the two profiles are of different devices: /device:TPU:25 before, /device:TPU:0 now
where the time goes in v4:
time: 41.3 us; the launch traced here: 41.2 us
  Pallas kernels  18.4 us (45%)
  starting transfers between devices  12.8 us (31%)
  waiting for transfers between devices  8.98 us (22%)
  between operations  0.79 us (2%)
    ppermute x10, starting transfers between devices, swap(): lax.ppermute(value, AXES, [(place, place ^ mask) for place in range(count)])  12.2 us
    ppermute x10, waiting for transfers between devices, swap(): lax.ppermute(value, AXES, [(place, place ^ mask) for place in range(count)])  8.97 us
    pallas_call x1, Pallas kernels, backward(): pl.pallas_call(functools.partial(backward_kernel, factor, subjects, per_s...  4.27 us
    pallas_call x3, Pallas kernels, scatter(): pl.pallas_call(functools.partial(scatter_kernel, first_row, rows, viewers...  4.06 us
    pallas_call x1, Pallas kernels, forward(): pl.pallas_call(forward_kernel, out_shape=(jax.ShapeDtypeStruct((width + 1...  4.04 us
    pallas_call x1, Pallas kernels, entry(): pl.pallas_call(functools.partial(entry_kernel, viewers, count), out_shape...  2.45 us
    pallas_call x1, Pallas kernels, gaussian_grads(): pl.pallas_call(gaussian_kernel, out_shape=(jax.ShapeDtypeStruct((width, m...  1.6 us
    pallas_call x1, Pallas kernels, attr_sum(): pl.pallas_call(functools.partial(attr_kernel, count), out_shape=jax.Shape...  0.99 us
  transfers between devices with their start and end apart: 12, of which 7 were waited for; matrix products, arithmetic and copies ran while one was open for 0% of the time, Pallas kernels for 26%

profile of v4, /device:TPU:0, one launch (start us, length us, event | category | flops | bytes accessed | tf_op | source)
XLA Modules:
  0.0 41.2 jit_solution(12957298059350610859)
XLA Ops:
  0.7 2.5 %shard_map.213 = (bf16[2,16,2560]{2,1,0:T(8,128)(2,1)S(1)}, s32[1,5120]{1,0:T(1,128)S(1)}, bf16[1,59,5120]{2,1,0:T(8,128)(2,1)S(1)}, bf16[256,2560]{1,0:T(8,128)...) custom-call(s32[1]{0:T(128)} %bitcast.view_ref, ...), custom_call_target="tpu_custom_call" | custom-call | tf_op jit(solution)/shard_map/pallas_call | solution.py:125
  3.1 0.5 %collective-permute-start = (bf16[16,2560]{1,0:T(8,128)(2,1)S(1)}, bf16[16,2560]{1,0:T(8,128)(2,1)S(1)}, u32[]{:S(2)}, u32[]{:S(2)}) collective-permute-start(bf16[16,2560]{1,0:T(8,128)(2,1)S(1)} %slice_bitcast_fusion.1), channel_id=1, source_target_pairs={{0,16},{16,0},{1,17},{17,1},{2,18},{18,2},{3,19},{19,3},{4,20},{20... | collective-permute-start | bytes 245768 | tf_op jit(solution)/shard_map/ppermute | solution.py:591
  3.7 4.0 %shard_map.214 = (bf16[272,2560]{1,0:T(8,128)(2,1)S(1)}, bf16[256,2560]{1,0:T(8,128)(2,1)S(1)}, bf16[256,2560]{1,0:T(8,128)(2,1)S(1)}, bf16[256,2560]{1,0:T(8,12...) custom-call(bf16[256,2560]{1,0:T(8,128)(2,1)S(1)} %get-tuple-element, ...), custom_call_target="tpu_custom_call" | custom-call | tf_op jit(solution)/shard_map/pallas_call | solution.py:261
  7.7 0.0 collective-permute-done.refs_3_.refs_1_
  7.7 4.3 %shard_map.215 = (f32[16,2560]{1,0:T(8,128)S(1)}, bf16[256,2560]{1,0:T(8,128)(2,1)S(1)}, bf16[4,112,256]{2,1,0:T(8,128)(2,1)S(1)}, bf16[4,112,256]{2,1,0:T(8,128)(2,1)S(1)}) custom-call(s32[1]{0:T(128)S(6)} %and.10.refs_0_.side_ref, s32[1]{0:T(128)} %bitcast.4.refs_1_.quarter_ref, bf16[2,16,2560]{2,1,0:T(8,128)(2,1)S(1)} %get-tuple-element.68.refs_2_.refs_0_, ...), custom_call_target="tpu_custom_call" | custom-call | tf_op jit(solution)/shard_map/pallas_call | solution.py:407
  12.0 0.1 collective-permute-start.1
  12.1 1.4 %collective-permute-done.1 = bf16[4,112,256]{2,1,0:T(8,128)(2,1)S(1)} collective-permute-done((bf16[4,112,256]{2,1,0:T(8,128)(2,1)S(1)}, bf16[4,112,256]{2,1,0:T(8,128)(2,1)S(1)}, u32[]{:S(2)}, u32[]{:S(2)}) %collective-permute-start.1) | collective-permute-done | bytes 229408 | tf_op jit(solution)/shard_map/ppermute | solution.py:540
  13.5 0.1 fusion.2
  13.6 2.7 %collective-permute-start.2 = (bf16[112,256]{1,0:T(8,128)(2,1)S(1)}, bf16[112,256]{1,0:T(8,128)(2,1)S(1)}, u32[]{:S(2)}, u32[]{:S(2)}) collective-permute-start(bf16[112,256]{1,0:T(8,128)(2,1)S(1)} %get-tuple-element.128), channel_id=1, source_target_pairs={{0,1},{1,0},{2,3},{3,2},{4,5},{5,4},{6,7},{7,6},{8,9},{9,8},{10,11... | collective-permute-start | bytes 172040 | tf_op jit(solution)/shard_map/ppermute | solution.py:540
  16.3 1.5 %collective-permute-start.3 = (bf16[112,256]{1,0:T(8,128)(2,1)S(1)}, bf16[112,256]{1,0:T(8,128)(2,1)S(1)}, u32[]{:S(2)}, u32[]{:S(2)}) collective-permute-start(bf16[112,256]{1,0:T(8,128)(2,1)S(1)} %get-tuple-element.126), channel_id=1, source_target_pairs={{0,2},{1,3},{2,0},{3,1},{4,6},{5,7},{6,4},{7,5},{8,10},{9,11},{10,... | collective-permute-start | bytes 172040 | tf_op jit(solution)/shard_map/ppermute | solution.py:540
  17.8 0.0 collective-permute-start.4
  17.8 1.4 %shard_map.217 = bf16[2,16,2560]{2,1,0:T(8,128)(2,1)S(1)} custom-call(s32[1]{0:T(128)} %bitcast.view_ref, bf16[1,59,5120]{2,1,0:T(8,128)(2,1)S(1)} %get-tuple-element.101.grads_ref, s32[1,5120]{1,0:T(1,128)S(1)} %get-tuple-element.102.ids_ref), custom_call_target="tpu_custom_call" | custom-call | tf_op jit(solution)/shard_map/pallas_call | solution.py:92
  19.2 1.4 %shard_map.216 = bf16[2,16,2560]{2,1,0:T(8,128)(2,1)S(1)} custom-call(s32[1]{0:T(128)} %bitcast.view_ref, bf16[1,59,5120]{2,1,0:T(8,128)(2,1)S(1)} %get-tuple-element.101.grads_ref, s32[1,5120]{1,0:T(1,128)S(1)} %get-tuple-element.102.ids_ref), custom_call_target="tpu_custom_call" | custom-call | tf_op jit(solution)/shard_map/pallas_call | solution.py:92
  20.6 0.0 collective-permute-done.2
  20.6 0.0 collective-permute-done.3
  20.6 2.3 %collective-permute-done.4 = bf16[112,256]{1,0:T(8,128)(2,1)S(1)} collective-permute-done((bf16[112,256]{1,0:T(8,128)(2,1)S(1)}, bf16[112,256]{1,0:T(8,128)(2,1)S(1)}, u32[]{:S(2)}, u32[]{:S(2)}) %collective-permute-start.4) | collective-permute-done | bytes 57376 | tf_op jit(solution)/shard_map/ppermute | solution.py:540
  22.9 1.6 %collective-permute-start.5 = (bf16[112,256]{1,0:T(8,128)(2,1)S(1)}, bf16[112,256]{1,0:T(8,128)(2,1)S(1)}, u32[]{:S(2)}, u32[]{:S(2)}) collective-permute-start(bf16[112,256]{1,0:T(8,128)(2,1)S(1)} %add_convert_fusion.2), channel_id=1, source_target_pairs={{0,4},{1,5},{2,6},{3,7},{4,0},{5,1},{6,2},{7,3},{8,12},{9,13},{10,... | collective-permute-start | bytes 172040 | tf_op jit(solution)/shard_map/ppermute | solution.py:540
  24.6 1.4 %shard_map.218 = bf16[2,16,2560]{2,1,0:T(8,128)(2,1)S(1)} custom-call(s32[1]{0:T(128)} %bitcast.view_ref, bf16[1,59,5120]{2,1,0:T(8,128)(2,1)S(1)} %get-tuple-element.101.grads_ref, s32[1,5120]{1,0:T(1,128)S(1)} %get-tuple-element.102.ids_ref), custom_call_target="tpu_custom_call" | custom-call | tf_op jit(solution)/shard_map/pallas_call | solution.py:92
  26.0 1.2 %collective-permute-done.5 = bf16[112,256]{1,0:T(8,128)(2,1)S(1)} collective-permute-done((bf16[112,256]{1,0:T(8,128)(2,1)S(1)}, bf16[112,256]{1,0:T(8,128)(2,1)S(1)}, u32[]{:S(2)}, u32[]{:S(2)}) %collective-permute-start.5) | collective-permute-done | bytes 57376 | tf_op jit(solution)/shard_map/ppermute | solution.py:540
  27.2 2.6 %collective-permute-start.7 = (bf16[112,256]{1,0:T(8,128)(2,1)S(1)}, bf16[112,256]{1,0:T(8,128)(2,1)S(1)}, u32[]{:S(2)}, u32[]{:S(2)}) collective-permute-start(bf16[112,256]{1,0:T(8,128)(2,1)S(1)} %add_convert_fusion.1), channel_id=1, source_target_pairs={{0,8},{1,9},{2,10},{3,11},{4,12},{5,13},{6,14},{7,15},{8,0},{9,1},... | collective-permute-start | bytes 172040 | tf_op jit(solution)/shard_map/ppermute | solution.py:540
  29.9 0.1 collective-permute-start.6
  30.0 1.6 %shard_map.220 = (bf16[256,2560]{1,0:T(8,128)(2,1)}, f32[4,1,2560]{2,1,0:T(1,128)}) custom-call(bf16[256,2560]{1,0:T(8,128)(2,1)S(1)} %get-tuple-element.108.back_ref, bf16[256,256]{1,0:T(8,128)(2,1)S(1)} %get-tuple-element.109.first_ref.refs_15_, f32[16,2560]{1,0:T(8,128)S(1)} %get-tuple-element.110.outer_ref, f32[4,16,2560]{2,1,0:T(8,128)S(1)} %get-tuple-element.111.matrix_ref), custom_call_target="tpu_custom_call" | custom-call | tf_op jit(solution)/shard_map/pallas_call | solution.py:452
  31.6 0.8 %collective-permute-done.7 = bf16[112,256]{1,0:T(8,128)(2,1)S(1)} collective-permute-done((bf16[112,256]{1,0:T(8,128)(2,1)S(1)}, bf16[112,256]{1,0:T(8,128)(2,1)S(1)}, u32[]{:S(2)}, u32[]{:S(2)}) %collective-permute-start.7) | collective-permute-done | bytes 57376 | tf_op jit(solution)/shard_map/ppermute | solution.py:540
  32.4 0.6 %collective-permute-start.8 = (bf16[112,256]{1,0:T(8,128)(2,1)S(1)}, bf16[112,256]{1,0:T(8,128)(2,1)S(1)}, u32[]{:S(2)}, u32[]{:S(2)}) collective-permute-start(bf16[112,256]{1,0:T(8,128)(2,1)S(1)} %add_convert_fusion.refs_0_), channel_id=1, source_target_pairs={{0,1},{1,0},{2,3},{3,2},{4,5},{5,4},{6,7},{7,6},{8,9},{9,8},{10,11... | collective-permute-start | bytes 172040 | tf_op jit(solution)/shard_map/ppermute | solution.py:540
  32.9 1.4 %collective-permute-start.10 = (bf16[112,256]{1,0:T(8,128)(2,1)S(1)}, bf16[112,256]{1,0:T(8,128)(2,1)S(1)}, u32[]{:S(2)}, u32[]{:S(2)}) collective-permute-start(bf16[112,256]{1,0:T(8,128)(2,1)S(1)} %add_convert_fusion.refs_0_), channel_id=1, source_target_pairs={{0,3},{1,2},{2,1},{3,0},{4,7},{5,6},{6,5},{7,4},{8,11},{9,10},{10,... | collective-permute-start | bytes 172040 | tf_op jit(solution)/shard_map/ppermute | solution.py:540
  34.4 1.5 %collective-permute-start.9 = (bf16[112,256]{1,0:T(8,128)(2,1)S(1)}, bf16[112,256]{1,0:T(8,128)(2,1)S(1)}, u32[]{:S(2)}, u32[]{:S(2)}) collective-permute-start(bf16[112,256]{1,0:T(8,128)(2,1)S(1)} %add_convert_fusion.refs_0_), channel_id=1, source_target_pairs={{0,2},{1,3},{2,0},{3,1},{4,6},{5,7},{6,4},{7,5},{8,10},{9,11},{10,... | collective-permute-start | bytes 172040 | tf_op jit(solution)/shard_map/ppermute | solution.py:540
  35.9 0.0 collective-permute-done.6.refs_3_
  35.9 1.0 %shard_map.219 = f32[59,1,2560]{2,1,0:T(1,128)} custom-call(bf16[2,16,2560]{2,1,0:T(8,128)(2,1)S(1)} %get-tuple-element.68.refs_2_.refs_0_, bf16[16,2560]{1,0:T(8,128)(2,1)S(1)} %collective-permute-done.refs_3_.refs_1_, bf16[2,48,2560]{2,1,0:T(8,128)(2,1)S(1)} %constant_dynamic-update-slice_fusion.refs_2_, bf16[48,2560]{1,0:T(8,128)(2,1)S(1)} %collective-permute-done.6.refs_3_), custom_call_target="tpu_custom_call" | custom-call | tf_op jit(solution)/shard_map/pallas_call | solution.py:526
  36.9 0.0 collective-permute-done.8.refs_1_
  36.9 1.1 %collective-permute-done.10.refs_3_ = bf16[112,256]{1,0:T(8,128)(2,1)S(1)} collective-permute-done((bf16[112,256]{1,0:T(8,128)(2,1)S(1)}, bf16[112,256]{1,0:T(8,128)(2,1)S(1)}, u32[]{:S(2)}, u32[]{:S(2)}) %collective-permute-start.10) | collective-permute-done | bytes 57376 | tf_op jit(solution)/shard_map/ppermute | solution.py:540
  38.0 0.6 %collective-permute-done.9.refs_2_ = bf16[112,256]{1,0:T(8,128)(2,1)S(1)} collective-permute-done((bf16[112,256]{1,0:T(8,128)(2,1)S(1)}, bf16[112,256]{1,0:T(8,128)(2,1)S(1)}, u32[]{:S(2)}, u32[]{:S(2)}) %collective-permute-start.9) | collective-permute-done | bytes 57376 | tf_op jit(solution)/shard_map/ppermute | solution.py:540
  38.7 0.1 collective-permute-start.11
  38.7 1.5 %collective-permute-done.11.refs_4_ = bf16[448,256]{1,0:T(8,128)(2,1)S(1)} collective-permute-done((bf16[448,256]{1,0:T(8,128)(2,1)S(1)}, bf16[448,256]{1,0:T(8,128)(2,1)S(1)}, u32[]{:S(2)}, u32[]{:S(2)}) %collective-permute-start.11) | collective-permute-done | bytes 229408 | tf_op jit(solution)/shard_map/ppermute | solution.py:540
  40.2 1.0 %shard_map.221 = (f32[256,256]{1,0:T(8,128)}, f32[256,256]{1,0:T(8,128)}, f32[256,256]{1,0:T(8,128)}, f32[3,256]{1,0:T(4,128)}, f32[3,256]{1,0:T(4,128)}, /*index=5*/f32[8,256]{1,0:T(8,128)}, f32[12,192]{1,0:T(8,128)}) custom-call(s32[1]{0:T(128)S(6)} %and.10.refs_0_.side_ref, s32[1]{0:T(128)} %bitcast.4.refs_1_.quarter_ref, ...), custom_call_target="tpu_custom_call" | custom-call | tf_op jit(solution)/shard_map/pallas_call | solution.py:492
  (9 shorter events, 0.1 us)
Async XLA Ops:
  3.1 4.6 %collective-permute-start = (bf16[16,2560]{1,0:T(8,128)(2,1)S(1)}, bf16[16,2560]{1,0:T(8,128)(2,1)S(1)}, u32[]{:S(2)}, u32[]{:S(2)}) collective-permute-start(bf16[16,2560]{1,0:T(8,128)(2,1)S(1)} %slice_bitcast_fusion.1), channel_id=1, source_target_pairs={{0,16},{16,0},{1,17},{17,1},{2,18},{18,2},{3,19},{19,3},{4,20},{20... | collective-permute-start | bytes 245768 | tf_op jit(solution)/shard_map/ppermute | solution.py:591
  12.0 1.6 %collective-permute-start.1 = (bf16[4,112,256]{2,1,0:T(8,128)(2,1)S(1)}, bf16[4,112,256]{2,1,0:T(8,128)(2,1)S(1)}, u32[]{:S(2)}, u32[]{:S(2)}) collective-permute-start(bf16[4,112,256]{2,1,0:T(8,128)(2,1)S(1)} %get-tuple-element.94), channel_id=1, source_target_pairs={{0,16},{1,17},{2,18},{3,19},{4,20},{5,21},{6,22},{7,23},{8,24},{9,... | collective-permute-start | bytes 688136 | tf_op jit(solution)/shard_map/ppermute | solution.py:540
  13.6 7.0 %collective-permute-start.2 = (bf16[112,256]{1,0:T(8,128)(2,1)S(1)}, bf16[112,256]{1,0:T(8,128)(2,1)S(1)}, u32[]{:S(2)}, u32[]{:S(2)}) collective-permute-start(bf16[112,256]{1,0:T(8,128)(2,1)S(1)} %get-tuple-element.128), channel_id=1, source_target_pairs={{0,1},{1,0},{2,3},{3,2},{4,5},{5,4},{6,7},{7,6},{8,9},{9,8},{10,11... | collective-permute-start | bytes 172040 | tf_op jit(solution)/shard_map/ppermute | solution.py:540
  16.3 4.3 %collective-permute-start.3 = (bf16[112,256]{1,0:T(8,128)(2,1)S(1)}, bf16[112,256]{1,0:T(8,128)(2,1)S(1)}, u32[]{:S(2)}, u32[]{:S(2)}) collective-permute-start(bf16[112,256]{1,0:T(8,128)(2,1)S(1)} %get-tuple-element.126), channel_id=1, source_target_pairs={{0,2},{1,3},{2,0},{3,1},{4,6},{5,7},{6,4},{7,5},{8,10},{9,11},{10,... | collective-permute-start | bytes 172040 | tf_op jit(solution)/shard_map/ppermute | solution.py:540
  17.8 5.1 %collective-permute-start.4 = (bf16[112,256]{1,0:T(8,128)(2,1)S(1)}, bf16[112,256]{1,0:T(8,128)(2,1)S(1)}, u32[]{:S(2)}, u32[]{:S(2)}) collective-permute-start(bf16[112,256]{1,0:T(8,128)(2,1)S(1)} %get-tuple-element.127), channel_id=1, source_target_pairs={{0,3},{1,2},{2,1},{3,0},{4,7},{5,6},{6,5},{7,4},{8,11},{9,10},{10,... | collective-permute-start | bytes 172040 | tf_op jit(solution)/shard_map/ppermute | solution.py:540
  22.9 4.2 %collective-permute-start.5 = (bf16[112,256]{1,0:T(8,128)(2,1)S(1)}, bf16[112,256]{1,0:T(8,128)(2,1)S(1)}, u32[]{:S(2)}, u32[]{:S(2)}) collective-permute-start(bf16[112,256]{1,0:T(8,128)(2,1)S(1)} %add_convert_fusion.2), channel_id=1, source_target_pairs={{0,4},{1,5},{2,6},{3,7},{4,0},{5,1},{6,2},{7,3},{8,12},{9,13},{10,... | collective-permute-start | bytes 172040 | tf_op jit(solution)/shard_map/ppermute | solution.py:540
  27.2 5.1 %collective-permute-start.7 = (bf16[112,256]{1,0:T(8,128)(2,1)S(1)}, bf16[112,256]{1,0:T(8,128)(2,1)S(1)}, u32[]{:S(2)}, u32[]{:S(2)}) collective-permute-start(bf16[112,256]{1,0:T(8,128)(2,1)S(1)} %add_convert_fusion.1), channel_id=1, source_target_pairs={{0,8},{1,9},{2,10},{3,11},{4,12},{5,13},{6,14},{7,15},{8,0},{9,1},... | collective-permute-start | bytes 172040 | tf_op jit(solution)/shard_map/ppermute | solution.py:540
  29.9 6.0 %collective-permute-start.6 = (bf16[48,2560]{1,0:T(8,128)(2,1)S(1)}, bf16[48,2560]{1,0:T(8,128)(2,1)S(1)}, u32[]{:S(2)}, u32[]{:S(2)}) collective-permute-start(bf16[48,2560]{1,0:T(8,128)(2,1)S(1)} %slice_bitcast_fusion), channel_id=1, source_target_pairs={{0,16},{16,0},{1,17},{17,1},{2,18},{18,2},{3,19},{19,3},{4,20},{20... | collective-permute-start | bytes 737288 | tf_op jit(solution)/shard_map/ppermute | solution.py:591
  32.4 4.5 %collective-permute-start.8 = (bf16[112,256]{1,0:T(8,128)(2,1)S(1)}, bf16[112,256]{1,0:T(8,128)(2,1)S(1)}, u32[]{:S(2)}, u32[]{:S(2)}) collective-permute-start(bf16[112,256]{1,0:T(8,128)(2,1)S(1)} %add_convert_fusion.refs_0_), channel_id=1, source_target_pairs={{0,1},{1,0},{2,3},{3,2},{4,5},{5,4},{6,7},{7,6},{8,9},{9,8},{10,11... | collective-permute-start | bytes 172040 | tf_op jit(solution)/shard_map/ppermute | solution.py:540
  32.9 5.1 %collective-permute-start.10 = (bf16[112,256]{1,0:T(8,128)(2,1)S(1)}, bf16[112,256]{1,0:T(8,128)(2,1)S(1)}, u32[]{:S(2)}, u32[]{:S(2)}) collective-permute-start(bf16[112,256]{1,0:T(8,128)(2,1)S(1)} %add_convert_fusion.refs_0_), channel_id=1, source_target_pairs={{0,3},{1,2},{2,1},{3,0},{4,7},{5,6},{6,5},{7,4},{8,11},{9,10},{10,... | collective-permute-start | bytes 172040 | tf_op jit(solution)/shard_map/ppermute | solution.py:540
  34.4 4.2 %collective-permute-start.9 = (bf16[112,256]{1,0:T(8,128)(2,1)S(1)}, bf16[112,256]{1,0:T(8,128)(2,1)S(1)}, u32[]{:S(2)}, u32[]{:S(2)}) collective-permute-start(bf16[112,256]{1,0:T(8,128)(2,1)S(1)} %add_convert_fusion.refs_0_), channel_id=1, source_target_pairs={{0,2},{1,3},{2,0},{3,1},{4,6},{5,7},{6,4},{7,5},{8,10},{9,11},{10,... | collective-permute-start | bytes 172040 | tf_op jit(solution)/shard_map/ppermute | solution.py:540
  38.7 1.6 %collective-permute-start.11 = (bf16[448,256]{1,0:T(8,128)(2,1)S(1)}, bf16[448,256]{1,0:T(8,128)(2,1)S(1)}, u32[]{:S(2)}, u32[]{:S(2)}) collective-permute-start(bf16[448,256]{1,0:T(8,128)(2,1)S(1)} %pad_maximum_fusion), channel_id=1, source_target_pairs={{0,16},{1,17},{2,18},{3,19},{4,20},{5,21},{6,22},{7,23},{8,24},{9,... | collective-permute-start | bytes 688136 | tf_op jit(solution)/shard_map/ppermute | solution.py:540

commit v5 on v4

--- a/solution.py
+++ b/solution.py
@@ -179,7 +179,7 @@
     table_cols = table_ref.shape[1]
     per_subject = table_cols // subjects
     influence = bone_ids_ref.shape[0]
-    padded = bone_out.shape[0] // 2
+    padded = bone_out.shape[0]
     pieces = table_s.shape[1] // 128
 
     head_s[...] = jnp.zeros_like(head_s)
@@ -201,19 +201,26 @@
     x = (feats_ref[...].astype(F32) + mm(code_w, hot)).astype(BF16)
     inputs_out[0:width, :] = x
     inputs_out[width : width + 16, :] = hot[0:16]
-    act = x
     layers = (
         (first_ref, act_one_out, slope_one_out),
         (second_ref, act_two_out, slope_two_out),
         (third_ref, act_three_out, slope_three_out),
     )
+    half = jnp.asarray(0.5, BF16)
+    source = inputs_out
     for layer, (weight, act_out, slope_out) in enumerate(layers):
-        pre = mm(weight[...], act) + bias_cols[:, layer : layer + 1]
-        sig = 0.5 * jnp.tanh(0.5 * pre) + 0.5
-        value = pre * sig
-        slope_out[...] = sig + value * (1.0 - sig)
-        act = value.astype(BF16)
-        act_out[...] = act
+        halved = weight[...] * half
+        bias = 0.5 * bias_cols[:, layer : layer + 1]
+        for lane in range(0, members, LOW):
+            tile = slice(lane, lane + LOW)
+            pre = mm(halved, source[0:width, tile]) + bias
+            turn = jnp.tanh(pre)
+            more = 1.0 + turn
+            value = pre * more
+            act_out[:, tile] = value.astype(BF16)
+            slope_out[:, tile] = more + value * (1.0 - turn)
+        source = act_out
+    act = act_three_out[...]
     moved = mm(head_w, act)
     for axis in range(3):
         point_out[axis : axis + 1, :] = canon_ref[axis] + moved[axis : axis + 1]
@@ -224,9 +231,7 @@
     for member in range(influence):
         chosen = bone_ids_ref[member]
         spread = spread + jnp.where(bone_rows == chosen, skin_ref[member], 0.0)
-    spread_hi, spread_lo = two_parts(spread)
-    bone_out[0:padded, :] = spread_hi
-    bone_out[padded : 2 * padded, :] = spread_lo.astype(BF16)
+    bone_out[...] = spread.astype(BF16)
 
     for tile in range(members // 128):
         lanes = slice(tile * 128, (tile + 1) * 128)
@@ -271,7 +276,7 @@
             jax.ShapeDtypeStruct((4, members), F32),
             jax.ShapeDtypeStruct((influence, 16, members), F32),
             jax.ShapeDtypeStruct((16, members), F32),
-            jax.ShapeDtypeStruct((2 * padded, members), BF16),
+            jax.ShapeDtypeStruct((padded, members), BF16),
         ),
         in_specs=[VMEM] * 12,
         out_specs=(VMEM,) * 11,
@@ -331,7 +336,6 @@
         masked_s,
     ) = refs
     width, members = act_one_ref.shape
-    padded = bone_ref.shape[0] // 2
     small = 3 * width
 
     head_s[...] = jnp.zeros_like(head_s)
@@ -360,16 +364,27 @@
     shift = jnp.where(rows[0:4] < 3, shift, 0.0)
     shift = jnp.concatenate([shift, jnp.zeros((12, members), F32)], axis=0).astype(BF16)
 
-    back = mm(head_w, shift, TN) * slope_three_ref[...]
+    outer = outer.astype(BF16)
+    subject = jnp.broadcast_to(subj_ref[...].astype(F32).astype(BF16), (16, members))
+    zero = jnp.zeros((), BF16)
+    for s in range(subjects):
+        masked_s[16 * s : 16 * s + 16, :] = jnp.where(subject == jnp.asarray(s, BF16), outer, zero)
+    product = mm(masked_s[...], bone_ref[...], NT)
+    for s in range(subjects):
+        columns = slice(s * per_subject, (s + 1) * per_subject)
+        total_s[small + 16 : small + 32, columns] = product[16 * s : 16 * s + 16, 0:per_subject]
+
+    half = jnp.asarray(0.5, BF16)
+    back = mm(head_w * half, shift, TN) * slope_three_ref[...]
     total_s[small + 5 : small + 6, :] = lane_sums(back)
     back = back.astype(BF16)
     total_s[0:width, :] = mm(back, act_two_ref[...], NT)
     total_s[small : small + 3, :] = mm(shift, act_three_ref[...], NT)[0:3]
-    back = mm(third_ref[...], back, TN) * slope_two_ref[...]
+    back = mm(third_ref[...] * half, back, TN) * slope_two_ref[...]
     total_s[small + 4 : small + 5, :] = lane_sums(back)
     back = back.astype(BF16)
     total_s[width : 2 * width, :] = mm(back, act_one_ref[...], NT)
-    back = (mm(second_ref[...], back, TN) * slope_one_ref[...]).astype(BF16)
+    back = (mm(second_ref[...] * half, back, TN) * slope_one_ref[...]).astype(BF16)
     back_out[...] = back
     product = mm(inputs_ref[...], back, NT)
     total_s[2 * width : 3 * width, :] = product[0:width].T
@@ -383,19 +398,6 @@
         code[0:subjects] + code[subjects : 2 * subjects] + code[2 * subjects : 3 * subjects]
     )
 
-    outer_hi, outer_lo = two_parts(outer)
-    outer_lo = outer_lo.astype(BF16)
-    subject = jnp.broadcast_to(subj_ref[...].astype(F32).astype(BF16), (16, members))
-    zero = jnp.zeros((), BF16)
-    for s in range(subjects):
-        inside = subject == jnp.asarray(s, BF16)
-        masked_s[32 * s : 32 * s + 16, :] = jnp.where(inside, outer_hi, zero)
-        masked_s[32 * s + 16 : 32 * s + 32, :] = jnp.where(inside, outer_lo, zero)
-    product = mm(masked_s[...], bone_ref[...], NT)
-    for s in range(subjects):
-        both = product[32 * s : 32 * s + 16] + product[32 * s + 16 : 32 * s + 32]
-        columns = slice(s * per_subject, (s + 1) * per_subject)
-        total_s[small + 16 : small + 32, columns] = both[:, 0:per_subject] + both[:, padded : padded + per_subject]
     split_blocks(side_ref[0], quarter_ref[0], total_s, mine_out, theirs_out, factor)
 
 
@@ -417,7 +419,7 @@
         scratch_shapes=[
             pltpu.VMEM((2 * FAN * rows, width), F32),
             pltpu.VMEM((16, width), F32),
-            pltpu.VMEM((32 * subjects, members), BF16),
+            pltpu.VMEM((16 * subjects, members), BF16),
         ],
         compiler_params=params(24),
     )(

time: 41.3 us -> 39.4 us (0.954)
  Pallas kernels: 18.4 us -> 16.4 us
    pallas_call x1, Pallas kernels: 4.27 us -> 3.15 us  [backward(): pl.pallas_call(functools.partial(backward_kernel, factor, subjects, per_s...]
    pallas_call x1, Pallas kernels: 4.04 us -> 3.24 us  [forward(): pl.pallas_call(forward_kernel, out_shape=(jax.ShapeDtypeStruct((width + 1...]
  transfers between devices with their start and end apart: 12 -> 12, of which waited for: 7 -> 7; matrix products, arithmetic and copies ran while one was open for 0% -> 0% of each run, Pallas kernels for 26% -> 25%
where the time goes in v5:
time: 39.4 us; the launch traced here: 39.3 us
  Pallas kernels  16.4 us (42%)
  starting transfers between devices  12.9 us (33%)
  waiting for transfers between devices  8.99 us (23%)
  between operations  0.79 us (2%)
    ppermute x10, starting transfers between devices, swap(): lax.ppermute(value, AXES, [(place, place ^ mask) for place in range(count)])  12.3 us
    ppermute x10, waiting for transfers between devices, swap(): lax.ppermute(value, AXES, [(place, place ^ mask) for place in range(count)])  8.99 us
    pallas_call x3, Pallas kernels, scatter(): pl.pallas_call(functools.partial(scatter_kernel, first_row, rows, viewers...  4.02 us
    pallas_call x1, Pallas kernels, forward(): pl.pallas_call(forward_kernel, out_shape=(jax.ShapeDtypeStruct((width + 1...  3.24 us
    pallas_call x1, Pallas kernels, backward(): pl.pallas_call(functools.partial(backward_kernel, factor, subjects, per_s...  3.15 us
    pallas_call x1, Pallas kernels, entry(): pl.pallas_call(functools.partial(entry_kernel, viewers, count), out_shape...  2.45 us
    pallas_call x1, Pallas kernels, gaussian_grads(): pl.pallas_call(gaussian_kernel, out_shape=(jax.ShapeDtypeStruct((width, m...  1.6 us
    pallas_call x1, Pallas kernels, attr_sum(): pl.pallas_call(functools.partial(attr_kernel, count), out_shape=jax.Shape...  0.99 us
  transfers between devices with their start and end apart: 12, of which 7 were waited for; matrix products, arithmetic and copies ran while one was open for 0% of the time, Pallas kernels for 25%

profile of v5, /device:TPU:0, one launch (start us, length us, event | category | flops | bytes accessed | tf_op | source)
XLA Modules:
  0.0 39.3 jit_solution(5948726802206977093)
XLA Ops:
  0.7 2.5 %shard_map.213 = (bf16[2,16,2560]{2,1,0:T(8,128)(2,1)S(1)}, s32[1,5120]{1,0:T(1,128)S(1)}, bf16[1,59,5120]{2,1,0:T(8,128)(2,1)S(1)}, bf16[256,2560]{1,0:T(8,128)...) custom-call(s32[1]{0:T(128)} %bitcast.view_ref, ...), custom_call_target="tpu_custom_call" | custom-call | tf_op jit(solution)/shard_map/pallas_call | solution.py:125
  3.1 0.5 %collective-permute-start = (bf16[16,2560]{1,0:T(8,128)(2,1)S(1)}, bf16[16,2560]{1,0:T(8,128)(2,1)S(1)}, u32[]{:S(2)}, u32[]{:S(2)}) collective-permute-start(bf16[16,2560]{1,0:T(8,128)(2,1)S(1)} %slice_bitcast_fusion.1), channel_id=1, source_target_pairs={{0,16},{16,0},{1,17},{17,1},{2,18},{18,2},{3,19},{19,3},{4,20},{20... | collective-permute-start | bytes 245768 | tf_op jit(solution)/shard_map/ppermute | solution.py:593
  3.7 3.2 %shard_map.214 = (bf16[272,2560]{1,0:T(8,128)(2,1)S(1)}, bf16[256,2560]{1,0:T(8,128)(2,1)S(1)}, bf16[256,2560]{1,0:T(8,128)(2,1)S(1)}, bf16[256,2560]{1,0:T(8,12...) custom-call(bf16[256,2560]{1,0:T(8,128)(2,1)S(1)} %get-tuple-element, ...), custom_call_target="tpu_custom_call" | custom-call | tf_op jit(solution)/shard_map/pallas_call | solution.py:266
  6.9 0.0 collective-permute-done.refs_3_.refs_1_
  6.9 3.2 %shard_map.215 = (f32[16,2560]{1,0:T(8,128)S(1)}, bf16[256,2560]{1,0:T(8,128)(2,1)S(1)}, bf16[4,112,256]{2,1,0:T(8,128)(2,1)S(1)}, bf16[4,112,256]{2,1,0:T(8,128)(2,1)S(1)}) custom-call(s32[1]{0:T(128)S(6)} %and.10.refs_0_.side_ref, s32[1]{0:T(128)} %bitcast.4.refs_1_.quarter_ref, bf16[2,16,2560]{2,1,0:T(8,128)(2,1)S(1)} %get-tuple-element.68.refs_2_.refs_0_, ...), custom_call_target="tpu_custom_call" | custom-call | tf_op jit(solution)/shard_map/pallas_call | solution.py:409
  10.1 0.1 collective-permute-start.1
  10.2 1.4 %collective-permute-done.1 = bf16[4,112,256]{2,1,0:T(8,128)(2,1)S(1)} collective-permute-done((bf16[4,112,256]{2,1,0:T(8,128)(2,1)S(1)}, bf16[4,112,256]{2,1,0:T(8,128)(2,1)S(1)}, u32[]{:S(2)}, u32[]{:S(2)}) %collective-permute-start.1) | collective-permute-done | bytes 229408 | tf_op jit(solution)/shard_map/ppermute | solution.py:542
  11.6 0.1 fusion.2
  11.7 2.7 %collective-permute-start.2 = (bf16[112,256]{1,0:T(8,128)(2,1)S(1)}, bf16[112,256]{1,0:T(8,128)(2,1)S(1)}, u32[]{:S(2)}, u32[]{:S(2)}) collective-permute-start(bf16[112,256]{1,0:T(8,128)(2,1)S(1)} %get-tuple-element.128), channel_id=1, source_target_pairs={{0,1},{1,0},{2,3},{3,2},{4,5},{5,4},{6,7},{7,6},{8,9},{9,8},{10,11... | collective-permute-start | bytes 172040 | tf_op jit(solution)/shard_map/ppermute | solution.py:542
  14.4 1.5 %collective-permute-start.3 = (bf16[112,256]{1,0:T(8,128)(2,1)S(1)}, bf16[112,256]{1,0:T(8,128)(2,1)S(1)}, u32[]{:S(2)}, u32[]{:S(2)}) collective-permute-start(bf16[112,256]{1,0:T(8,128)(2,1)S(1)} %get-tuple-element.126), channel_id=1, source_target_pairs={{0,2},{1,3},{2,0},{3,1},{4,6},{5,7},{6,4},{7,5},{8,10},{9,11},{10,... | collective-permute-start | bytes 172040 | tf_op jit(solution)/shard_map/ppermute | solution.py:542
  15.9 0.0 collective-permute-start.4
  15.9 1.3 %shard_map.217 = bf16[2,16,2560]{2,1,0:T(8,128)(2,1)S(1)} custom-call(s32[1]{0:T(128)} %bitcast.view_ref, bf16[1,59,5120]{2,1,0:T(8,128)(2,1)S(1)} %get-tuple-element.101.grads_ref, s32[1,5120]{1,0:T(1,128)S(1)} %get-tuple-element.102.ids_ref), custom_call_target="tpu_custom_call" | custom-call | tf_op jit(solution)/shard_map/pallas_call | solution.py:92
  17.3 1.4 %shard_map.216 = bf16[2,16,2560]{2,1,0:T(8,128)(2,1)S(1)} custom-call(s32[1]{0:T(128)} %bitcast.view_ref, bf16[1,59,5120]{2,1,0:T(8,128)(2,1)S(1)} %get-tuple-element.101.grads_ref, s32[1,5120]{1,0:T(1,128)S(1)} %get-tuple-element.102.ids_ref), custom_call_target="tpu_custom_call" | custom-call | tf_op jit(solution)/shard_map/pallas_call | solution.py:92
  18.6 0.0 collective-permute-done.2
  18.6 0.0 collective-permute-done.3
  18.6 2.3 %collective-permute-done.4 = bf16[112,256]{1,0:T(8,128)(2,1)S(1)} collective-permute-done((bf16[112,256]{1,0:T(8,128)(2,1)S(1)}, bf16[112,256]{1,0:T(8,128)(2,1)S(1)}, u32[]{:S(2)}, u32[]{:S(2)}) %collective-permute-start.4) | collective-permute-done | bytes 57376 | tf_op jit(solution)/shard_map/ppermute | solution.py:542
  21.0 1.6 %collective-permute-start.5 = (bf16[112,256]{1,0:T(8,128)(2,1)S(1)}, bf16[112,256]{1,0:T(8,128)(2,1)S(1)}, u32[]{:S(2)}, u32[]{:S(2)}) collective-permute-start(bf16[112,256]{1,0:T(8,128)(2,1)S(1)} %add_convert_fusion.2), channel_id=1, source_target_pairs={{0,4},{1,5},{2,6},{3,7},{4,0},{5,1},{6,2},{7,3},{8,12},{9,13},{10,... | collective-permute-start | bytes 172040 | tf_op jit(solution)/shard_map/ppermute | solution.py:542
  22.7 1.3 %shard_map.218 = bf16[2,16,2560]{2,1,0:T(8,128)(2,1)S(1)} custom-call(s32[1]{0:T(128)} %bitcast.view_ref, bf16[1,59,5120]{2,1,0:T(8,128)(2,1)S(1)} %get-tuple-element.101.grads_ref, s32[1,5120]{1,0:T(1,128)S(1)} %get-tuple-element.102.ids_ref), custom_call_target="tpu_custom_call" | custom-call | tf_op jit(solution)/shard_map/pallas_call | solution.py:92
  24.0 1.2 %collective-permute-done.5 = bf16[112,256]{1,0:T(8,128)(2,1)S(1)} collective-permute-done((bf16[112,256]{1,0:T(8,128)(2,1)S(1)}, bf16[112,256]{1,0:T(8,128)(2,1)S(1)}, u32[]{:S(2)}, u32[]{:S(2)}) %collective-permute-start.5) | collective-permute-done | bytes 57376 | tf_op jit(solution)/shard_map/ppermute | solution.py:542
  25.3 2.6 %collective-permute-start.7 = (bf16[112,256]{1,0:T(8,128)(2,1)S(1)}, bf16[112,256]{1,0:T(8,128)(2,1)S(1)}, u32[]{:S(2)}, u32[]{:S(2)}) collective-permute-start(bf16[112,256]{1,0:T(8,128)(2,1)S(1)} %add_convert_fusion.1), channel_id=1, source_target_pairs={{0,8},{1,9},{2,10},{3,11},{4,12},{5,13},{6,14},{7,15},{8,0},{9,1},... | collective-permute-start | bytes 172040 | tf_op jit(solution)/shard_map/ppermute | solution.py:542
  28.0 0.1 collective-permute-start.6
  28.0 1.6 %shard_map.220 = (bf16[256,2560]{1,0:T(8,128)(2,1)}, f32[4,1,2560]{2,1,0:T(1,128)}) custom-call(bf16[256,2560]{1,0:T(8,128)(2,1)S(1)} %get-tuple-element.108.back_ref, bf16[256,256]{1,0:T(8,128)(2,1)S(1)} %get-tuple-element.109.first_ref.refs_15_, f32[16,2560]{1,0:T(8,128)S(1)} %get-tuple-element.110.outer_ref, f32[4,16,2560]{2,1,0:T(8,128)S(1)} %get-tuple-element.111.matrix_ref), custom_call_target="tpu_custom_call" | custom-call | tf_op jit(solution)/shard_map/pallas_call | solution.py:454
  29.6 0.8 %collective-permute-done.7 = bf16[112,256]{1,0:T(8,128)(2,1)S(1)} collective-permute-done((bf16[112,256]{1,0:T(8,128)(2,1)S(1)}, bf16[112,256]{1,0:T(8,128)(2,1)S(1)}, u32[]{:S(2)}, u32[]{:S(2)}) %collective-permute-start.7) | collective-permute-done | bytes 57376 | tf_op jit(solution)/shard_map/ppermute | solution.py:542
  30.4 0.6 %collective-permute-start.8 = (bf16[112,256]{1,0:T(8,128)(2,1)S(1)}, bf16[112,256]{1,0:T(8,128)(2,1)S(1)}, u32[]{:S(2)}, u32[]{:S(2)}) collective-permute-start(bf16[112,256]{1,0:T(8,128)(2,1)S(1)} %add_convert_fusion.refs_0_), channel_id=1, source_target_pairs={{0,1},{1,0},{2,3},{3,2},{4,5},{5,4},{6,7},{7,6},{8,9},{9,8},{10,11... | collective-permute-start | bytes 172040 | tf_op jit(solution)/shard_map/ppermute | solution.py:542
  31.0 1.4 %collective-permute-start.10 = (bf16[112,256]{1,0:T(8,128)(2,1)S(1)}, bf16[112,256]{1,0:T(8,128)(2,1)S(1)}, u32[]{:S(2)}, u32[]{:S(2)}) collective-permute-start(bf16[112,256]{1,0:T(8,128)(2,1)S(1)} %add_convert_fusion.refs_0_), channel_id=1, source_target_pairs={{0,3},{1,2},{2,1},{3,0},{4,7},{5,6},{6,5},{7,4},{8,11},{9,10},{10,... | collective-permute-start | bytes 172040 | tf_op jit(solution)/shard_map/ppermute | solution.py:542
  32.5 1.5 %collective-permute-start.9 = (bf16[112,256]{1,0:T(8,128)(2,1)S(1)}, bf16[112,256]{1,0:T(8,128)(2,1)S(1)}, u32[]{:S(2)}, u32[]{:S(2)}) collective-permute-start(bf16[112,256]{1,0:T(8,128)(2,1)S(1)} %add_convert_fusion.refs_0_), channel_id=1, source_target_pairs={{0,2},{1,3},{2,0},{3,1},{4,6},{5,7},{6,4},{7,5},{8,10},{9,11},{10,... | collective-permute-start | bytes 172040 | tf_op jit(solution)/shard_map/ppermute | solution.py:542
  34.0 0.0 collective-permute-done.6.refs_3_
  34.0 1.0 %shard_map.219 = f32[59,1,2560]{2,1,0:T(1,128)} custom-call(bf16[2,16,2560]{2,1,0:T(8,128)(2,1)S(1)} %get-tuple-element.68.refs_2_.refs_0_, bf16[16,2560]{1,0:T(8,128)(2,1)S(1)} %collective-permute-done.refs_3_.refs_1_, bf16[2,48,2560]{2,1,0:T(8,128)(2,1)S(1)} %constant_dynamic-update-slice_fusion.refs_2_, bf16[48,2560]{1,0:T(8,128)(2,1)S(1)} %collective-permute-done.6.refs_3_), custom_call_target="tpu_custom_call" | custom-call | tf_op jit(solution)/shard_map/pallas_call | solution.py:528
  35.0 0.0 collective-permute-done.8.refs_1_
  35.0 1.1 %collective-permute-done.10.refs_3_ = bf16[112,256]{1,0:T(8,128)(2,1)S(1)} collective-permute-done((bf16[112,256]{1,0:T(8,128)(2,1)S(1)}, bf16[112,256]{1,0:T(8,128)(2,1)S(1)}, u32[]{:S(2)}, u32[]{:S(2)}) %collective-permute-start.10) | collective-permute-done | bytes 57376 | tf_op jit(solution)/shard_map/ppermute | solution.py:542
  36.1 0.6 %collective-permute-done.9.refs_2_ = bf16[112,256]{1,0:T(8,128)(2,1)S(1)} collective-permute-done((bf16[112,256]{1,0:T(8,128)(2,1)S(1)}, bf16[112,256]{1,0:T(8,128)(2,1)S(1)}, u32[]{:S(2)}, u32[]{:S(2)}) %collective-permute-start.9) | collective-permute-done | bytes 57376 | tf_op jit(solution)/shard_map/ppermute | solution.py:542
  36.7 0.1 collective-permute-start.11
  36.8 1.5 %collective-permute-done.11.refs_4_ = bf16[448,256]{1,0:T(8,128)(2,1)S(1)} collective-permute-done((bf16[448,256]{1,0:T(8,128)(2,1)S(1)}, bf16[448,256]{1,0:T(8,128)(2,1)S(1)}, u32[]{:S(2)}, u32[]{:S(2)}) %collective-permute-start.11) | collective-permute-done | bytes 229408 | tf_op jit(solution)/shard_map/ppermute | solution.py:542
  38.3 1.0 %shard_map.221 = (f32[256,256]{1,0:T(8,128)}, f32[256,256]{1,0:T(8,128)}, f32[256,256]{1,0:T(8,128)}, f32[3,256]{1,0:T(4,128)}, f32[3,256]{1,0:T(4,128)}, /*index=5*/f32[8,256]{1,0:T(8,128)}, f32[12,192]{1,0:T(8,128)}) custom-call(s32[1]{0:T(128)S(6)} %and.10.refs_0_.side_ref, s32[1]{0:T(128)} %bitcast.4.refs_1_.quarter_ref, ...), custom_call_target="tpu_custom_call" | custom-call | tf_op jit(solution)/shard_map/pallas_call | solution.py:494
  (9 shorter events, 0.1 us)
Async XLA Ops:
  3.1 3.8 %collective-permute-start = (bf16[16,2560]{1,0:T(8,128)(2,1)S(1)}, bf16[16,2560]{1,0:T(8,128)(2,1)S(1)}, u32[]{:S(2)}, u32[]{:S(2)}) collective-permute-start(bf16[16,2560]{1,0:T(8,128)(2,1)S(1)} %slice_bitcast_fusion.1), channel_id=1, source_target_pairs={{0,16},{16,0},{1,17},{17,1},{2,18},{18,2},{3,19},{19,3},{4,20},{20... | collective-permute-start | bytes 245768 | tf_op jit(solution)/shard_map/ppermute | solution.py:593
  10.1 1.6 %collective-permute-start.1 = (bf16[4,112,256]{2,1,0:T(8,128)(2,1)S(1)}, bf16[4,112,256]{2,1,0:T(8,128)(2,1)S(1)}, u32[]{:S(2)}, u32[]{:S(2)}) collective-permute-start(bf16[4,112,256]{2,1,0:T(8,128)(2,1)S(1)} %get-tuple-element.94), channel_id=1, source_target_pairs={{0,16},{1,17},{2,18},{3,19},{4,20},{5,21},{6,22},{7,23},{8,24},{9,... | collective-permute-start | bytes 688136 | tf_op jit(solution)/shard_map/ppermute | solution.py:542
  11.7 7.0 %collective-permute-start.2 = (bf16[112,256]{1,0:T(8,128)(2,1)S(1)}, bf16[112,256]{1,0:T(8,128)(2,1)S(1)}, u32[]{:S(2)}, u32[]{:S(2)}) collective-permute-start(bf16[112,256]{1,0:T(8,128)(2,1)S(1)} %get-tuple-element.128), channel_id=1, source_target_pairs={{0,1},{1,0},{2,3},{3,2},{4,5},{5,4},{6,7},{7,6},{8,9},{9,8},{10,11... | collective-permute-start | bytes 172040 | tf_op jit(solution)/shard_map/ppermute | solution.py:542
  14.4 4.3 %collective-permute-start.3 = (bf16[112,256]{1,0:T(8,128)(2,1)S(1)}, bf16[112,256]{1,0:T(8,128)(2,1)S(1)}, u32[]{:S(2)}, u32[]{:S(2)}) collective-permute-start(bf16[112,256]{1,0:T(8,128)(2,1)S(1)} %get-tuple-element.126), channel_id=1, source_target_pairs={{0,2},{1,3},{2,0},{3,1},{4,6},{5,7},{6,4},{7,5},{8,10},{9,11},{10,... | collective-permute-start | bytes 172040 | tf_op jit(solution)/shard_map/ppermute | solution.py:542
  15.9 5.1 %collective-permute-start.4 = (bf16[112,256]{1,0:T(8,128)(2,1)S(1)}, bf16[112,256]{1,0:T(8,128)(2,1)S(1)}, u32[]{:S(2)}, u32[]{:S(2)}) collective-permute-start(bf16[112,256]{1,0:T(8,128)(2,1)S(1)} %get-tuple-element.127), channel_id=1, source_target_pairs={{0,3},{1,2},{2,1},{3,0},{4,7},{5,6},{6,5},{7,4},{8,11},{9,10},{10,... | collective-permute-start | bytes 172040 | tf_op jit(solution)/shard_map/ppermute | solution.py:542
  21.0 4.2 %collective-permute-start.5 = (bf16[112,256]{1,0:T(8,128)(2,1)S(1)}, bf16[112,256]{1,0:T(8,128)(2,1)S(1)}, u32[]{:S(2)}, u32[]{:S(2)}) collective-permute-start(bf16[112,256]{1,0:T(8,128)(2,1)S(1)} %add_convert_fusion.2), channel_id=1, source_target_pairs={{0,4},{1,5},{2,6},{3,7},{4,0},{5,1},{6,2},{7,3},{8,12},{9,13},{10,... | collective-permute-start | bytes 172040 | tf_op jit(solution)/shard_map/ppermute | solution.py:542
  25.3 5.1 %collective-permute-start.7 = (bf16[112,256]{1,0:T(8,128)(2,1)S(1)}, bf16[112,256]{1,0:T(8,128)(2,1)S(1)}, u32[]{:S(2)}, u32[]{:S(2)}) collective-permute-start(bf16[112,256]{1,0:T(8,128)(2,1)S(1)} %add_convert_fusion.1), channel_id=1, source_target_pairs={{0,8},{1,9},{2,10},{3,11},{4,12},{5,13},{6,14},{7,15},{8,0},{9,1},... | collective-permute-start | bytes 172040 | tf_op jit(solution)/shard_map/ppermute | solution.py:542
  28.0 6.0 %collective-permute-start.6 = (bf16[48,2560]{1,0:T(8,128)(2,1)S(1)}, bf16[48,2560]{1,0:T(8,128)(2,1)S(1)}, u32[]{:S(2)}, u32[]{:S(2)}) collective-permute-start(bf16[48,2560]{1,0:T(8,128)(2,1)S(1)} %slice_bitcast_fusion), channel_id=1, source_target_pairs={{0,16},{16,0},{1,17},{17,1},{2,18},{18,2},{3,19},{19,3},{4,20},{20... | collective-permute-start | bytes 737288 | tf_op jit(solution)/shard_map/ppermute | solution.py:593
  30.4 4.5 %collective-permute-start.8 = (bf16[112,256]{1,0:T(8,128)(2,1)S(1)}, bf16[112,256]{1,0:T(8,128)(2,1)S(1)}, u32[]{:S(2)}, u32[]{:S(2)}) collective-permute-start(bf16[112,256]{1,0:T(8,128)(2,1)S(1)} %add_convert_fusion.refs_0_), channel_id=1, source_target_pairs={{0,1},{1,0},{2,3},{3,2},{4,5},{5,4},{6,7},{7,6},{8,9},{9,8},{10,11... | collective-permute-start | bytes 172040 | tf_op jit(solution)/shard_map/ppermute | solution.py:542
  31.0 5.1 %collective-permute-start.10 = (bf16[112,256]{1,0:T(8,128)(2,1)S(1)}, bf16[112,256]{1,0:T(8,128)(2,1)S(1)}, u32[]{:S(2)}, u32[]{:S(2)}) collective-permute-start(bf16[112,256]{1,0:T(8,128)(2,1)S(1)} %add_convert_fusion.refs_0_), channel_id=1, source_target_pairs={{0,3},{1,2},{2,1},{3,0},{4,7},{5,6},{6,5},{7,4},{8,11},{9,10},{10,... | collective-permute-start | bytes 172040 | tf_op jit(solution)/shard_map/ppermute | solution.py:542
  32.5 4.2 %collective-permute-start.9 = (bf16[112,256]{1,0:T(8,128)(2,1)S(1)}, bf16[112,256]{1,0:T(8,128)(2,1)S(1)}, u32[]{:S(2)}, u32[]{:S(2)}) collective-permute-start(bf16[112,256]{1,0:T(8,128)(2,1)S(1)} %add_convert_fusion.refs_0_), channel_id=1, source_target_pairs={{0,2},{1,3},{2,0},{3,1},{4,6},{5,7},{6,4},{7,5},{8,10},{9,11},{10,... | collective-permute-start | bytes 172040 | tf_op jit(solution)/shard_map/ppermute | solution.py:542
  36.7 1.6 %collective-permute-start.11 = (bf16[448,256]{1,0:T(8,128)(2,1)S(1)}, bf16[448,256]{1,0:T(8,128)(2,1)S(1)}, u32[]{:S(2)}, u32[]{:S(2)}) collective-permute-start(bf16[448,256]{1,0:T(8,128)(2,1)S(1)} %pad_maximum_fusion), channel_id=1, source_target_pairs={{0,16},{1,17},{2,18},{3,19},{4,20},{5,21},{6,22},{7,23},{8,24},{9,... | collective-permute-start | bytes 688136 | tf_op jit(solution)/shard_map/ppermute | solution.py:542

commit v6 on v5

--- a/solution.py
+++ b/solution.py
@@ -13,6 +13,8 @@
 AXES = ("view", "gauss")
 LOW = 256
 GROUP = 16
+BAND = 32
+SMALL = 8
 FAN = 4
 NT = (((1,), (1,)), ((), ()))
 TN = (((0,), (0,)), ((), ()))
@@ -34,6 +36,11 @@
         if total % choice == 0:
             return choice
     return total
+
+
+def entry_step(entries, rows):
+    fitting = [step for step in (2560, 1280, 1024, 512, 256, 128) if rows * step * 2 <= 8 << 20]
+    return divisor(entries, fitting)
 
 
 def scatter_kernel(first_row, rows, viewers, view_ref, grads_ref, ids_ref, out_ref, acc_ref, left_ref):
@@ -88,7 +95,7 @@
 def scatter(view, entry_grads, vis_ids, first_row, rows, members, viewers):
     height = -(-rows // GROUP) * GROUP
     blocks = members * viewers // LOW
-    step = divisor(vis_ids.shape[1], (2560, 2048, 1024, 512, 256, 128))
+    step = entry_step(vis_ids.shape[1], blocks * height)
     return pl.pallas_call(
         functools.partial(scatter_kernel, first_row, rows, viewers),
         out_shape=jax.ShapeDtypeStruct((viewers, height, members), BF16),
@@ -99,28 +106,73 @@
     )(view, entry_grads, vis_ids)
 
 
+def position_kernel(viewers, view_ref, grads_ref, ids_ref, out_ref, acc_ref, left_ref, rows_ref):
+    entries = ids_ref.shape[1]
+    step = left_ref.shape[1]
+    height = left_ref.shape[0] // 3
+    blocks = out_ref.shape[2] * viewers // 128
+    per = blocks // viewers
+    high_rows = lax.broadcasted_iota(jnp.int32, (height, step), 0).astype(F32).astype(BF16)
+    low_rows = lax.broadcasted_iota(jnp.int32, (128, step), 0).astype(F32).astype(BF16)
+    one = jnp.ones((), BF16)
+    zero = jnp.zeros((), BF16)
+
+    def chunk(index, carry):
+        spot = pl.ds(pl.multiple_of(index * step, step), step)
+        ids = ids_ref[0:1, spot]
+        high = lax.shift_right_logical(ids, 7).astype(F32).astype(BF16)
+        low = lax.bitwise_and(ids, 127).astype(F32).astype(BF16)
+        hot = jnp.where(low_rows == low, one, zero)
+        inside = high_rows == high
+        values = grads_ref[0, :, spot].astype(F32)
+        for axis in range(3):
+            value = jnp.broadcast_to(values[axis : axis + 1], (height, step)).astype(BF16)
+            left_ref[axis * height : (axis + 1) * height, :] = jnp.where(inside, value, zero)
+        product = mm(left_ref[...], hot, NT)
+
+        @pl.when(index == 0)
+        def _():
+            acc_ref[...] = product
+
+        @pl.when(index != 0)
+        def _():
+            acc_ref[...] += product
+
+        return carry
+
+    lax.fori_loop(0, entries // step, chunk, 0)
+    rows_ref[...] = jnp.zeros_like(rows_ref)
+    for block in range(blocks):
+        slot = lax.rem(block // per - view_ref[0] + viewers, viewers)
+        lanes = slice(block % per * 128, (block % per + 1) * 128)
+        for axis in range(3):
+            place = axis * height + block
+            rows_ref[slot, axis : axis + 1, lanes] = acc_ref[place : place + 1, :]
+    out_ref[...] = rows_ref[...].astype(BF16)
+
+
 def entry_kernel(viewers, count, view_ref, *refs):
     sources, out_ref, targets = refs[:count], refs[count], refs[count + 1 : 2 * count + 1]
-    acc_ref, left_ref, rows_ref, sems = refs[2 * count + 1 :]
+    acc_ref, left_ref, rows_ref, grads_ref, sems = refs[2 * count + 1 :]
     copies = [
         pltpu.make_async_copy(source, target, sems.at[index])
         for index, (source, target) in enumerate(zip(sources, targets))
     ]
-    early = pltpu.make_async_copy(sources[1].at[:, 0:GROUP, :], rows_ref, sems.at[count])
+    early = pltpu.make_async_copy(sources[1].at[:, 0:GROUP, :], grads_ref, sems.at[count])
     copies[0].start()
     early.start()
     for copy in copies[1:]:
         copy.start()
     copies[0].wait()
     early.wait()
-    scatter_kernel(0, GROUP, viewers, view_ref, rows_ref, targets[0], out_ref, acc_ref, left_ref)
+    position_kernel(viewers, view_ref, grads_ref, targets[0], out_ref, acc_ref, left_ref, rows_ref)
     for copy in copies[1:]:
         copy.wait()
 
 
 def entry(view, arrays, members, viewers):
-    blocks = members * viewers // LOW
-    step = divisor(arrays[0].shape[1], (2560, 2048, 1024, 512, 256, 128))
+    height = -(-(members * viewers // 128) // 16) * 16
+    step = entry_step(arrays[0].shape[1], 3 * height)
     count = len(arrays)
     results = pl.pallas_call(
         functools.partial(entry_kernel, viewers, count),
@@ -131,8 +183,9 @@
         in_specs=[SMEM] + [HBM] * count,
         out_specs=(VMEM,) * (count + 1),
         scratch_shapes=[
-            pltpu.VMEM((blocks * GROUP, LOW), F32),
-            pltpu.VMEM((blocks * GROUP, step), BF16),
+            pltpu.VMEM((3 * height, 128), F32),
+            pltpu.VMEM((3 * height, step), BF16),
+            pltpu.VMEM((viewers, GROUP, members), F32),
             pltpu.VMEM((1, GROUP, arrays[0].shape[1]), BF16),
             pltpu.SemaphoreType.DMA((count + 1,)),
         ],
@@ -289,16 +342,22 @@
     )(feats, code, subj, bone_ids, skin, canon, table, w1, w2, w3, bias, head)
 
 
-def block_rows(width):
-    return -(-(3 * width + 48) // (2 * FAN * 16)) * 16
+def block_pieces(width):
+    piece = width // (2 * FAN)
+    return piece, 3 * piece + SMALL
 
 
 def split_blocks(side, quarter, total_s, mine_out, theirs_out, factor):
-    rows = mine_out.shape[1]
+    width = mine_out.shape[2]
+    piece, rows = block_pieces(width)
     for core, out in ((side, mine_out), (1 - side, theirs_out)):
         for slot in range(FAN):
-            place = (core * FAN + lax.bitwise_xor(quarter, slot)) * rows
-            out[slot] = (total_s[pl.ds(pl.multiple_of(place, 16), rows), :] * factor).astype(BF16)
+            place = core * FAN + lax.bitwise_xor(quarter, slot)
+            for square in range(3):
+                spot = pl.ds(pl.multiple_of(square * width + place * piece, 16), piece)
+                out[slot, square * piece : (square + 1) * piece, :] = (total_s[spot, :] * factor).astype(BF16)
+            spot = pl.ds(pl.multiple_of(3 * width + place * SMALL, SMALL), SMALL)
+            out[slot, 3 * piece : rows, :] = (total_s[spot, :] * factor).astype(BF16)
 
 
 def lane_sums(value):
@@ -372,7 +431,7 @@
     product = mm(masked_s[...], bone_ref[...], NT)
     for s in range(subjects):
         columns = slice(s * per_subject, (s + 1) * per_subject)
-        total_s[small + 16 : small + 32, columns] = product[16 * s : 16 * s + 16, 0:per_subject]
+        total_s[small + 8 : small + 24, columns] = product[16 * s : 16 * s + 16, 0:per_subject]
 
     half = jnp.asarray(0.5, BF16)
     back = mm(head_w * half, shift, TN) * slope_three_ref[...]
@@ -394,7 +453,7 @@
     by_mid, by_lo = two_parts(by_rest)
     by_parts = jnp.concatenate([by_hi.astype(F32), by_mid.astype(F32), by_lo], axis=0).astype(BF16)
     code = mm(by_parts, first_ref[...])
-    total_s[small + 32 : small + 32 + subjects, :] = (
+    total_s[small + 24 : small + 24 + subjects, :] = (
         code[0:subjects] + code[subjects : 2 * subjects] + code[2 * subjects : 3 * subjects]
     )
 
@@ -404,7 +463,7 @@
 def backward(side, quarter, pos, got, forwarded, subj, weights, head, factor, subjects, per_subject):
     inputs, act_one, act_two, act_three, *slopes, point, _, blend, bone = forwarded
     width, members = act_one.shape
-    rows = block_rows(width)
+    piece, rows = block_pieces(width)
     part = jax.ShapeDtypeStruct((FAN, rows, width), BF16)
     return pl.pallas_call(
         functools.partial(backward_kernel, factor, subjects, per_subject, len(got)),
@@ -417,7 +476,7 @@
         in_specs=[SMEM] * 2 + [VMEM] * (16 + len(got)),
         out_specs=(VMEM,) * 4,
         scratch_shapes=[
-            pltpu.VMEM((2 * FAN * rows, width), F32),
+            pltpu.VMEM((3 * width + 2 * FAN * SMALL, width), F32),
             pltpu.VMEM((16, width), F32),
             pltpu.VMEM((16 * subjects, members), BF16),
         ],
@@ -465,33 +524,30 @@
 
 def finish_kernel(side_ref, quarter_ref, *refs):
     mine_refs, refs = refs[:FAN], refs[FAN:]
-    theirs_ref, first_out, second_out, third_out, bias_out, head_out, code_out, bone_out, total_s = refs
-    width = third_out.shape[0]
-    table_cols = bone_out.shape[1]
-    subjects = code_out.shape[0]
-    rows = mine_refs[0].shape[0]
-    side = side_ref[0]
-    for slot in range(FAN):
-        place = lax.bitwise_xor(quarter_ref[0], slot)
-        mine = pl.multiple_of((side * FAN + place) * rows, 16)
-        theirs = pl.multiple_of(((1 - side) * FAN + place) * rows, 16)
-        total_s[pl.ds(mine, rows), :] = mine_refs[slot][...].astype(F32)
-        total_s[pl.ds(theirs, rows), :] = theirs_ref[slot * rows : (slot + 1) * rows, :].astype(F32)
-    third_out[...] = total_s[0:width, :]
-    second_out[...] = total_s[width : 2 * width, :]
-    first_out[...] = total_s[2 * width : 3 * width, :]
-    small = total_s[3 * width : 3 * width + 48, :]
+    theirs_ref, *square_outs, bias_out, head_out, code_out, bone_out, small_s = refs
+    piece, rows = block_pieces(theirs_ref.shape[1])
+    for core in range(2):
+        owner = side_ref[0] if core == 0 else 1 - side_ref[0]
+        for slot in range(FAN):
+            block = mine_refs[slot] if core == 0 else theirs_ref.at[slot * rows : (slot + 1) * rows]
+            place = owner * FAN + lax.bitwise_xor(quarter_ref[0], slot)
+            spot = pl.ds(pl.multiple_of(place * piece, piece), piece)
+            for square, out in enumerate(square_outs):
+                out[spot, :] = block[square * piece : (square + 1) * piece, :].astype(F32)
+            spot = pl.ds(pl.multiple_of(place * SMALL, SMALL), SMALL)
+            small_s[spot, :] = block[3 * piece : rows, :].astype(F32)
+    small = small_s[...]
     head_out[...] = small[0:3]
     bias_out[...] = small[3:6]
-    bone_out[...] = small[16:28, 0:table_cols]
-    code_out[...] = small[32 : 32 + subjects]
+    bone_out[...] = small[8:20, 0 : bone_out.shape[1]]
+    code_out[...] = small[24 : 24 + code_out.shape[0]]
 
 
 def finish(side, quarter, mine, theirs, subjects, table_cols):
-    rows, width = mine[0].shape
+    width = mine[0].shape[1]
     square = jax.ShapeDtypeStruct((width, width), F32)
     lines = jax.ShapeDtypeStruct((3, width), F32)
-    return pl.pallas_call(
+    third, second, first, *small = pl.pallas_call(
         finish_kernel,
         out_shape=(
             square,
@@ -504,34 +560,35 @@
         ),
         in_specs=[SMEM] * 2 + [VMEM] * (FAN + 1),
         out_specs=(VMEM,) * 7,
-        scratch_shapes=[pltpu.VMEM((2 * FAN * rows, width), F32)],
+        scratch_shapes=[pltpu.VMEM((2 * FAN * SMALL, width), F32)],
         compiler_params=params(16),
     )(side, quarter, *mine, theirs)
-
-
-def attr_kernel(count, *refs):
+    return first, second, third, *small
+
+
+def attr_kernel(groups, *refs):
     out_ref = refs[-1]
-    attrs = out_ref.shape[0]
+    count = (len(refs) - 1) // groups
     row = 0
-    for start in (0, count):
+    for start in range(0, groups * count, count):
         total = refs[start][0].astype(F32)
         for ref in refs[start + 1 : start + count]:
             total = total + ref[...].astype(F32)
-        for place in range(min(total.shape[0], attrs - row)):
+        for place in range(min(total.shape[0], out_ref.shape[0] - row)):
             out_ref[row + place] = total[place : place + 1]
         row += total.shape[0]
 
 
-def attr_sum(position, position_got, others, others_got, attrs):
-    members = position.shape[2]
-    count = 1 + len(position_got)
+def attr_sum(groups, attrs):
+    members = groups[0][0].shape[2]
+    operands = [value for group in groups for value in group]
     return pl.pallas_call(
-        functools.partial(attr_kernel, count),
+        functools.partial(attr_kernel, len(groups)),
         out_shape=jax.ShapeDtypeStruct((attrs, 1, members), F32),
-        in_specs=[VMEM] * (2 * count),
+        in_specs=[VMEM] * len(operands),
         out_specs=VMEM,
         compiler_params=params(16),
-    )(position, *position_got, others, *others_got)
+    )(*operands)
 
 
 def add(left, right):
@@ -661,20 +718,19 @@
 
     def scatter_rows(row):
         def call(grads, ids):
-            return [scatter(view, grads, ids, row, min(GROUP, attrs - row), members, viewers)]
+            return [scatter(view, grads, ids, row, min(BAND, attrs - row), members, viewers)]
 
         return Work(call, entry_grads, vis_ids)
 
-    works = [scatter_rows(row) for row in range(GROUP, attrs, GROUP)]
+    works = [scatter_rows(row) for row in range(0, attrs, BAND)]
     per_gaussian = Work(gaussian_grads, back_one, weights[0], outer, forwarded[8])
 
     def attributes(_):
-        others = jnp.concatenate([work.results[0] for work in works], axis=1)
-        others_got = received(others, viewers)
-        return [attr_sum(position, position_got, others, others_got, attrs)]
+        sums = [work.results[0] for work in works]
+        return [attr_sum([[value, *received(value, viewers)] for value in sums], attrs)]
 
     last = Work(attributes, view)
-    between = {"scatter": works[:2], 0: works[2:], 1: [per_gaussian], "gather": [last]}
+    between = {"scatter": works[:1], 0: works[1:], 1: [per_gaussian], "gather": [last]}
     mine, theirs = sum_over_devices(mine, theirs, viewers, shards, between)
     attr = last.results[0]
     feat_grads, skin_grads = per_gaussian.results

time: 39.4 us -> 38.9 us (0.987)
  waiting for transfers between devices: 8.99 us -> 8.51 us
    pallas_call x1, Pallas kernels: 2.45 us -> 1.96 us  [entry(): pl.pallas_call(functools.partial(entry_kernel, viewers, count), out_shape...]
    ppermute x10, waiting for transfers between devices: 8.99 us -> 8.5 us  [swap(): lax.ppermute(value, AXES, [(place, place ^ mask) for place in range(count)])]
    pallas_call x3 -> x2, Pallas kernels: 4.02 us -> 4.51 us  [scatter(): pl.pallas_call(functools.partial(scatter_kernel, first_row, rows, viewers...]
  transfers between devices with their start and end apart: 12 -> 13, of which waited for: 7 -> 8; matrix products, arithmetic and copies ran while one was open for 0% -> 0% of each run, Pallas kernels for 25% -> 27%
where the time goes in v6:
time: 38.9 us; the launch traced here: 38.8 us
  Pallas kernels  16.3 us (42%)
  starting transfers between devices  13 us (33%)
  waiting for transfers between devices  8.51 us (22%)
  between operations  0.75 us (2%)
    ppermute x10, starting transfers between devices, swap(): lax.ppermute(value, AXES, [(place, place ^ mask) for place in range(count)])  12.3 us
    ppermute x10, waiting for transfers between devices, swap(): lax.ppermute(value, AXES, [(place, place ^ mask) for place in range(count)])  8.5 us
    pallas_call x2, Pallas kernels, scatter(): pl.pallas_call(functools.partial(scatter_kernel, first_row, rows, viewers...  4.51 us
    pallas_call x1, Pallas kernels, forward(): pl.pallas_call(forward_kernel, out_shape=(jax.ShapeDtypeStruct((width + 1...  3.24 us
    pallas_call x1, Pallas kernels, backward(): pl.pallas_call(functools.partial(backward_kernel, factor, subjects, per_s...  3.16 us
    pallas_call x1, Pallas kernels, entry(): pl.pallas_call(functools.partial(entry_kernel, viewers, count), out_shape...  1.96 us
    pallas_call x1, Pallas kernels, gaussian_grads(): pl.pallas_call(gaussian_kernel, out_shape=(jax.ShapeDtypeStruct((width, m...  1.6 us
    pallas_call x1, Pallas kernels, attr_sum(): pl.pallas_call(functools.partial(attr_kernel, len(groups)), out_shape=jax...  0.99 us
  transfers between devices with their start and end apart: 13, of which 8 were waited for; matrix products, arithmetic and copies ran while one was open for 0% of the time, Pallas kernels for 27%

profile of v6, /device:TPU:0, one launch (start us, length us, event | category | flops | bytes accessed | tf_op | source)
XLA Modules:
  0.0 38.8 jit_solution(17879015770541032178)
XLA Ops:
  0.7 2.0 %shard_map.213 = (bf16[2,16,2560]{2,1,0:T(8,128)(2,1)S(1)}, s32[1,5120]{1,0:T(1,128)S(1)}, bf16[1,59,5120]{2,1,0:T(8,128)(2,1)S(1)}, bf16[256,2560]{1,0:T(8,128)...) custom-call(s32[1]{0:T(128)} %bitcast.view_ref, ...), custom_call_target="tpu_custom_call" | custom-call | tf_op jit(solution)/shard_map/pallas_call | solution.py:177
  2.6 0.5 %collective-permute-start = (bf16[16,2560]{1,0:T(8,128)(2,1)S(1)}, bf16[16,2560]{1,0:T(8,128)(2,1)S(1)}, u32[]{:S(2)}, u32[]{:S(2)}) collective-permute-start(bf16[16,2560]{1,0:T(8,128)(2,1)S(1)} %slice_bitcast_fusion.2), channel_id=1, source_target_pairs={{0,16},{16,0},{1,17},{17,1},{2,18},{18,2},{3,19},{19,3},{4,20},{20... | collective-permute-start | bytes 245768 | tf_op jit(solution)/shard_map/ppermute | solution.py:650
  3.2 3.2 %shard_map.214 = (bf16[272,2560]{1,0:T(8,128)(2,1)S(1)}, bf16[256,2560]{1,0:T(8,128)(2,1)S(1)}, bf16[256,2560]{1,0:T(8,128)(2,1)S(1)}, bf16[256,2560]{1,0:T(8,12...) custom-call(bf16[256,2560]{1,0:T(8,128)(2,1)S(1)} %get-tuple-element, ...), custom_call_target="tpu_custom_call" | custom-call | tf_op jit(solution)/shard_map/pallas_call | solution.py:319
  6.4 0.0 collective-permute-done.refs_3_
  6.4 3.2 %shard_map.215 = (f32[16,2560]{1,0:T(8,128)S(1)}, bf16[256,2560]{1,0:T(8,128)(2,1)S(1)}, bf16[4,104,256]{2,1,0:T(8,128)(2,1)S(1)}, bf16[4,104,256]{2,1,0:T(8,128)(2,1)S(1)}) custom-call(s32[1]{0:T(128)S(6)} %and.10.refs_0_.side_ref, s32[1]{0:T(128)} %bitcast.3.refs_1_.quarter_ref, bf16[2,16,2560]{2,1,0:T(8,128)(2,1)S(1)} %get-tuple-element.68.refs_2_, ...), custom_call_target="tpu_custom_call" | custom-call | tf_op jit(solution)/shard_map/pallas_call | solution.py:468
  9.6 0.1 collective-permute-start.1
  9.7 1.4 %collective-permute-done.1 = bf16[4,104,256]{2,1,0:T(8,128)(2,1)S(1)} collective-permute-done((bf16[4,104,256]{2,1,0:T(8,128)(2,1)S(1)}, bf16[4,104,256]{2,1,0:T(8,128)(2,1)S(1)}, u32[]{:S(2)}, u32[]{:S(2)}) %collective-permute-start.1) | collective-permute-done | bytes 213024 | tf_op jit(solution)/shard_map/ppermute | solution.py:599
  11.1 0.1 fusion.2
  11.1 2.7 %collective-permute-start.2 = (bf16[104,256]{1,0:T(8,128)(2,1)S(1)}, bf16[104,256]{1,0:T(8,128)(2,1)S(1)}, u32[]{:S(2)}, u32[]{:S(2)}) collective-permute-start(bf16[104,256]{1,0:T(8,128)(2,1)S(1)} %get-tuple-element.124), channel_id=1, source_target_pairs={{0,1},{1,0},{2,3},{3,2},{4,5},{5,4},{6,7},{7,6},{8,9},{9,8},{10,11... | collective-permute-start | bytes 159752 | tf_op jit(solution)/shard_map/ppermute | solution.py:599
  13.8 1.5 %collective-permute-start.4 = (bf16[104,256]{1,0:T(8,128)(2,1)S(1)}, bf16[104,256]{1,0:T(8,128)(2,1)S(1)}, u32[]{:S(2)}, u32[]{:S(2)}) collective-permute-start(bf16[104,256]{1,0:T(8,128)(2,1)S(1)} %get-tuple-element.122), channel_id=1, source_target_pairs={{0,2},{1,3},{2,0},{3,1},{4,6},{5,7},{6,4},{7,5},{8,10},{9,11},{10,... | collective-permute-start | bytes 159752 | tf_op jit(solution)/shard_map/ppermute | solution.py:599
  15.3 0.0 collective-permute-start.5
  15.4 2.3 %shard_map.216.refs_0_ = bf16[2,32,2560]{2,1,0:T(8,128)(2,1)S(1)} custom-call(s32[1]{0:T(128)} %bitcast.view_ref, bf16[1,59,5120]{2,1,0:T(8,128)(2,1)S(1)} %get-tuple-element.97.grads_ref, s32[1,5120]{1,0:T(1,128)S(1)} %get-tuple-element.98.ids_ref), custom_call_target="tpu_custom_call" | custom-call | tf_op jit(solution)/shard_map/pallas_call | solution.py:99
  17.6 0.0 collective-permute-done.2
  17.7 0.3 collective-permute-done.4
  18.0 2.4 %collective-permute-done.5 = bf16[104,256]{1,0:T(8,128)(2,1)S(1)} collective-permute-done((bf16[104,256]{1,0:T(8,128)(2,1)S(1)}, bf16[104,256]{1,0:T(8,128)(2,1)S(1)}, u32[]{:S(2)}, u32[]{:S(2)}) %collective-permute-start.5) | collective-permute-done | bytes 53280 | tf_op jit(solution)/shard_map/ppermute | solution.py:599
  20.4 1.7 %collective-permute-start.6 = (bf16[104,256]{1,0:T(8,128)(2,1)S(1)}, bf16[104,256]{1,0:T(8,128)(2,1)S(1)}, u32[]{:S(2)}, u32[]{:S(2)}) collective-permute-start(bf16[104,256]{1,0:T(8,128)(2,1)S(1)} %add_convert_fusion.2), channel_id=1, source_target_pairs={{0,4},{1,5},{2,6},{3,7},{4,0},{5,1},{6,2},{7,3},{8,12},{9,13},{10,... | collective-permute-start | bytes 159752 | tf_op jit(solution)/shard_map/ppermute | solution.py:599
  22.1 0.1 collective-permute-start.3
  22.2 2.3 %shard_map.217.refs_2_ = bf16[2,32,2560]{2,1,0:T(8,128)(2,1)S(1)} custom-call(s32[1]{0:T(128)} %bitcast.view_ref, bf16[1,59,5120]{2,1,0:T(8,128)(2,1)S(1)} %get-tuple-element.97.grads_ref, s32[1,5120]{1,0:T(1,128)S(1)} %get-tuple-element.98.ids_ref), custom_call_target="tpu_custom_call" | custom-call | tf_op jit(solution)/shard_map/pallas_call | solution.py:99
  24.4 0.2 collective-permute-done.6
  24.6 2.7 %collective-permute-start.8 = (bf16[104,256]{1,0:T(8,128)(2,1)S(1)}, bf16[104,256]{1,0:T(8,128)(2,1)S(1)}, u32[]{:S(2)}, u32[]{:S(2)}) collective-permute-start(bf16[104,256]{1,0:T(8,128)(2,1)S(1)} %add_convert_fusion.1), channel_id=1, source_target_pairs={{0,8},{1,9},{2,10},{3,11},{4,12},{5,13},{6,14},{7,15},{8,0},{9,1},... | collective-permute-start | bytes 159752 | tf_op jit(solution)/shard_map/ppermute | solution.py:599
  27.3 0.1 collective-permute-start.7
  27.4 1.6 %shard_map.219 = (bf16[256,2560]{1,0:T(8,128)(2,1)}, f32[4,1,2560]{2,1,0:T(1,128)}) custom-call(bf16[256,2560]{1,0:T(8,128)(2,1)S(1)} %get-tuple-element.104.back_ref, bf16[256,256]{1,0:T(8,128)(2,1)S(1)} %get-tuple-element.105.first_ref.refs_15_, f32[16,2560]{1,0:T(8,128)S(1)} %get-tuple-element.106.outer_ref, f32[4,16,2560]{2,1,0:T(8,128)S(1)} %get-tuple-element.107.matrix_ref), custom_call_target="tpu_custom_call" | custom-call | tf_op jit(solution)/shard_map/pallas_call | solution.py:513
  29.0 1.1 %collective-permute-done.8 = bf16[104,256]{1,0:T(8,128)(2,1)S(1)} collective-permute-done((bf16[104,256]{1,0:T(8,128)(2,1)S(1)}, bf16[104,256]{1,0:T(8,128)(2,1)S(1)}, u32[]{:S(2)}, u32[]{:S(2)}) %collective-permute-start.8) | collective-permute-done | bytes 53280 | tf_op jit(solution)/shard_map/ppermute | solution.py:599
  30.1 0.6 %collective-permute-start.9 = (bf16[104,256]{1,0:T(8,128)(2,1)S(1)}, bf16[104,256]{1,0:T(8,128)(2,1)S(1)}, u32[]{:S(2)}, u32[]{:S(2)}) collective-permute-start(bf16[104,256]{1,0:T(8,128)(2,1)S(1)} %add_convert_fusion.refs_0_), channel_id=1, source_target_pairs={{0,1},{1,0},{2,3},{3,2},{4,5},{5,4},{6,7},{7,6},{8,9},{9,8},{10,11... | collective-permute-start | bytes 159752 | tf_op jit(solution)/shard_map/ppermute | solution.py:599
  30.7 1.4 %collective-permute-start.11 = (bf16[104,256]{1,0:T(8,128)(2,1)S(1)}, bf16[104,256]{1,0:T(8,128)(2,1)S(1)}, u32[]{:S(2)}, u32[]{:S(2)}) collective-permute-start(bf16[104,256]{1,0:T(8,128)(2,1)S(1)} %add_convert_fusion.refs_0_), channel_id=1, source_target_pairs={{0,3},{1,2},{2,1},{3,0},{4,7},{5,6},{6,5},{7,4},{8,11},{9,10},{10,... | collective-permute-start | bytes 159752 | tf_op jit(solution)/shard_map/ppermute | solution.py:599
  32.2 1.5 %collective-permute-start.10 = (bf16[104,256]{1,0:T(8,128)(2,1)S(1)}, bf16[104,256]{1,0:T(8,128)(2,1)S(1)}, u32[]{:S(2)}, u32[]{:S(2)}) collective-permute-start(bf16[104,256]{1,0:T(8,128)(2,1)S(1)} %add_convert_fusion.refs_0_), channel_id=1, source_target_pairs={{0,2},{1,3},{2,0},{3,1},{4,6},{5,7},{6,4},{7,5},{8,10},{9,11},{10,... | collective-permute-start | bytes 159752 | tf_op jit(solution)/shard_map/ppermute | solution.py:599
  33.7 0.0 collective-permute-done.3.refs_1_
  33.7 0.0 collective-permute-done.7.refs_3_
  33.7 1.0 %shard_map.218 = f32[59,1,2560]{2,1,0:T(1,128)} custom-call(bf16[2,32,2560]{2,1,0:T(8,128)(2,1)S(1)} %shard_map.216.refs_0_, bf16[32,2560]{1,0:T(8,128)(2,1)S(1)} %collective-permute-done.3.refs_1_, bf16[2,32,2560]{2,1,0:T(8,128)(2,1)S(1)} %shard_map.217.refs_2_, bf16[32,2560]{1,0:T(8,128)(2,1)S(1)} %collective-permute-done.7.refs_3_), custom_call_target="tpu_custom_call" | custom-call | tf_op jit(solution)/shard_map/pallas_call | solution.py:585
  34.7 0.0 collective-permute-done.9.refs_1_
  34.7 1.1 %collective-permute-done.11.refs_3_ = bf16[104,256]{1,0:T(8,128)(2,1)S(1)} collective-permute-done((bf16[104,256]{1,0:T(8,128)(2,1)S(1)}, bf16[104,256]{1,0:T(8,128)(2,1)S(1)}, u32[]{:S(2)}, u32[]{:S(2)}) %collective-permute-start.11) | collective-permute-done | bytes 53280 | tf_op jit(solution)/shard_map/ppermute | solution.py:599
  35.8 0.6 %collective-permute-done.10.refs_2_ = bf16[104,256]{1,0:T(8,128)(2,1)S(1)} collective-permute-done((bf16[104,256]{1,0:T(8,128)(2,1)S(1)}, bf16[104,256]{1,0:T(8,128)(2,1)S(1)}, u32[]{:S(2)}, u32[]{:S(2)}) %collective-permute-start.10) | collective-permute-done | bytes 53280 | tf_op jit(solution)/shard_map/ppermute | solution.py:599
  36.4 0.1 collective-permute-start.12
  36.4 1.5 %collective-permute-done.12.refs_4_ = bf16[416,256]{1,0:T(8,128)(2,1)S(1)} collective-permute-done((bf16[416,256]{1,0:T(8,128)(2,1)S(1)}, bf16[416,256]{1,0:T(8,128)(2,1)S(1)}, u32[]{:S(2)}, u32[]{:S(2)}) %collective-permute-start.12) | collective-permute-done | bytes 213024 | tf_op jit(solution)/shard_map/ppermute | solution.py:599
  37.9 0.9 %shard_map.220 = (f32[256,256]{1,0:T(8,128)}, f32[256,256]{1,0:T(8,128)}, f32[256,256]{1,0:T(8,128)}, f32[3,256]{1,0:T(4,128)}, f32[3,256]{1,0:T(4,128)}, /*index=5*/f32[8,256]{1,0:T(8,128)}, f32[12,192]{1,0:T(8,128)}) custom-call(s32[1]{0:T(128)S(6)} %and.10.refs_0_.side_ref, s32[1]{0:T(128)} %bitcast.3.refs_1_.quarter_ref, ...), custom_call_target="tpu_custom_call" | custom-call | tf_op jit(solution)/shard_map/pallas_call | solution.py:550
  (7 shorter events, 0.1 us)
Async XLA Ops:
  2.6 3.8 %collective-permute-start = (bf16[16,2560]{1,0:T(8,128)(2,1)S(1)}, bf16[16,2560]{1,0:T(8,128)(2,1)S(1)}, u32[]{:S(2)}, u32[]{:S(2)}) collective-permute-start(bf16[16,2560]{1,0:T(8,128)(2,1)S(1)} %slice_bitcast_fusion.2), channel_id=1, source_target_pairs={{0,16},{16,0},{1,17},{17,1},{2,18},{18,2},{3,19},{19,3},{4,20},{20... | collective-permute-start | bytes 245768 | tf_op jit(solution)/shard_map/ppermute | solution.py:650
  9.6 1.5 %collective-permute-start.1 = (bf16[4,104,256]{2,1,0:T(8,128)(2,1)S(1)}, bf16[4,104,256]{2,1,0:T(8,128)(2,1)S(1)}, u32[]{:S(2)}, u32[]{:S(2)}) collective-permute-start(bf16[4,104,256]{2,1,0:T(8,128)(2,1)S(1)} %get-tuple-element.92), channel_id=1, source_target_pairs={{0,16},{1,17},{2,18},{3,19},{4,20},{5,21},{6,22},{7,23},{8,24},{9,... | collective-permute-start | bytes 638984 | tf_op jit(solution)/shard_map/ppermute | solution.py:599
  11.1 6.5 %collective-permute-start.2 = (bf16[104,256]{1,0:T(8,128)(2,1)S(1)}, bf16[104,256]{1,0:T(8,128)(2,1)S(1)}, u32[]{:S(2)}, u32[]{:S(2)}) collective-permute-start(bf16[104,256]{1,0:T(8,128)(2,1)S(1)} %get-tuple-element.124), channel_id=1, source_target_pairs={{0,1},{1,0},{2,3},{3,2},{4,5},{5,4},{6,7},{7,6},{8,9},{9,8},{10,11... | collective-permute-start | bytes 159752 | tf_op jit(solution)/shard_map/ppermute | solution.py:599
  13.8 4.1 %collective-permute-start.4 = (bf16[104,256]{1,0:T(8,128)(2,1)S(1)}, bf16[104,256]{1,0:T(8,128)(2,1)S(1)}, u32[]{:S(2)}, u32[]{:S(2)}) collective-permute-start(bf16[104,256]{1,0:T(8,128)(2,1)S(1)} %get-tuple-element.122), channel_id=1, source_target_pairs={{0,2},{1,3},{2,0},{3,1},{4,6},{5,7},{6,4},{7,5},{8,10},{9,11},{10,... | collective-permute-start | bytes 159752 | tf_op jit(solution)/shard_map/ppermute | solution.py:599
  15.3 5.0 %collective-permute-start.5 = (bf16[104,256]{1,0:T(8,128)(2,1)S(1)}, bf16[104,256]{1,0:T(8,128)(2,1)S(1)}, u32[]{:S(2)}, u32[]{:S(2)}) collective-permute-start(bf16[104,256]{1,0:T(8,128)(2,1)S(1)} %get-tuple-element.123), channel_id=1, source_target_pairs={{0,3},{1,2},{2,1},{3,0},{4,7},{5,6},{6,5},{7,4},{8,11},{9,10},{10,... | collective-permute-start | bytes 159752 | tf_op jit(solution)/shard_map/ppermute | solution.py:599
  20.4 4.2 %collective-permute-start.6 = (bf16[104,256]{1,0:T(8,128)(2,1)S(1)}, bf16[104,256]{1,0:T(8,128)(2,1)S(1)}, u32[]{:S(2)}, u32[]{:S(2)}) collective-permute-start(bf16[104,256]{1,0:T(8,128)(2,1)S(1)} %add_convert_fusion.2), channel_id=1, source_target_pairs={{0,4},{1,5},{2,6},{3,7},{4,0},{5,1},{6,2},{7,3},{8,12},{9,13},{10,... | collective-permute-start | bytes 159752 | tf_op jit(solution)/shard_map/ppermute | solution.py:599
  22.1 11.6 %collective-permute-start.3 = (bf16[32,2560]{1,0:T(8,128)(2,1)S(1)}, bf16[32,2560]{1,0:T(8,128)(2,1)S(1)}, u32[]{:S(2)}, u32[]{:S(2)}) collective-permute-start(bf16[32,2560]{1,0:T(8,128)(2,1)S(1)} %slice_bitcast_fusion.1), channel_id=1, source_target_pairs={{0,16},{16,0},{1,17},{17,1},{2,18},{18,2},{3,19},{19,3},{4,20},{20... | collective-permute-start | bytes 491528 | tf_op jit(solution)/shard_map/ppermute | solution.py:650
  24.6 5.5 %collective-permute-start.8 = (bf16[104,256]{1,0:T(8,128)(2,1)S(1)}, bf16[104,256]{1,0:T(8,128)(2,1)S(1)}, u32[]{:S(2)}, u32[]{:S(2)}) collective-permute-start(bf16[104,256]{1,0:T(8,128)(2,1)S(1)} %add_convert_fusion.1), channel_id=1, source_target_pairs={{0,8},{1,9},{2,10},{3,11},{4,12},{5,13},{6,14},{7,15},{8,0},{9,1},... | collective-permute-start | bytes 159752 | tf_op jit(solution)/shard_map/ppermute | solution.py:599
  27.3 6.3 %collective-permute-start.7 = (bf16[32,2560]{1,0:T(8,128)(2,1)S(1)}, bf16[32,2560]{1,0:T(8,128)(2,1)S(1)}, u32[]{:S(2)}, u32[]{:S(2)}) collective-permute-start(bf16[32,2560]{1,0:T(8,128)(2,1)S(1)} %slice_bitcast_fusion), channel_id=1, source_target_pairs={{0,16},{16,0},{1,17},{17,1},{2,18},{18,2},{3,19},{19,3},{4,20},{20... | collective-permute-start | bytes 491528 | tf_op jit(solution)/shard_map/ppermute | solution.py:650
  30.1 4.6 %collective-permute-start.9 = (bf16[104,256]{1,0:T(8,128)(2,1)S(1)}, bf16[104,256]{1,0:T(8,128)(2,1)S(1)}, u32[]{:S(2)}, u32[]{:S(2)}) collective-permute-start(bf16[104,256]{1,0:T(8,128)(2,1)S(1)} %add_convert_fusion.refs_0_), channel_id=1, source_target_pairs={{0,1},{1,0},{2,3},{3,2},{4,5},{5,4},{6,7},{7,6},{8,9},{9,8},{10,11... | collective-permute-start | bytes 159752 | tf_op jit(solution)/shard_map/ppermute | solution.py:599
  30.7 5.0 %collective-permute-start.11 = (bf16[104,256]{1,0:T(8,128)(2,1)S(1)}, bf16[104,256]{1,0:T(8,128)(2,1)S(1)}, u32[]{:S(2)}, u32[]{:S(2)}) collective-permute-start(bf16[104,256]{1,0:T(8,128)(2,1)S(1)} %add_convert_fusion.refs_0_), channel_id=1, source_target_pairs={{0,3},{1,2},{2,1},{3,0},{4,7},{5,6},{6,5},{7,4},{8,11},{9,10},{10,... | collective-permute-start | bytes 159752 | tf_op jit(solution)/shard_map/ppermute | solution.py:599
  32.2 4.2 %collective-permute-start.10 = (bf16[104,256]{1,0:T(8,128)(2,1)S(1)}, bf16[104,256]{1,0:T(8,128)(2,1)S(1)}, u32[]{:S(2)}, u32[]{:S(2)}) collective-permute-start(bf16[104,256]{1,0:T(8,128)(2,1)S(1)} %add_convert_fusion.refs_0_), channel_id=1, source_target_pairs={{0,2},{1,3},{2,0},{3,1},{4,6},{5,7},{6,4},{7,5},{8,10},{9,11},{10,... | collective-permute-start | bytes 159752 | tf_op jit(solution)/shard_map/ppermute | solution.py:599
  36.4 1.5 %collective-permute-start.12 = (bf16[416,256]{1,0:T(8,128)(2,1)S(1)}, bf16[416,256]{1,0:T(8,128)(2,1)S(1)}, u32[]{:S(2)}, u32[]{:S(2)}) collective-permute-start(bf16[416,256]{1,0:T(8,128)(2,1)S(1)} %pad_maximum_fusion), channel_id=1, source_target_pairs={{0,16},{1,17},{2,18},{3,19},{4,20},{5,21},{6,22},{7,23},{8,24},{9,... | collective-permute-start | bytes 638984 | tf_op jit(solution)/shard_map/ppermute | solution.py:599

commit v7 on v6

--- a/solution.py
+++ b/solution.py
@@ -249,8 +249,8 @@
     code_w = jnp.concatenate([code_hi.astype(F32), code_mid.astype(F32), code_lo], axis=0).T.astype(BF16)
 
     subject = subj_ref[0:1, :]
-    hot_rows = lax.broadcasted_iota(jnp.int32, (3 * subjects, members), 0) % subjects
-    hot = (hot_rows == subject).astype(F32).astype(BF16)
+    hot = (lax.broadcasted_iota(jnp.int32, (subjects, members), 0) == subject).astype(F32)
+    hot = jnp.concatenate([hot, hot, hot], axis=0).astype(BF16)
     x = (feats_ref[...].astype(F32) + mm(code_w, hot)).astype(BF16)
     inputs_out[0:width, :] = x
     inputs_out[width : width + 16, :] = hot[0:16]
@@ -405,8 +405,8 @@
     for ref in got_refs:
         grad = grad + ref[...].astype(F32)
     rows = lax.broadcasted_iota(jnp.int32, (16, members), 0)
-    quarter = rows // 4
-    place = rows % 4
+    quarter = lax.shift_right_logical(rows, 2)
+    place = lax.bitwise_and(rows, 3)
     grad_rows = jnp.where(
         quarter == 0,
         grad[0:1],
@@ -525,11 +525,11 @@
 def finish_kernel(side_ref, quarter_ref, *refs):
     mine_refs, refs = refs[:FAN], refs[FAN:]
     theirs_ref, *square_outs, bias_out, head_out, code_out, bone_out, small_s = refs
-    piece, rows = block_pieces(theirs_ref.shape[1])
+    piece, rows = block_pieces(theirs_ref.shape[2])
     for core in range(2):
         owner = side_ref[0] if core == 0 else 1 - side_ref[0]
         for slot in range(FAN):
-            block = mine_refs[slot] if core == 0 else theirs_ref.at[slot * rows : (slot + 1) * rows]
+            block = mine_refs[slot] if core == 0 else theirs_ref.at[slot]
             place = owner * FAN + lax.bitwise_xor(quarter_ref[0], slot)
             spot = pl.ds(pl.multiple_of(place * piece, piece), piece)
             for square, out in enumerate(square_outs):
@@ -626,7 +626,7 @@
     got = [swap(total, slot, count) for slot in range(1, FAN)]
     got = work("gather", total, got)
     mine = [total, *got]
-    theirs = swap(jnp.concatenate(mine, axis=0), pair, count)
+    theirs = swap(jnp.stack(mine), pair, count)
     return mine, theirs
 
 

time: 38.9 us -> 39 us (level)
  no operation moved by 1% of the time
where the time goes in v7:
time: 39 us; the launch traced here: 38.9 us
  Pallas kernels  16.3 us (42%)
  starting transfers between devices  13 us (33%)
  waiting for transfers between devices  8.57 us (22%)
  between operations  0.77 us (2%)
    ppermute x10, starting transfers between devices, swap(): lax.ppermute(value, AXES, [(place, place ^ mask) for place in range(count)])  12.3 us
    ppermute x10, waiting for transfers between devices, swap(): lax.ppermute(value, AXES, [(place, place ^ mask) for place in range(count)])  8.56 us
    pallas_call x2, Pallas kernels, scatter(): pl.pallas_call(functools.partial(scatter_kernel, first_row, rows, viewers...  4.48 us
    pallas_call x1, Pallas kernels, forward(): pl.pallas_call(forward_kernel, out_shape=(jax.ShapeDtypeStruct((width + 1...  3.29 us
    pallas_call x1, Pallas kernels, backward(): pl.pallas_call(functools.partial(backward_kernel, factor, subjects, per_s...  3.13 us
    pallas_call x1, Pallas kernels, entry(): pl.pallas_call(functools.partial(entry_kernel, viewers, count), out_shape...  1.96 us
    pallas_call x1, Pallas kernels, gaussian_grads(): pl.pallas_call(gaussian_kernel, out_shape=(jax.ShapeDtypeStruct((width, m...  1.6 us
    pallas_call x1, Pallas kernels, attr_sum(): pl.pallas_call(functools.partial(attr_kernel, len(groups)), out_shape=jax...  0.99 us
  transfers between devices with their start and end apart: 13, of which 8 were waited for; matrix products, arithmetic and copies ran while one was open for 0% of the time, Pallas kernels for 27%

profile of v7, /device:TPU:0, one launch (start us, length us, event | category | flops | bytes accessed | tf_op | source)
XLA Modules:
  0.0 38.9 jit_solution(3683818115150700078)
XLA Ops:
  0.7 2.0 %shard_map.213 = (bf16[2,16,2560]{2,1,0:T(8,128)(2,1)S(1)}, s32[1,5120]{1,0:T(1,128)S(1)}, bf16[1,59,5120]{2,1,0:T(8,128)(2,1)S(1)}, bf16[256,2560]{1,0:T(8,128)...) custom-call(s32[1]{0:T(128)} %bitcast.view_ref, ...), custom_call_target="tpu_custom_call" | custom-call | tf_op jit(solution)/shard_map/pallas_call | solution.py:177
  2.6 0.5 %collective-permute-start = (bf16[16,2560]{1,0:T(8,128)(2,1)S(1)}, bf16[16,2560]{1,0:T(8,128)(2,1)S(1)}, u32[]{:S(2)}, u32[]{:S(2)}) collective-permute-start(bf16[16,2560]{1,0:T(8,128)(2,1)S(1)} %slice_bitcast_fusion.2), channel_id=1, source_target_pairs={{0,16},{16,0},{1,17},{17,1},{2,18},{18,2},{3,19},{19,3},{4,20},{20... | collective-permute-start | bytes 245768 | tf_op jit(solution)/shard_map/ppermute | solution.py:650
  3.2 3.3 %shard_map.214 = (bf16[272,2560]{1,0:T(8,128)(2,1)S(1)}, bf16[256,2560]{1,0:T(8,128)(2,1)S(1)}, bf16[256,2560]{1,0:T(8,128)(2,1)S(1)}, bf16[256,2560]{1,0:T(8,12...) custom-call(bf16[256,2560]{1,0:T(8,128)(2,1)S(1)} %get-tuple-element, ...), custom_call_target="tpu_custom_call" | custom-call | tf_op jit(solution)/shard_map/pallas_call | solution.py:319
  6.4 0.0 collective-permute-done.refs_3_
  6.5 3.1 %shard_map.215 = (f32[16,2560]{1,0:T(8,128)S(1)}, bf16[256,2560]{1,0:T(8,128)(2,1)S(1)}, bf16[4,104,256]{2,1,0:T(8,128)(2,1)S(1)}, bf16[4,104,256]{2,1,0:T(8,128)(2,1)S(1)}) custom-call(s32[1]{0:T(128)S(6)} %and.10.refs_0_.side_ref, s32[1]{0:T(128)} %bitcast.3.refs_1_.quarter_ref, bf16[2,16,2560]{2,1,0:T(8,128)(2,1)S(1)} %get-tuple-element.68.refs_2_, ...), custom_call_target="tpu_custom_call" | custom-call | tf_op jit(solution)/shard_map/pallas_call | solution.py:468
  9.6 0.1 collective-permute-start.1
  9.7 1.4 %collective-permute-done.1 = bf16[4,104,256]{2,1,0:T(8,128)(2,1)S(1)} collective-permute-done((bf16[4,104,256]{2,1,0:T(8,128)(2,1)S(1)}, bf16[4,104,256]{2,1,0:T(8,128)(2,1)S(1)}, u32[]{:S(2)}, u32[]{:S(2)}) %collective-permute-start.1) | collective-permute-done | bytes 213024 | tf_op jit(solution)/shard_map/ppermute | solution.py:599
  11.1 0.1 fusion.2
  11.2 2.7 %collective-permute-start.2 = (bf16[104,256]{1,0:T(8,128)(2,1)S(1)}, bf16[104,256]{1,0:T(8,128)(2,1)S(1)}, u32[]{:S(2)}, u32[]{:S(2)}) collective-permute-start(bf16[104,256]{1,0:T(8,128)(2,1)S(1)} %get-tuple-element.124), channel_id=1, source_target_pairs={{0,1},{1,0},{2,3},{3,2},{4,5},{5,4},{6,7},{7,6},{8,9},{9,8},{10,11... | collective-permute-start | bytes 159752 | tf_op jit(solution)/shard_map/ppermute | solution.py:599
  13.9 1.5 %collective-permute-start.4 = (bf16[104,256]{1,0:T(8,128)(2,1)S(1)}, bf16[104,256]{1,0:T(8,128)(2,1)S(1)}, u32[]{:S(2)}, u32[]{:S(2)}) collective-permute-start(bf16[104,256]{1,0:T(8,128)(2,1)S(1)} %get-tuple-element.122), channel_id=1, source_target_pairs={{0,2},{1,3},{2,0},{3,1},{4,6},{5,7},{6,4},{7,5},{8,10},{9,11},{10,... | collective-permute-start | bytes 159752 | tf_op jit(solution)/shard_map/ppermute | solution.py:599
  15.4 0.0 collective-permute-start.5
  15.4 2.2 %shard_map.216.refs_0_ = bf16[2,32,2560]{2,1,0:T(8,128)(2,1)S(1)} custom-call(s32[1]{0:T(128)} %bitcast.view_ref, bf16[1,59,5120]{2,1,0:T(8,128)(2,1)S(1)} %get-tuple-element.97.grads_ref, s32[1,5120]{1,0:T(1,128)S(1)} %get-tuple-element.98.ids_ref), custom_call_target="tpu_custom_call" | custom-call | tf_op jit(solution)/shard_map/pallas_call | solution.py:99
  17.7 0.0 collective-permute-done.2
  17.7 0.3 collective-permute-done.4
  18.0 2.4 %collective-permute-done.5 = bf16[104,256]{1,0:T(8,128)(2,1)S(1)} collective-permute-done((bf16[104,256]{1,0:T(8,128)(2,1)S(1)}, bf16[104,256]{1,0:T(8,128)(2,1)S(1)}, u32[]{:S(2)}, u32[]{:S(2)}) %collective-permute-start.5) | collective-permute-done | bytes 53280 | tf_op jit(solution)/shard_map/ppermute | solution.py:599
  20.5 1.7 %collective-permute-start.6 = (bf16[104,256]{1,0:T(8,128)(2,1)S(1)}, bf16[104,256]{1,0:T(8,128)(2,1)S(1)}, u32[]{:S(2)}, u32[]{:S(2)}) collective-permute-start(bf16[104,256]{1,0:T(8,128)(2,1)S(1)} %add_convert_fusion.2), channel_id=1, source_target_pairs={{0,4},{1,5},{2,6},{3,7},{4,0},{5,1},{6,2},{7,3},{8,12},{9,13},{10,... | collective-permute-start | bytes 159752 | tf_op jit(solution)/shard_map/ppermute | solution.py:599
  22.1 0.1 collective-permute-start.3
  22.2 2.2 %shard_map.217.refs_2_ = bf16[2,32,2560]{2,1,0:T(8,128)(2,1)S(1)} custom-call(s32[1]{0:T(128)} %bitcast.view_ref, bf16[1,59,5120]{2,1,0:T(8,128)(2,1)S(1)} %get-tuple-element.97.grads_ref, s32[1,5120]{1,0:T(1,128)S(1)} %get-tuple-element.98.ids_ref), custom_call_target="tpu_custom_call" | custom-call | tf_op jit(solution)/shard_map/pallas_call | solution.py:99
  24.5 0.2 collective-permute-done.6
  24.7 2.7 %collective-permute-start.8 = (bf16[104,256]{1,0:T(8,128)(2,1)S(1)}, bf16[104,256]{1,0:T(8,128)(2,1)S(1)}, u32[]{:S(2)}, u32[]{:S(2)}) collective-permute-start(bf16[104,256]{1,0:T(8,128)(2,1)S(1)} %add_convert_fusion.1), channel_id=1, source_target_pairs={{0,8},{1,9},{2,10},{3,11},{4,12},{5,13},{6,14},{7,15},{8,0},{9,1},... | collective-permute-start | bytes 159752 | tf_op jit(solution)/shard_map/ppermute | solution.py:599
  27.4 0.1 collective-permute-start.7
  27.5 1.6 %shard_map.219 = (bf16[256,2560]{1,0:T(8,128)(2,1)}, f32[4,1,2560]{2,1,0:T(1,128)}) custom-call(bf16[256,2560]{1,0:T(8,128)(2,1)S(1)} %get-tuple-element.104.back_ref, bf16[256,256]{1,0:T(8,128)(2,1)S(1)} %get-tuple-element.105.first_ref.refs_15_, f32[16,2560]{1,0:T(8,128)S(1)} %get-tuple-element.106.outer_ref, f32[4,16,2560]{2,1,0:T(8,128)S(1)} %get-tuple-element.107.matrix_ref), custom_call_target="tpu_custom_call" | custom-call | tf_op jit(solution)/shard_map/pallas_call | solution.py:513
  29.1 1.1 %collective-permute-done.8 = bf16[104,256]{1,0:T(8,128)(2,1)S(1)} collective-permute-done((bf16[104,256]{1,0:T(8,128)(2,1)S(1)}, bf16[104,256]{1,0:T(8,128)(2,1)S(1)}, u32[]{:S(2)}, u32[]{:S(2)}) %collective-permute-start.8) | collective-permute-done | bytes 53280 | tf_op jit(solution)/shard_map/ppermute | solution.py:599
  30.2 0.6 %collective-permute-start.9 = (bf16[104,256]{1,0:T(8,128)(2,1)S(1)}, bf16[104,256]{1,0:T(8,128)(2,1)S(1)}, u32[]{:S(2)}, u32[]{:S(2)}) collective-permute-start(bf16[104,256]{1,0:T(8,128)(2,1)S(1)} %add_convert_fusion.refs_0_), channel_id=1, source_target_pairs={{0,1},{1,0},{2,3},{3,2},{4,5},{5,4},{6,7},{7,6},{8,9},{9,8},{10,11... | collective-permute-start | bytes 159752 | tf_op jit(solution)/shard_map/ppermute | solution.py:599
  30.8 1.4 %collective-permute-start.11 = (bf16[104,256]{1,0:T(8,128)(2,1)S(1)}, bf16[104,256]{1,0:T(8,128)(2,1)S(1)}, u32[]{:S(2)}, u32[]{:S(2)}) collective-permute-start(bf16[104,256]{1,0:T(8,128)(2,1)S(1)} %add_convert_fusion.refs_0_), channel_id=1, source_target_pairs={{0,3},{1,2},{2,1},{3,0},{4,7},{5,6},{6,5},{7,4},{8,11},{9,10},{10,... | collective-permute-start | bytes 159752 | tf_op jit(solution)/shard_map/ppermute | solution.py:599
  32.2 1.5 %collective-permute-start.10 = (bf16[104,256]{1,0:T(8,128)(2,1)S(1)}, bf16[104,256]{1,0:T(8,128)(2,1)S(1)}, u32[]{:S(2)}, u32[]{:S(2)}) collective-permute-start(bf16[104,256]{1,0:T(8,128)(2,1)S(1)} %add_convert_fusion.refs_0_), channel_id=1, source_target_pairs={{0,2},{1,3},{2,0},{3,1},{4,6},{5,7},{6,4},{7,5},{8,10},{9,11},{10,... | collective-permute-start | bytes 159752 | tf_op jit(solution)/shard_map/ppermute | solution.py:599
  33.7 0.0 collective-permute-done.3.refs_1_
  33.7 0.0 collective-permute-done.7.refs_3_
  33.7 1.0 %shard_map.218 = f32[59,1,2560]{2,1,0:T(1,128)} custom-call(bf16[2,32,2560]{2,1,0:T(8,128)(2,1)S(1)} %shard_map.216.refs_0_, bf16[32,2560]{1,0:T(8,128)(2,1)S(1)} %collective-permute-done.3.refs_1_, bf16[2,32,2560]{2,1,0:T(8,128)(2,1)S(1)} %shard_map.217.refs_2_, bf16[32,2560]{1,0:T(8,128)(2,1)S(1)} %collective-permute-done.7.refs_3_), custom_call_target="tpu_custom_call" | custom-call | tf_op jit(solution)/shard_map/pallas_call | solution.py:585
  34.7 0.0 collective-permute-done.9.refs_1_
  34.7 1.1 %collective-permute-done.11.refs_3_ = bf16[104,256]{1,0:T(8,128)(2,1)S(1)} collective-permute-done((bf16[104,256]{1,0:T(8,128)(2,1)S(1)}, bf16[104,256]{1,0:T(8,128)(2,1)S(1)}, u32[]{:S(2)}, u32[]{:S(2)}) %collective-permute-start.11) | collective-permute-done | bytes 53280 | tf_op jit(solution)/shard_map/ppermute | solution.py:599
  35.8 0.6 %collective-permute-done.10.refs_2_ = bf16[104,256]{1,0:T(8,128)(2,1)S(1)} collective-permute-done((bf16[104,256]{1,0:T(8,128)(2,1)S(1)}, bf16[104,256]{1,0:T(8,128)(2,1)S(1)}, u32[]{:S(2)}, u32[]{:S(2)}) %collective-permute-start.10) | collective-permute-done | bytes 53280 | tf_op jit(solution)/shard_map/ppermute | solution.py:599
  36.4 0.1 collective-permute-start.12
  36.5 1.5 %collective-permute-done.12.refs_4_ = bf16[4,104,256]{2,1,0:T(8,128)(2,1)S(1)} collective-permute-done((bf16[4,104,256]{2,1,0:T(8,128)(2,1)S(1)}, bf16[4,104,256]{2,1,0:T(8,128)(2,1)S(1)}, u32[]{:S(2)}, u32[]{:S(2)}) %collective-permute-start.12) | collective-permute-done | bytes 213024 | tf_op jit(solution)/shard_map/ppermute | solution.py:599
  37.9 0.9 %shard_map.220 = (f32[256,256]{1,0:T(8,128)}, f32[256,256]{1,0:T(8,128)}, f32[256,256]{1,0:T(8,128)}, f32[3,256]{1,0:T(4,128)}, f32[3,256]{1,0:T(4,128)}, /*index=5*/f32[8,256]{1,0:T(8,128)}, f32[12,192]{1,0:T(8,128)}) custom-call(s32[1]{0:T(128)S(6)} %and.10.refs_0_.side_ref, s32[1]{0:T(128)} %bitcast.3.refs_1_.quarter_ref, ...), custom_call_target="tpu_custom_call" | custom-call | tf_op jit(solution)/shard_map/pallas_call | solution.py:550
  (7 shorter events, 0.1 us)
Async XLA Ops:
  2.6 3.8 %collective-permute-start = (bf16[16,2560]{1,0:T(8,128)(2,1)S(1)}, bf16[16,2560]{1,0:T(8,128)(2,1)S(1)}, u32[]{:S(2)}, u32[]{:S(2)}) collective-permute-start(bf16[16,2560]{1,0:T(8,128)(2,1)S(1)} %slice_bitcast_fusion.2), channel_id=1, source_target_pairs={{0,16},{16,0},{1,17},{17,1},{2,18},{18,2},{3,19},{19,3},{4,20},{20... | collective-permute-start | bytes 245768 | tf_op jit(solution)/shard_map/ppermute | solution.py:650
  9.6 1.5 %collective-permute-start.1 = (bf16[4,104,256]{2,1,0:T(8,128)(2,1)S(1)}, bf16[4,104,256]{2,1,0:T(8,128)(2,1)S(1)}, u32[]{:S(2)}, u32[]{:S(2)}) collective-permute-start(bf16[4,104,256]{2,1,0:T(8,128)(2,1)S(1)} %get-tuple-element.92), channel_id=1, source_target_pairs={{0,16},{1,17},{2,18},{3,19},{4,20},{5,21},{6,22},{7,23},{8,24},{9,... | collective-permute-start | bytes 638984 | tf_op jit(solution)/shard_map/ppermute | solution.py:599
  11.2 6.5 %collective-permute-start.2 = (bf16[104,256]{1,0:T(8,128)(2,1)S(1)}, bf16[104,256]{1,0:T(8,128)(2,1)S(1)}, u32[]{:S(2)}, u32[]{:S(2)}) collective-permute-start(bf16[104,256]{1,0:T(8,128)(2,1)S(1)} %get-tuple-element.124), channel_id=1, source_target_pairs={{0,1},{1,0},{2,3},{3,2},{4,5},{5,4},{6,7},{7,6},{8,9},{9,8},{10,11... | collective-permute-start | bytes 159752 | tf_op jit(solution)/shard_map/ppermute | solution.py:599
  13.9 4.1 %collective-permute-start.4 = (bf16[104,256]{1,0:T(8,128)(2,1)S(1)}, bf16[104,256]{1,0:T(8,128)(2,1)S(1)}, u32[]{:S(2)}, u32[]{:S(2)}) collective-permute-start(bf16[104,256]{1,0:T(8,128)(2,1)S(1)} %get-tuple-element.122), channel_id=1, source_target_pairs={{0,2},{1,3},{2,0},{3,1},{4,6},{5,7},{6,4},{7,5},{8,10},{9,11},{10,... | collective-permute-start | bytes 159752 | tf_op jit(solution)/shard_map/ppermute | solution.py:599
  15.4 5.0 %collective-permute-start.5 = (bf16[104,256]{1,0:T(8,128)(2,1)S(1)}, bf16[104,256]{1,0:T(8,128)(2,1)S(1)}, u32[]{:S(2)}, u32[]{:S(2)}) collective-permute-start(bf16[104,256]{1,0:T(8,128)(2,1)S(1)} %get-tuple-element.123), channel_id=1, source_target_pairs={{0,3},{1,2},{2,1},{3,0},{4,7},{5,6},{6,5},{7,4},{8,11},{9,10},{10,... | collective-permute-start | bytes 159752 | tf_op jit(solution)/shard_map/ppermute | solution.py:599
  20.5 4.2 %collective-permute-start.6 = (bf16[104,256]{1,0:T(8,128)(2,1)S(1)}, bf16[104,256]{1,0:T(8,128)(2,1)S(1)}, u32[]{:S(2)}, u32[]{:S(2)}) collective-permute-start(bf16[104,256]{1,0:T(8,128)(2,1)S(1)} %add_convert_fusion.2), channel_id=1, source_target_pairs={{0,4},{1,5},{2,6},{3,7},{4,0},{5,1},{6,2},{7,3},{8,12},{9,13},{10,... | collective-permute-start | bytes 159752 | tf_op jit(solution)/shard_map/ppermute | solution.py:599
  22.1 11.6 %collective-permute-start.3 = (bf16[32,2560]{1,0:T(8,128)(2,1)S(1)}, bf16[32,2560]{1,0:T(8,128)(2,1)S(1)}, u32[]{:S(2)}, u32[]{:S(2)}) collective-permute-start(bf16[32,2560]{1,0:T(8,128)(2,1)S(1)} %slice_bitcast_fusion.1), channel_id=1, source_target_pairs={{0,16},{16,0},{1,17},{17,1},{2,18},{18,2},{3,19},{19,3},{4,20},{20... | collective-permute-start | bytes 491528 | tf_op jit(solution)/shard_map/ppermute | solution.py:650
  24.7 5.5 %collective-permute-start.8 = (bf16[104,256]{1,0:T(8,128)(2,1)S(1)}, bf16[104,256]{1,0:T(8,128)(2,1)S(1)}, u32[]{:S(2)}, u32[]{:S(2)}) collective-permute-start(bf16[104,256]{1,0:T(8,128)(2,1)S(1)} %add_convert_fusion.1), channel_id=1, source_target_pairs={{0,8},{1,9},{2,10},{3,11},{4,12},{5,13},{6,14},{7,15},{8,0},{9,1},... | collective-permute-start | bytes 159752 | tf_op jit(solution)/shard_map/ppermute | solution.py:599
  27.4 6.4 %collective-permute-start.7 = (bf16[32,2560]{1,0:T(8,128)(2,1)S(1)}, bf16[32,2560]{1,0:T(8,128)(2,1)S(1)}, u32[]{:S(2)}, u32[]{:S(2)}) collective-permute-start(bf16[32,2560]{1,0:T(8,128)(2,1)S(1)} %slice_bitcast_fusion), channel_id=1, source_target_pairs={{0,16},{16,0},{1,17},{17,1},{2,18},{18,2},{3,19},{19,3},{4,20},{20... | collective-permute-start | bytes 491528 | tf_op jit(solution)/shard_map/ppermute | solution.py:650
  30.2 4.6 %collective-permute-start.9 = (bf16[104,256]{1,0:T(8,128)(2,1)S(1)}, bf16[104,256]{1,0:T(8,128)(2,1)S(1)}, u32[]{:S(2)}, u32[]{:S(2)}) collective-permute-start(bf16[104,256]{1,0:T(8,128)(2,1)S(1)} %add_convert_fusion.refs_0_), channel_id=1, source_target_pairs={{0,1},{1,0},{2,3},{3,2},{4,5},{5,4},{6,7},{7,6},{8,9},{9,8},{10,11... | collective-permute-start | bytes 159752 | tf_op jit(solution)/shard_map/ppermute | solution.py:599
  30.8 5.0 %collective-permute-start.11 = (bf16[104,256]{1,0:T(8,128)(2,1)S(1)}, bf16[104,256]{1,0:T(8,128)(2,1)S(1)}, u32[]{:S(2)}, u32[]{:S(2)}) collective-permute-start(bf16[104,256]{1,0:T(8,128)(2,1)S(1)} %add_convert_fusion.refs_0_), channel_id=1, source_target_pairs={{0,3},{1,2},{2,1},{3,0},{4,7},{5,6},{6,5},{7,4},{8,11},{9,10},{10,... | collective-permute-start | bytes 159752 | tf_op jit(solution)/shard_map/ppermute | solution.py:599
  32.2 4.2 %collective-permute-start.10 = (bf16[104,256]{1,0:T(8,128)(2,1)S(1)}, bf16[104,256]{1,0:T(8,128)(2,1)S(1)}, u32[]{:S(2)}, u32[]{:S(2)}) collective-permute-start(bf16[104,256]{1,0:T(8,128)(2,1)S(1)} %add_convert_fusion.refs_0_), channel_id=1, source_target_pairs={{0,2},{1,3},{2,0},{3,1},{4,6},{5,7},{6,4},{7,5},{8,10},{9,11},{10,... | collective-permute-start | bytes 159752 | tf_op jit(solution)/shard_map/ppermute | solution.py:599
  36.4 1.5 %collective-permute-start.12 = (bf16[4,104,256]{2,1,0:T(8,128)(2,1)S(1)}, bf16[4,104,256]{2,1,0:T(8,128)(2,1)S(1)}, u32[]{:S(2)}, u32[]{:S(2)}) collective-permute-start(bf16[4,104,256]{2,1,0:T(8,128)(2,1)S(1)} %pad_maximum_fusion), channel_id=1, source_target_pairs={{0,16},{1,17},{2,18},{3,19},{4,20},{5,21},{6,22},{7,23},{8,24},{9,... | collective-permute-start | bytes 638984 | tf_op jit(solution)/shard_map/ppermute | solution.py:599

commit v8 on v6

--- a/solution.py
+++ b/solution.py
@@ -730,7 +730,7 @@
         return [attr_sum([[value, *received(value, viewers)] for value in sums], attrs)]
 
     last = Work(attributes, view)
-    between = {"scatter": works[:1], 0: works[1:], 1: [per_gaussian], "gather": [last]}
+    between = {"scatter": [*works[:1], per_gaussian], 0: works[1:], 1: [last]}
     mine, theirs = sum_over_devices(mine, theirs, viewers, shards, between)
     attr = last.results[0]
     feat_grads, skin_grads = per_gaussian.results

time: 38.9 us -> 40.4 us (1.039)
  waiting for transfers between devices: 8.51 us -> 9.67 us
    ppermute x10, waiting for transfers between devices: 8.5 us -> 9.66 us  [swap(): lax.ppermute(value, AXES, [(place, place ^ mask) for place in range(count)])]
  transfers between devices with their start and end apart: 13 -> 13, of which waited for: 8 -> 8; matrix products, arithmetic and copies ran while one was open for 0% -> 0% of each run, Pallas kernels for 27% -> 26%
where the time goes in v8:
time: 40.4 us; the launch traced here: 40.2 us
  Pallas kernels  16.4 us (41%)
  starting transfers between devices  13.3 us (33%)
  waiting for transfers between devices  9.67 us (24%)
  between operations  0.75 us (2%)
    ppermute x10, starting transfers between devices, swap(): lax.ppermute(value, AXES, [(place, place ^ mask) for place in range(count)])  12.3 us
    ppermute x10, waiting for transfers between devices, swap(): lax.ppermute(value, AXES, [(place, place ^ mask) for place in range(count)])  9.66 us
    pallas_call x2, Pallas kernels, scatter(): pl.pallas_call(functools.partial(scatter_kernel, first_row, rows, viewers...  4.5 us
    pallas_call x1, Pallas kernels, forward(): pl.pallas_call(forward_kernel, out_shape=(jax.ShapeDtypeStruct((width + 1...  3.24 us
    pallas_call x1, Pallas kernels, backward(): pl.pallas_call(functools.partial(backward_kernel, factor, subjects, per_s...  3.16 us
    pallas_call x1, Pallas kernels, entry(): pl.pallas_call(functools.partial(entry_kernel, viewers, count), out_shape...  1.96 us
    pallas_call x1, Pallas kernels, gaussian_grads(): pl.pallas_call(gaussian_kernel, out_shape=(jax.ShapeDtypeStruct((width, m...  1.6 us
    pallas_call x1, Pallas kernels, attr_sum(): pl.pallas_call(functools.partial(attr_kernel, len(groups)), out_shape=jax...  0.99 us
  transfers between devices with their start and end apart: 13, of which 8 were waited for; matrix products, arithmetic and copies ran while one was open for 0% of the time, Pallas kernels for 26%

profile of v8, /device:TPU:0, one launch (start us, length us, event | category | flops | bytes accessed | tf_op | source)
XLA Modules:
  0.0 40.2 jit_solution(7083679908482822911)
XLA Ops:
  0.7 2.0 %shard_map.213 = (bf16[2,16,2560]{2,1,0:T(8,128)(2,1)S(1)}, s32[1,5120]{1,0:T(1,128)S(1)}, bf16[1,59,5120]{2,1,0:T(8,128)(2,1)S(1)}, bf16[256,2560]{1,0:T(8,128)...) custom-call(s32[1]{0:T(128)} %bitcast.view_ref, ...), custom_call_target="tpu_custom_call" | custom-call | tf_op jit(solution)/shard_map/pallas_call | solution.py:177
  2.6 0.5 %collective-permute-start = (bf16[16,2560]{1,0:T(8,128)(2,1)S(1)}, bf16[16,2560]{1,0:T(8,128)(2,1)S(1)}, u32[]{:S(2)}, u32[]{:S(2)}) collective-permute-start(bf16[16,2560]{1,0:T(8,128)(2,1)S(1)} %slice_bitcast_fusion.2), channel_id=1, source_target_pairs={{0,16},{16,0},{1,17},{17,1},{2,18},{18,2},{3,19},{19,3},{4,20},{20... | collective-permute-start | bytes 245768 | tf_op jit(solution)/shard_map/ppermute | solution.py:650
  3.2 3.2 %shard_map.214 = (bf16[272,2560]{1,0:T(8,128)(2,1)S(1)}, bf16[256,2560]{1,0:T(8,128)(2,1)S(1)}, bf16[256,2560]{1,0:T(8,128)(2,1)S(1)}, bf16[256,2560]{1,0:T(8,12...) custom-call(bf16[256,2560]{1,0:T(8,128)(2,1)S(1)} %get-tuple-element, ...), custom_call_target="tpu_custom_call" | custom-call | tf_op jit(solution)/shard_map/pallas_call | solution.py:319
  6.4 0.0 collective-permute-done.refs_3_
  6.4 3.2 %shard_map.215 = (f32[16,2560]{1,0:T(8,128)S(1)}, bf16[256,2560]{1,0:T(8,128)(2,1)S(1)}, bf16[4,104,256]{2,1,0:T(8,128)(2,1)S(1)}, bf16[4,104,256]{2,1,0:T(8,128)(2,1)S(1)}) custom-call(s32[1]{0:T(128)S(6)} %and.10.refs_0_.side_ref, s32[1]{0:T(128)} %bitcast.3.refs_1_.quarter_ref, bf16[2,16,2560]{2,1,0:T(8,128)(2,1)S(1)} %get-tuple-element.68.refs_2_, ...), custom_call_target="tpu_custom_call" | custom-call | tf_op jit(solution)/shard_map/pallas_call | solution.py:468
  9.6 0.1 collective-permute-start.1
  9.7 1.4 %collective-permute-done.1 = bf16[4,104,256]{2,1,0:T(8,128)(2,1)S(1)} collective-permute-done((bf16[4,104,256]{2,1,0:T(8,128)(2,1)S(1)}, bf16[4,104,256]{2,1,0:T(8,128)(2,1)S(1)}, u32[]{:S(2)}, u32[]{:S(2)}) %collective-permute-start.1) | collective-permute-done | bytes 213024 | tf_op jit(solution)/shard_map/ppermute | solution.py:599
  11.1 0.1 fusion.2
  11.1 2.7 %collective-permute-start.2 = (bf16[104,256]{1,0:T(8,128)(2,1)S(1)}, bf16[104,256]{1,0:T(8,128)(2,1)S(1)}, u32[]{:S(2)}, u32[]{:S(2)}) collective-permute-start(bf16[104,256]{1,0:T(8,128)(2,1)S(1)} %get-tuple-element.124), channel_id=1, source_target_pairs={{0,1},{1,0},{2,3},{3,2},{4,5},{5,4},{6,7},{7,6},{8,9},{9,8},{10,11... | collective-permute-start | bytes 159752 | tf_op jit(solution)/shard_map/ppermute | solution.py:599
  13.8 1.5 %collective-permute-start.4 = (bf16[104,256]{1,0:T(8,128)(2,1)S(1)}, bf16[104,256]{1,0:T(8,128)(2,1)S(1)}, u32[]{:S(2)}, u32[]{:S(2)}) collective-permute-start(bf16[104,256]{1,0:T(8,128)(2,1)S(1)} %get-tuple-element.122), channel_id=1, source_target_pairs={{0,2},{1,3},{2,0},{3,1},{4,6},{5,7},{6,4},{7,5},{8,10},{9,11},{10,... | collective-permute-start | bytes 159752 | tf_op jit(solution)/shard_map/ppermute | solution.py:599
  15.3 0.0 collective-permute-start.5
  15.4 2.3 %shard_map.216.refs_0_ = bf16[2,32,2560]{2,1,0:T(8,128)(2,1)S(1)} custom-call(s32[1]{0:T(128)} %bitcast.view_ref, bf16[1,59,5120]{2,1,0:T(8,128)(2,1)S(1)} %get-tuple-element.107.grads_ref, s32[1,5120]{1,0:T(1,128)S(1)} %get-tuple-element.108.ids_ref), custom_call_target="tpu_custom_call" | custom-call | tf_op jit(solution)/shard_map/pallas_call | solution.py:99
  17.6 1.6 %shard_map.217 = (bf16[256,2560]{1,0:T(8,128)(2,1)}, f32[4,1,2560]{2,1,0:T(1,128)}) custom-call(bf16[256,2560]{1,0:T(8,128)(2,1)S(1)} %get-tuple-element.99.back_ref, bf16[256,256]{1,0:T(8,128)(2,1)S(1)} %get-tuple-element.100.first_ref.refs_15_, f32[16,2560]{1,0:T(8,128)S(1)} %get-tuple-element.101.outer_ref, f32[4,16,2560]{2,1,0:T(8,128)S(1)} %get-tuple-element.102.matrix_ref), custom_call_target="tpu_custom_call" | custom-call | tf_op jit(solution)/shard_map/pallas_call | solution.py:513
  19.2 0.0 collective-permute-done.2
  19.2 0.0 collective-permute-done.4
  19.3 1.1 %collective-permute-done.5 = bf16[104,256]{1,0:T(8,128)(2,1)S(1)} collective-permute-done((bf16[104,256]{1,0:T(8,128)(2,1)S(1)}, bf16[104,256]{1,0:T(8,128)(2,1)S(1)}, u32[]{:S(2)}, u32[]{:S(2)}) %collective-permute-start.5) | collective-permute-done | bytes 53280 | tf_op jit(solution)/shard_map/ppermute | solution.py:599
  20.4 1.7 %collective-permute-start.6 = (bf16[104,256]{1,0:T(8,128)(2,1)S(1)}, bf16[104,256]{1,0:T(8,128)(2,1)S(1)}, u32[]{:S(2)}, u32[]{:S(2)}) collective-permute-start(bf16[104,256]{1,0:T(8,128)(2,1)S(1)} %add_convert_fusion.2), channel_id=1, source_target_pairs={{0,4},{1,5},{2,6},{3,7},{4,0},{5,1},{6,2},{7,3},{8,12},{9,13},{10,... | collective-permute-start | bytes 159752 | tf_op jit(solution)/shard_map/ppermute | solution.py:599
  22.1 0.1 collective-permute-start.3
  22.2 2.2 %shard_map.218.refs_2_ = bf16[2,32,2560]{2,1,0:T(8,128)(2,1)S(1)} custom-call(s32[1]{0:T(128)} %bitcast.view_ref, bf16[1,59,5120]{2,1,0:T(8,128)(2,1)S(1)} %get-tuple-element.107.grads_ref, s32[1,5120]{1,0:T(1,128)S(1)} %get-tuple-element.108.ids_ref), custom_call_target="tpu_custom_call" | custom-call | tf_op jit(solution)/shard_map/pallas_call | solution.py:99
  24.4 0.2 collective-permute-done.6
  24.6 0.4 collective-permute-start.7
  25.0 2.7 %collective-permute-start.8 = (bf16[104,256]{1,0:T(8,128)(2,1)S(1)}, bf16[104,256]{1,0:T(8,128)(2,1)S(1)}, u32[]{:S(2)}, u32[]{:S(2)}) collective-permute-start(bf16[104,256]{1,0:T(8,128)(2,1)S(1)} %add_convert_fusion.1), channel_id=1, source_target_pairs={{0,8},{1,9},{2,10},{3,11},{4,12},{5,13},{6,14},{7,15},{8,0},{9,1},... | collective-permute-start | bytes 159752 | tf_op jit(solution)/shard_map/ppermute | solution.py:599
  27.7 0.0 collective-permute-done.3.refs_1_
  27.7 0.0 collective-permute-done.7.refs_3_
  27.7 1.0 %shard_map.219 = f32[59,1,2560]{2,1,0:T(1,128)} custom-call(bf16[2,32,2560]{2,1,0:T(8,128)(2,1)S(1)} %shard_map.216.refs_0_, bf16[32,2560]{1,0:T(8,128)(2,1)S(1)} %collective-permute-done.3.refs_1_, bf16[2,32,2560]{2,1,0:T(8,128)(2,1)S(1)} %shard_map.218.refs_2_, bf16[32,2560]{1,0:T(8,128)(2,1)S(1)} %collective-permute-done.7.refs_3_), custom_call_target="tpu_custom_call" | custom-call | tf_op jit(solution)/shard_map/pallas_call | solution.py:585
  28.7 2.6 %collective-permute-done.8 = bf16[104,256]{1,0:T(8,128)(2,1)S(1)} collective-permute-done((bf16[104,256]{1,0:T(8,128)(2,1)S(1)}, bf16[104,256]{1,0:T(8,128)(2,1)S(1)}, u32[]{:S(2)}, u32[]{:S(2)}) %collective-permute-start.8) | collective-permute-done | bytes 53280 | tf_op jit(solution)/shard_map/ppermute | solution.py:599
  31.3 1.8 %collective-permute-start.11 = (bf16[104,256]{1,0:T(8,128)(2,1)S(1)}, bf16[104,256]{1,0:T(8,128)(2,1)S(1)}, u32[]{:S(2)}, u32[]{:S(2)}) collective-permute-start(bf16[104,256]{1,0:T(8,128)(2,1)S(1)} %add_convert_fusion.refs_0_), channel_id=1, source_target_pairs={{0,3},{1,2},{2,1},{3,0},{4,7},{5,6},{6,5},{7,4},{8,11},{9,10},{10,... | collective-permute-start | bytes 159752 | tf_op jit(solution)/shard_map/ppermute | solution.py:599
  33.1 0.5 %collective-permute-start.10 = (bf16[104,256]{1,0:T(8,128)(2,1)S(1)}, bf16[104,256]{1,0:T(8,128)(2,1)S(1)}, u32[]{:S(2)}, u32[]{:S(2)}) collective-permute-start(bf16[104,256]{1,0:T(8,128)(2,1)S(1)} %add_convert_fusion.refs_0_), channel_id=1, source_target_pairs={{0,2},{1,3},{2,0},{3,1},{4,6},{5,7},{6,4},{7,5},{8,10},{9,11},{10,... | collective-permute-start | bytes 159752 | tf_op jit(solution)/shard_map/ppermute | solution.py:599
  33.6 1.2 %collective-permute-start.9 = (bf16[104,256]{1,0:T(8,128)(2,1)S(1)}, bf16[104,256]{1,0:T(8,128)(2,1)S(1)}, u32[]{:S(2)}, u32[]{:S(2)}) collective-permute-start(bf16[104,256]{1,0:T(8,128)(2,1)S(1)} %add_convert_fusion.refs_0_), channel_id=1, source_target_pairs={{0,1},{1,0},{2,3},{3,2},{4,5},{5,4},{6,7},{7,6},{8,9},{9,8},{10,11... | collective-permute-start | bytes 159752 | tf_op jit(solution)/shard_map/ppermute | solution.py:599
  34.8 1.5 %collective-permute-done.11.refs_3_ = bf16[104,256]{1,0:T(8,128)(2,1)S(1)} collective-permute-done((bf16[104,256]{1,0:T(8,128)(2,1)S(1)}, bf16[104,256]{1,0:T(8,128)(2,1)S(1)}, u32[]{:S(2)}, u32[]{:S(2)}) %collective-permute-start.11) | collective-permute-done | bytes 53280 | tf_op jit(solution)/shard_map/ppermute | solution.py:599
  36.4 0.9 %collective-permute-done.10.refs_2_ = bf16[104,256]{1,0:T(8,128)(2,1)S(1)} collective-permute-done((bf16[104,256]{1,0:T(8,128)(2,1)S(1)}, bf16[104,256]{1,0:T(8,128)(2,1)S(1)}, u32[]{:S(2)}, u32[]{:S(2)}) %collective-permute-start.10) | collective-permute-done | bytes 53280 | tf_op jit(solution)/shard_map/ppermute | solution.py:599
  37.3 0.5 %collective-permute-done.9.refs_1_ = bf16[104,256]{1,0:T(8,128)(2,1)S(1)} collective-permute-done((bf16[104,256]{1,0:T(8,128)(2,1)S(1)}, bf16[104,256]{1,0:T(8,128)(2,1)S(1)}, u32[]{:S(2)}, u32[]{:S(2)}) %collective-permute-start.9) | collective-permute-done | bytes 53280 | tf_op jit(solution)/shard_map/ppermute | solution.py:599
  37.8 0.1 collective-permute-start.12
  37.9 1.5 %collective-permute-done.12.refs_4_ = bf16[416,256]{1,0:T(8,128)(2,1)S(1)} collective-permute-done((bf16[416,256]{1,0:T(8,128)(2,1)S(1)}, bf16[416,256]{1,0:T(8,128)(2,1)S(1)}, u32[]{:S(2)}, u32[]{:S(2)}) %collective-permute-start.12) | collective-permute-done | bytes 213024 | tf_op jit(solution)/shard_map/ppermute | solution.py:599
  39.3 0.9 %shard_map.220 = (f32[256,256]{1,0:T(8,128)}, f32[256,256]{1,0:T(8,128)}, f32[256,256]{1,0:T(8,128)}, f32[3,256]{1,0:T(4,128)}, f32[3,256]{1,0:T(4,128)}, /*index=5*/f32[8,256]{1,0:T(8,128)}, f32[12,192]{1,0:T(8,128)}) custom-call(s32[1]{0:T(128)S(6)} %and.10.refs_0_.side_ref, s32[1]{0:T(128)} %bitcast.3.refs_1_.quarter_ref, ...), custom_call_target="tpu_custom_call" | custom-call | tf_op jit(solution)/shard_map/pallas_call | solution.py:550
  (7 shorter events, 0.1 us)
Async XLA Ops:
  2.6 3.8 %collective-permute-start = (bf16[16,2560]{1,0:T(8,128)(2,1)S(1)}, bf16[16,2560]{1,0:T(8,128)(2,1)S(1)}, u32[]{:S(2)}, u32[]{:S(2)}) collective-permute-start(bf16[16,2560]{1,0:T(8,128)(2,1)S(1)} %slice_bitcast_fusion.2), channel_id=1, source_target_pairs={{0,16},{16,0},{1,17},{17,1},{2,18},{18,2},{3,19},{19,3},{4,20},{20... | collective-permute-start | bytes 245768 | tf_op jit(solution)/shard_map/ppermute | solution.py:650
  9.6 1.5 %collective-permute-start.1 = (bf16[4,104,256]{2,1,0:T(8,128)(2,1)S(1)}, bf16[4,104,256]{2,1,0:T(8,128)(2,1)S(1)}, u32[]{:S(2)}, u32[]{:S(2)}) collective-permute-start(bf16[4,104,256]{2,1,0:T(8,128)(2,1)S(1)} %get-tuple-element.92), channel_id=1, source_target_pairs={{0,16},{1,17},{2,18},{3,19},{4,20},{5,21},{6,22},{7,23},{8,24},{9,... | collective-permute-start | bytes 638984 | tf_op jit(solution)/shard_map/ppermute | solution.py:599
  11.1 8.1 %collective-permute-start.2 = (bf16[104,256]{1,0:T(8,128)(2,1)S(1)}, bf16[104,256]{1,0:T(8,128)(2,1)S(1)}, u32[]{:S(2)}, u32[]{:S(2)}) collective-permute-start(bf16[104,256]{1,0:T(8,128)(2,1)S(1)} %get-tuple-element.124), channel_id=1, source_target_pairs={{0,1},{1,0},{2,3},{3,2},{4,5},{5,4},{6,7},{7,6},{8,9},{9,8},{10,11... | collective-permute-start | bytes 159752 | tf_op jit(solution)/shard_map/ppermute | solution.py:599
  13.8 5.4 %collective-permute-start.4 = (bf16[104,256]{1,0:T(8,128)(2,1)S(1)}, bf16[104,256]{1,0:T(8,128)(2,1)S(1)}, u32[]{:S(2)}, u32[]{:S(2)}) collective-permute-start(bf16[104,256]{1,0:T(8,128)(2,1)S(1)} %get-tuple-element.122), channel_id=1, source_target_pairs={{0,2},{1,3},{2,0},{3,1},{4,6},{5,7},{6,4},{7,5},{8,10},{9,11},{10,... | collective-permute-start | bytes 159752 | tf_op jit(solution)/shard_map/ppermute | solution.py:599
  15.3 5.0 %collective-permute-start.5 = (bf16[104,256]{1,0:T(8,128)(2,1)S(1)}, bf16[104,256]{1,0:T(8,128)(2,1)S(1)}, u32[]{:S(2)}, u32[]{:S(2)}) collective-permute-start(bf16[104,256]{1,0:T(8,128)(2,1)S(1)} %get-tuple-element.123), channel_id=1, source_target_pairs={{0,3},{1,2},{2,1},{3,0},{4,7},{5,6},{6,5},{7,4},{8,11},{9,10},{10,... | collective-permute-start | bytes 159752 | tf_op jit(solution)/shard_map/ppermute | solution.py:599
  20.4 4.2 %collective-permute-start.6 = (bf16[104,256]{1,0:T(8,128)(2,1)S(1)}, bf16[104,256]{1,0:T(8,128)(2,1)S(1)}, u32[]{:S(2)}, u32[]{:S(2)}) collective-permute-start(bf16[104,256]{1,0:T(8,128)(2,1)S(1)} %add_convert_fusion.2), channel_id=1, source_target_pairs={{0,4},{1,5},{2,6},{3,7},{4,0},{5,1},{6,2},{7,3},{8,12},{9,13},{10,... | collective-permute-start | bytes 159752 | tf_op jit(solution)/shard_map/ppermute | solution.py:599
  22.1 5.6 %collective-permute-start.3 = (bf16[32,2560]{1,0:T(8,128)(2,1)S(1)}, bf16[32,2560]{1,0:T(8,128)(2,1)S(1)}, u32[]{:S(2)}, u32[]{:S(2)}) collective-permute-start(bf16[32,2560]{1,0:T(8,128)(2,1)S(1)} %slice_bitcast_fusion.1), channel_id=1, source_target_pairs={{0,16},{16,0},{1,17},{17,1},{2,18},{18,2},{3,19},{19,3},{4,20},{20... | collective-permute-start | bytes 491528 | tf_op jit(solution)/shard_map/ppermute | solution.py:650
  24.6 3.1 %collective-permute-start.7 = (bf16[32,2560]{1,0:T(8,128)(2,1)S(1)}, bf16[32,2560]{1,0:T(8,128)(2,1)S(1)}, u32[]{:S(2)}, u32[]{:S(2)}) collective-permute-start(bf16[32,2560]{1,0:T(8,128)(2,1)S(1)} %slice_bitcast_fusion), channel_id=1, source_target_pairs={{0,16},{16,0},{1,17},{17,1},{2,18},{18,2},{3,19},{19,3},{4,20},{20... | collective-permute-start | bytes 491528 | tf_op jit(solution)/shard_map/ppermute | solution.py:650
  25.0 6.2 %collective-permute-start.8 = (bf16[104,256]{1,0:T(8,128)(2,1)S(1)}, bf16[104,256]{1,0:T(8,128)(2,1)S(1)}, u32[]{:S(2)}, u32[]{:S(2)}) collective-permute-start(bf16[104,256]{1,0:T(8,128)(2,1)S(1)} %add_convert_fusion.1), channel_id=1, source_target_pairs={{0,8},{1,9},{2,10},{3,11},{4,12},{5,13},{6,14},{7,15},{8,0},{9,1},... | collective-permute-start | bytes 159752 | tf_op jit(solution)/shard_map/ppermute | solution.py:599
  31.3 5.1 %collective-permute-start.11 = (bf16[104,256]{1,0:T(8,128)(2,1)S(1)}, bf16[104,256]{1,0:T(8,128)(2,1)S(1)}, u32[]{:S(2)}, u32[]{:S(2)}) collective-permute-start(bf16[104,256]{1,0:T(8,128)(2,1)S(1)} %add_convert_fusion.refs_0_), channel_id=1, source_target_pairs={{0,3},{1,2},{2,1},{3,0},{4,7},{5,6},{6,5},{7,4},{8,11},{9,10},{10,... | collective-permute-start | bytes 159752 | tf_op jit(solution)/shard_map/ppermute | solution.py:599
  33.1 4.1 %collective-permute-start.10 = (bf16[104,256]{1,0:T(8,128)(2,1)S(1)}, bf16[104,256]{1,0:T(8,128)(2,1)S(1)}, u32[]{:S(2)}, u32[]{:S(2)}) collective-permute-start(bf16[104,256]{1,0:T(8,128)(2,1)S(1)} %add_convert_fusion.refs_0_), channel_id=1, source_target_pairs={{0,2},{1,3},{2,0},{3,1},{4,6},{5,7},{6,4},{7,5},{8,10},{9,11},{10,... | collective-permute-start | bytes 159752 | tf_op jit(solution)/shard_map/ppermute | solution.py:599
  33.6 4.1 %collective-permute-start.9 = (bf16[104,256]{1,0:T(8,128)(2,1)S(1)}, bf16[104,256]{1,0:T(8,128)(2,1)S(1)}, u32[]{:S(2)}, u32[]{:S(2)}) collective-permute-start(bf16[104,256]{1,0:T(8,128)(2,1)S(1)} %add_convert_fusion.refs_0_), channel_id=1, source_target_pairs={{0,1},{1,0},{2,3},{3,2},{4,5},{5,4},{6,7},{7,6},{8,9},{9,8},{10,11... | collective-permute-start | bytes 159752 | tf_op jit(solution)/shard_map/ppermute | solution.py:599
  37.8 1.5 %collective-permute-start.12 = (bf16[416,256]{1,0:T(8,128)(2,1)S(1)}, bf16[416,256]{1,0:T(8,128)(2,1)S(1)}, u32[]{:S(2)}, u32[]{:S(2)}) collective-permute-start(bf16[416,256]{1,0:T(8,128)(2,1)S(1)} %pad_maximum_fusion), channel_id=1, source_target_pairs={{0,16},{1,17},{2,18},{3,19},{4,20},{5,21},{6,22},{7,23},{8,24},{9,... | collective-permute-start | bytes 638984 | tf_op jit(solution)/shard_map/ppermute | solution.py:599
